TPU v7x, 32 devices: a whole 2x2x4 slice. The times are simulated.
32 devices in a mesh: groups: 2 (over y), slab: 4 (over x, core), head: 4 (over z).
Axes of the slice: x: 2, y: 2, z: 4, core: 2. Of those that a mesh axis runs over, the one named last changes fastest.
Arguments:
- query_rows: bfloat16 [2048, 5120], P(('groups', 'slab', 'head')), parts along dimension 0, may hold values from -16 to 16
- key_rows: bfloat16 [2048, 5120], P(('groups', 'slab', 'head')), parts along dimension 0, may hold values from -16 to 16
- value_rows: bfloat16 [2048, 5120], P(('groups', 'slab', 'head')), parts along dimension 0, may hold values from -4 to 4
- tile_mask: int32 [40, 16, 5], P(None, ('groups', 'slab')), parts along dimension 1, may hold values from 0 to 1, as said below
- head_slot: int32 [40], replicated, may hold values from 0 to 39, as said below
Outputs:
- attended: bfloat16 [2048, 5120], P(('groups', 'slab', 'head')), parts along dimension 0
- slot_lse: float32 [40, 2048], P('head', ('groups', 'slab')), parts along dimension 1
There are 2 independent parts, one for each index of `groups`. A program takes and returns all parts, laid end to end along the dimension named above; an argument that names none is the same for every part. Nothing has to cross between parts.
Inputs may be any that keep to these rules, and one draw needn't show every extreme that they name: `tile_mask`: entry 2 of every row of every head is 1. `head_slot`: distinct; slots o * 10 to o * 10 + 9 belong to owner o along the head axis; every owner holds at most 10 heads and some owner holds 10.
All inputs are finite; a program needn't handle non-finite values.
Results may differ from a plain program's by a relative error of at most 0.0045.
Values may be sent and summed in bfloat16 or wider, within the bound.
No kernel may reach another device: no remote copies, remote signals or barrier semaphores. Data moves between devices by JAX's collectives and lax.ppermute only.
A program may use at most 64 MiB of HBM per device.

v0:
```python
import math

import jax
import jax.numpy as jnp
from jax import lax
from jax.sharding import PartitionSpec as P


def with_halo(x, sides, width):
    for axis, dim in sides:
        size, length = (lax.axis_size(axis), x.shape[dim])
        up = [(i, (i + 1) % size) for i in range(size - 1)]
        down = [(j, i) for i, j in up]
        last = lax.slice_in_dim(x, length - width, length, axis=dim)
        leading = lax.slice_in_dim(x, 0, width, axis=dim)
        before = lax.ppermute(last, axis, up)
        after = lax.ppermute(leading, axis, down)
        x = jnp.concatenate([before, x, after], axis=dim)
    return x


def on_device(query_rows, key_rows, value_rows, tile_mask, head_slot):
    owners = lax.axis_size("head")
    owner = lax.axis_index("head")
    slab_index = lax.axis_index("slab")
    tok_dev = query_rows.shape[0]
    heads = tile_mask.shape[0]
    head_dim = query_rows.shape[1] // heads
    capacity = (heads + owners - 1) // owners
    slots = capacity * owners
    band = tile_mask.shape[2]
    reach = (band - 1) // 2
    tiles_dev = tile_mask.shape[1]
    tok_slab = tok_dev * owners
    tile_rows = tok_slab // tiles_dev
    halo = reach * tile_rows
    tiles_all = tiles_dev * lax.axis_size("slab")
    scale = head_dim ** (-0.5)
    slot_ids = jnp.arange(slots, dtype=jnp.int32)
    placed = (head_slot[None, :] == slot_ids[:, None]).astype(jnp.bfloat16)

    def spread(source):
        shaped = source.reshape(tok_dev, heads, head_dim)
        moved = jnp.einsum("jh,thd->jtd", placed, shaped, preferred_element_type=jnp.float32)
        return moved.astype(jnp.bfloat16)

    stacked = jnp.stack([spread(query_rows), spread(key_rows), spread(value_rows)])
    mine = lax.all_to_all(stacked, "head", split_axis=1, concat_axis=2, tiled=True)
    queries = mine[0]
    pair_ext = with_halo(mine[1:], (("slab", 2),), halo)
    own_slots = owner * capacity + jnp.arange(capacity, dtype=jnp.int32)
    own_match = head_slot[None, :] == own_slots[:, None]
    slot_valid = jnp.any(own_match, axis=1)
    slot_tiles = jnp.einsum(
        "ch,hbj->cbj", own_match.astype(jnp.float32), tile_mask.astype(jnp.float32)
    )
    query_block = math.gcd(tok_slab, 512) if tok_slab >= 512 else tok_slab
    query_tiles = query_block // tile_rows
    key_tiles = query_tiles + 2 * reach
    key_block = key_tiles * tile_rows
    block_count = tok_slab // query_block
    offset = (
        jnp.arange(key_tiles, dtype=jnp.int32)[None, :]
        - jnp.arange(query_tiles, dtype=jnp.int32)[:, None]
    )
    select = (offset[:, :, None] == jnp.arange(band, dtype=jnp.int32)[None, None, :]).astype(
        jnp.float32
    )

    def one_block(index, carry):
        out_buffer, lse_buffer = carry
        start = index * query_block
        tile_first = index * query_tiles
        block_queries = lax.dynamic_slice_in_dim(queries, start, query_block, 1)
        block_pair = lax.dynamic_slice_in_dim(pair_ext, start, key_block, 2)
        scores = (
            jnp.einsum(
                "cqd,ckd->cqk", block_queries, block_pair[0], preferred_element_type=jnp.float32
            )
            * scale
        )
        band_rows = lax.dynamic_slice_in_dim(slot_tiles, tile_first, query_tiles, 1)
        permitted = jnp.einsum("cqj,qkj->cqk", band_rows, select) > 0.5
        key_global = (
            slab_index * tiles_dev + tile_first + jnp.arange(key_tiles, dtype=jnp.int32) - reach
        )
        in_range = (key_global >= 0) & (key_global < tiles_all)
        permitted = permitted & in_range[None, None, :]
        permitted_rows = jnp.repeat(jnp.repeat(permitted, tile_rows, axis=1), tile_rows, axis=2)
        masked = jnp.where(permitted_rows, scores, -1e30)
        highest = jnp.max(masked, axis=2, keepdims=True)
        weights = jnp.exp(masked - highest)
        total = jnp.sum(weights, axis=2)
        summed = jnp.einsum(
            "cqk,ckd->cqd",
            weights.astype(jnp.bfloat16),
            block_pair[1],
            preferred_element_type=jnp.float32,
        )
        result = (summed / total[:, :, None]).astype(jnp.bfloat16)
        out_buffer = lax.dynamic_update_slice_in_dim(out_buffer, result, start, 1)
        lse_buffer = lax.dynamic_update_slice_in_dim(
            lse_buffer, highest[:, :, 0] + jnp.log(total), start, 1
        )
        return (out_buffer, lse_buffer)

    start_out = jnp.zeros((capacity, tok_slab, head_dim), jnp.bfloat16)
    start_lse = jnp.zeros((capacity, tok_slab), jnp.float32)
    owner_out, owner_lse = lax.fori_loop(0, block_count, one_block, (start_out, start_lse))
    slot_lse = jnp.where(slot_valid[:, None], owner_lse, 0.0)
    returned = lax.all_to_all(owner_out, "head", split_axis=1, concat_axis=0, tiled=True)
    gathered = jnp.einsum("jh,jtd->thd", placed, returned, preferred_element_type=jnp.float32)
    attended = gathered.astype(jnp.bfloat16).reshape(tok_dev, heads * head_dim)
    return (attended, slot_lse)


def solution(mesh):
    in_specs = (
        P(("groups", "slab", "head"), None),
        P(("groups", "slab", "head"), None),
        P(("groups", "slab", "head"), None),
        P(None, ("groups", "slab"), None),
        P(),
    )
    out_specs = (P(("groups", "slab", "head"), None), P("head", ("groups", "slab")))
    return jax.shard_map(
        on_device, mesh=mesh, in_specs=in_specs, out_specs=out_specs, check_vma=False
    )
```

profile of v0, /device:TPU:2, one launch (start us, length us, event | category | flops | bytes accessed | tf_op | source)
XLA Modules:
  0.0 108.3 jit_solution(17828716468529784090)
XLA Ops:
  0.6 0.0 copy-start.1
  0.6 1.2 %copy.68 = bf16[8,8,40,128]{3,2,1,0:T(8,128)(2,1)S(1)} copy(bf16[8,8,40,128]{3,1,2,0:T(8,128)(2,1)} %bitcast.71) | data formatting | bytes 1310720
  1.8 0.0 copy-start
  1.9 1.3 %copy.69 = bf16[8,8,40,128]{3,2,1,0:T(8,128)(2,1)S(1)} copy(bf16[8,8,40,128]{3,1,2,0:T(8,128)(2,1)} %bitcast.72) | data formatting | bytes 1310720
  3.1 0.0 copy-done.1
  3.1 0.5 fusion.9
  3.6 0.5 fusion.10
  4.0 0.0 copy-done
  4.1 0.1 copy.70
  4.1 0.5 fusion.11
  4.6 0.2 pad_maximum_fusion.1
  4.8 0.5 copy.52
  5.3 50.1 %all_to_all.33 = bf16[3,40,64,128]{3,2,0,1:T(8,128)(2,1)S(1)} all-to-all(bf16[3,40,64,128]{3,2,0,1:T(8,128)(2,1)S(1)} %copy.52), channel_id=1, replica_groups=mesh['groups'=2,'slab'=4,'head'=4] {'head'}, dimensions={1} | all-to-all | bytes 3932160 | tf_op jit(solution)/shard_map/all_to_all | solution.py:48
  55.4 0.2 copy.53
  55.6 0.1 slice.24
  55.7 0.0 copy-start.2
  55.7 0.1 copy.55
  55.9 1.9 %collective-permute-start.1 = (bf16[2,10,256,128]{3,2,1,0:T(8,128)(2,1)S(1)}, bf16[2,10,256,128]{3,2,1,0:T(8,128)(2,1)}, u32[]{:S(2)}, u32[]{:S(2)}) collective-permute-start(bf16[2,10,256,128]{3,2,1,0:T(8,128)(2,1)S(1)} %bitcast.61), channel_id=1, source_target_pairs={{4,0},{8,4},{12,8},{5,1},{9,5},{13,9},{6,2},{10,6},{14,10},{7,3},{... | collective-permute-start | bytes 3932168 | tf_op jit(solution)/shard_map/ppermute | solution.py:17
  57.8 3.5 %collective-permute-start = (bf16[2,10,256,128]{3,2,1,0:T(8,128)(2,1)S(1)}, bf16[2,10,256,128]{3,2,1,0:T(8,128)(2,1)}, u32[]{:S(2)}, u32[]{:S(2)}) collective-permute-start(bf16[2,10,256,128]{3,2,1,0:T(8,128)(2,1)S(1)} %bitcast.62), channel_id=1, source_target_pairs={{0,4},{4,8},{8,12},{1,5},{5,9},{9,13},{2,6},{6,10},{10,14},{3,7},{... | collective-permute-start | bytes 3932168 | tf_op jit(solution)/shard_map/ppermute | solution.py:16
  61.2 0.0 copy-done.2
  61.3 0.3 fusion.21
  61.6 0.1 copy.48
  61.8 0.1 broadcast_bitcast_fusion
  61.9 0.5 broadcast_in_dim.43
  62.4 2.1 %copy.56 = pred[10,256,768]{2,1,0:T(32,128)(4,1)S(1)} copy(pred[10,256,768]{1,2,0:T(32,128)(4,1)S(1)} %bitcast.60) | data formatting | bytes 3932160 | tf_op jit(solution)/shard_map/while/body/eval_jaxpr/reshape | solution.py:89
  64.6 8.3 %collective-permute-done.1 = bf16[2,10,256,128]{3,2,1,0:T(8,128)(2,1)} collective-permute-done((bf16[2,10,256,128]{3,2,1,0:T(8,128)(2,1)S(1)}, bf16[2,10,256,128]{3,2,1,0:T(8,128)(2,1)}, u32[]{:S(2)}, u32[]{:S(2)}) %collective-permute-start.1) | collective-permute-done | bytes 1310752 | tf_op jit(solution)/shard_map/ppermute | solution.py:17
  72.9 3.9 %collective-permute-done = bf16[2,10,256,128]{3,2,1,0:T(8,128)(2,1)} collective-permute-done((bf16[2,10,256,128]{3,2,1,0:T(8,128)(2,1)S(1)}, bf16[2,10,256,128]{3,2,1,0:T(8,128)(2,1)}, u32[]{:S(2)}, u32[]{:S(2)}) %collective-permute-start) | collective-permute-done | bytes 1310752 | tf_op jit(solution)/shard_map/ppermute | solution.py:16
  76.8 1.9 %pad_maximum_fusion = bf16[2,10,768,128]{3,2,1,0:T(8,128)(2,1)S(1)} fusion(bf16[2,10,256,128]{3,2,1,0:T(8,128)(2,1)} %collective-permute-done.1, bf16[2,10,256,128]{3,2,1,0:T(8,128)(2,1)S(1)} %bitcast.63, bf16[2,10,256,128]{3,2,1,0:T(8,128)(2,1)} %collective-permute-done), kind=kLoop, calls=%fused_computation.6 | loop fusion | flops 11796480 | bytes 7864320 | tf_op jit(solution)/shard_map/concatenate | solution.py:18
  78.7 1.8 %fusion.2 = (f32[10,256]{1,0:T(8,128)S(1)}, f32[10,256,768]{2,1,0:T(8,128)S(1)}) fusion(pred[10,256,768]{2,1,0:T(32,128)(4,1)S(1)} %copy.56, bf16[10,256,128]{2,1,0:T(8,128)(2,1)S(1)} %bitcast.65, bf16[2,10,768,128]{3,2,1,0:T(8,128)(2,1)S(1)} %pad_maximum_fusion), kind=kOutput, calls=%fused_computation.4 | convolution fusion | flops 509212160 | bytes 12462080 | tf_op jit(solution)/shard_map/while/body/eval_jaxpr/cqd,ckd->cqk/dot_general | solution.py:77
  80.5 2.5 %fusion = f32[10,256]{1,0:T(8,128)S(1)} fusion(pred[10,256,768]{2,1,0:T(32,128)(4,1)S(1)} %copy.56, f32[10,256,768]{2,1,0:T(8,128)S(1)} %get-tuple-element.21, f32[10,256]{1,0:T(8,128)S(1)} %get-tuple-element.20), kind=kLoop, calls=%fused_computation.2 | loop fusion | flops 7861760 | bytes 9850880 | tf_op jit(solution)/shard_map/while/body/eval_jaxpr/reduce_sum | solution.py:93
  82.9 2.9 %divide_convert_fusion = bf16[10,256,128]{2,1,0:T(8,128)(2,1)S(1)} fusion(bf16[2,10,768,128]{3,2,1,0:T(8,128)(2,1)S(1)} %pad_maximum_fusion, pred[10,256,768]{2,1,0:T(32,128)(4,1)S(1)} %copy.56, f32[10,256,768]{2,1,0:T(8,128)S(1)} %get-tuple-element.21, f32[10,256]{1,0:T(8,128)S(1)} %get-tuple-element.20, f32[10,256]{1,0:T(8,128)S(1)} %fusion), kind=kOutput, calls=%fused_computation.18 | convolution fusion | flops 511836160 | bytes 12484608 | tf_op jit(solution)/shard_map/while/body/eval_jaxpr/cqk,ckd->cqd/dot_general | solution.py:94
  85.8 1.5 %copy.57 = bf16[10,256,128]{2,0,1:T(8,128)(2,1)} copy(bf16[10,256,128]{2,1,0:T(8,128)(2,1)S(1)} %divide_convert_fusion) | data formatting | bytes 1310720 | tf_op jit(solution)/shard_map/while/body/eval_jaxpr/convert_element_type | solution.py:100
  87.3 3.5 %all-to-all-start.1 = ((bf16[10,256,128]{2,0,1:T(8,128)(2,1)}), bf16[10,256,128]{2,0,1:T(8,128)(2,1)S(1)}, u32[]{:S(2)}, u32[]{:S(2)}) async-start(bf16[10,256,128]{2,0,1:T(8,128)(2,1)} %copy.57), calls=%async_computation.1 | async-start | bytes 2097152 | tf_op jit(solution)/shard_map/all_to_all | solution.py:111
  90.8 0.2 compare_reduce_fusion
  91.0 0.7 add_select_fusion
  91.7 15.0 %all-to-all-done.1 = bf16[10,256,128]{2,0,1:T(8,128)(2,1)S(1)} async-done(((bf16[10,256,128]{2,0,1:T(8,128)(2,1)}), bf16[10,256,128]{2,0,1:T(8,128)(2,1)S(1)}, u32[]{:S(2)}, u32[]{:S(2)}) %all-to-all-start.1) | async-done | bytes 655392 | tf_op jit(solution)/shard_map/all_to_all | solution.py:111
  106.7 0.2 copy.59
  106.9 0.5 convolution_convert_fusion
  107.4 0.9 copy.78
  (6 shorter events, 0.1 us)
Async XLA Ops:
  0.6 2.5 %copy-start.1 = (s32[40]{0:T(128)S(1)}, s32[40]{0:T(128)}, u32[]{:S(2)}) copy-start(s32[40]{0:T(128)} %param.9) | copy-start | bytes 484
  1.8 2.2 %copy-start = (bf16[64,5120]{1,0:T(8,128)(2,1)S(1)}, bf16[64,5120]{1,0:T(8,128)(2,1)}, u32[]{:S(2)}) copy-start(bf16[64,5120]{1,0:T(8,128)(2,1)} %param.7) | copy-start | bytes 1966084
  55.7 5.5 %copy-start.2 = (s32[40,2,5]{0,1,2:T(2,128)S(1)}, s32[40,2,5]{0,1,2:T(2,128)}, u32[]{:S(2)}) copy-start(s32[40,2,5]{0,1,2:T(2,128)} %param.8) | copy-start | bytes 4804
  55.9 17.0 %collective-permute-start.1 = (bf16[2,10,256,128]{3,2,1,0:T(8,128)(2,1)S(1)}, bf16[2,10,256,128]{3,2,1,0:T(8,128)(2,1)}, u32[]{:S(2)}, u32[]{:S(2)}) collective-permute-start(bf16[2,10,256,128]{3,2,1,0:T(8,128)(2,1)S(1)} %bitcast.61), channel_id=1, source_target_pairs={{4,0},{8,4},{12,8},{5,1},{9,5},{13,9},{6,2},{10,6},{14,10},{7,3},{... | collective-permute-start | bytes 3932168 | tf_op jit(solution)/shard_map/ppermute | solution.py:17
  57.8 19.0 %collective-permute-start = (bf16[2,10,256,128]{3,2,1,0:T(8,128)(2,1)S(1)}, bf16[2,10,256,128]{3,2,1,0:T(8,128)(2,1)}, u32[]{:S(2)}, u32[]{:S(2)}) collective-permute-start(bf16[2,10,256,128]{3,2,1,0:T(8,128)(2,1)S(1)} %bitcast.62), channel_id=1, source_target_pairs={{0,4},{4,8},{8,12},{1,5},{5,9},{9,13},{2,6},{6,10},{10,14},{3,7},{... | collective-permute-start | bytes 3932168 | tf_op jit(solution)/shard_map/ppermute | solution.py:16
  87.3 19.4 %all-to-all-start.1 = ((bf16[10,256,128]{2,0,1:T(8,128)(2,1)}), bf16[10,256,128]{2,0,1:T(8,128)(2,1)S(1)}, u32[]{:S(2)}, u32[]{:S(2)}) async-start(bf16[10,256,128]{2,0,1:T(8,128)(2,1)} %copy.57), calls=%async_computation.1 | async-start | bytes 2097152 | tf_op jit(solution)/shard_map/all_to_all | solution.py:111
where the time goes:
time: 109 us; the launch traced here: 108 us
  blocking collectives  50.1 us (46%)
  waiting for transfers between devices  27.2 us (25%)
  local copies, waits for them, and re-layouts  8.98 us (8%)
  starting transfers between devices  8.89 us (8%)
  matrix products  6.85 us (6%)
  other arithmetic  5.45 us (5%)
    all_to_all x1, blocking collectives, on_device(): lax.all_to_all(stacked, 'head', split_axis=1, concat_axis=2, tiled=True)  50.1 us
    all_to_all x1, waiting for transfers between devices, on_device(): lax.all_to_all(owner_out, 'head', split_axis=1, concat_axis=0, tiled=True)  15 us
    ppermute x1, waiting for transfers between devices, with_halo(): after = lax.ppermute(leading, axis, down)  8.28 us
    ppermute x1, waiting for transfers between devices, with_halo(): before = lax.ppermute(last, axis, up)  3.93 us
    all_to_all x1, starting transfers between devices, on_device(): lax.all_to_all(owner_out, 'head', split_axis=1, concat_axis=0, tiled=True)  3.51 us
    unnamed x10, local copies, waits for them, and re-layouts  3.5 us
    ppermute x1, starting transfers between devices, with_halo(): before = lax.ppermute(last, axis, up)  3.45 us
    dot_general x1, matrix products, one_block(): jnp.einsum('cqk,ckd->cqd', weights.astype(jnp.bfloat16), block_pair[1], p...  2.91 us
  transfers between devices with their start and end apart: 3, of which 3 were waited for; matrix products, arithmetic and copies ran while one was open for 4% of the time, Pallas kernels for 0%

commit v1 on v0

v1 whole, which is shorter than its diff:
```python
import functools
import math

import jax
import jax.numpy as jnp
from jax import lax
from jax.experimental import pallas as pl
from jax.experimental.pallas import tpu as pltpu
from jax.sharding import PartitionSpec as P

VMEM_BYTES = 24 * 1024 * 1024
ANY = pl.BlockSpec(memory_space=pl.ANY)
SMEM = pl.BlockSpec(memory_space=pltpu.SMEM)
VMEM = pl.BlockSpec(memory_space=pltpu.VMEM)


def params(aliasing=False):
    return pltpu.CompilerParams(vmem_limit_bytes=VMEM_BYTES)


def invert(head_slot, head_of):
    for j in range(head_of.shape[0]):
        head_of[j] = 0
    for h in range(head_slot.shape[0]):
        head_of[head_slot[h]] = h


def pack_kernel(owners, capacity, first, count, dim, sources, head_slot, *refs):
    rows = refs[:sources]
    outs = refs[sources : sources + owners]
    head_of, sem = refs[sources + owners :]
    me = lax.axis_index("head")
    invert(head_slot, head_of)
    copies = []
    for k in range(owners):
        owner = lax.rem(me + k, owners)
        for c in range(count):
            head = head_of[owner * capacity + first + c]
            columns = pl.ds(pl.multiple_of(head * dim, dim), dim)
            for s in range(sources):
                copies.append(
                    pltpu.make_async_copy(
                        rows[s].at[:, columns], outs[k].at[s, c], sem.at[len(copies)]
                    )
                )
                copies[-1].start()
    for copy in copies:
        copy.wait()


def pack(head_slot, rows, owners, capacity, first, count, heads):
    tokens, width = rows[0].shape
    dim = width // heads
    shape = jax.ShapeDtypeStruct((len(rows), count, tokens, dim), rows[0].dtype)
    nbytes = 2 * owners * math.prod(shape.shape) * 2
    return pl.pallas_call(
        functools.partial(pack_kernel, owners, capacity, first, count, dim, len(rows)),
        out_shape=[shape] * owners,
        in_specs=[SMEM] + [ANY] * len(rows),
        out_specs=[ANY] * owners,
        scratch_shapes=[
            pltpu.SMEM((owners * capacity,), jnp.int32),
            pltpu.SemaphoreType.DMA((owners * count * len(rows),)),
        ],
        compiler_params=params(),
        cost_estimate=pl.CostEstimate(flops=0, bytes_accessed=nbytes, transcendentals=0),
        name="pack",
    )(head_slot, *rows)


def join_kernel(owners, *refs):
    blocks, out, sem = refs[:owners], refs[owners], refs[owners + 1]
    me = lax.axis_index("head")
    tokens = blocks[0].shape[2]
    copies = []
    for k in range(owners):
        start = lax.rem(me - k + owners, owners) * tokens
        place = pl.ds(pl.multiple_of(start, tokens), tokens)
        copies.append(pltpu.make_async_copy(blocks[k], out.at[:, :, place], sem.at[k]))
        copies[-1].start()
    for copy in copies:
        copy.wait()


def join(blocks):
    owners = len(blocks)
    s, c, t, d = blocks[0].shape
    shape = jax.ShapeDtypeStruct((s, c, t * owners, d), blocks[0].dtype)
    return pl.pallas_call(
        functools.partial(join_kernel, owners),
        out_shape=shape,
        in_specs=[ANY] * owners,
        out_specs=ANY,
        scratch_shapes=[pltpu.SemaphoreType.DMA((owners,))],
        compiler_params=params(),
        cost_estimate=pl.CostEstimate(
            flops=0, bytes_accessed=4 * math.prod(shape.shape), transcendentals=0
        ),
        name="join",
    )(*blocks)


def attend_kernel(owners, capacity, first, tiles, tiles_all, band, head_slot, mask, *refs):
    q_blocks = refs[:owners]
    mid, before, after = refs[owners : owners + 3]
    outs = refs[owners + 3 : 2 * owners + 3]
    lse_ref, q_all, o_all, head_of, used = refs[2 * owners + 3 :]
    me = lax.axis_index("head")
    tile_base = lax.axis_index("slab") * tiles
    _, count, tok, dim = q_blocks[0].shape
    reach = (band - 1) // 2
    rows = tok * owners // tiles
    scale = dim ** (-0.5)
    base2 = scale * math.log2(math.e)

    for j in range(owners * capacity):
        head_of[j] = 0
        used[j] = 0
    for h in range(head_slot.shape[0]):
        head_of[head_slot[h]] = h
        used[head_slot[h]] = 1

    for k in range(owners):
        place = pl.ds(pl.multiple_of(lax.rem(me - k + owners, owners) * tok, tok), tok)
        q_all[:, place, :] = q_blocks[k][0]

    def window(which, c, first_tile):
        parts = []
        low, high = first_tile * rows, (first_tile + band) * rows
        halo, own = reach * rows, tiles * rows
        if low < halo:
            parts.append(before[which, c, low : min(high, halo)])
        if low < halo + own and high > halo:
            parts.append(mid[which, c, max(low - halo, 0) : min(high - halo, own)])
        if high > halo + own:
            parts.append(after[which, c, max(low - halo - own, 0) : high - halo - own])
        return jnp.concatenate(parts, axis=0) if len(parts) > 1 else parts[0]

    for c in range(count):
        slot = me * capacity + first + c
        head = head_of[slot]
        valid = used[slot] > 0
        for t in range(tiles):
            queries = q_all[c, t * rows : (t + 1) * rows, :]
            scores = lax.dot_general(
                queries,
                window(0, c, t),
                (((1,), (1,)), ((), ())),
                preferred_element_type=jnp.float32,
            )
            kept = []
            for b in range(band):
                tile = tile_base + t + b - reach
                flag = mask[(head * tiles + t) * band + b]
                allowed = (flag > 0) & (tile >= 0) & (tile < tiles_all)
                part = scores[:, b * rows : (b + 1) * rows]
                kept.append(jnp.where(allowed, part, -1e30))
            masked = jnp.concatenate(kept, axis=1)
            highest = jnp.max(masked, axis=1, keepdims=True)
            weights = jnp.exp2((masked - highest) * base2)
            total = jnp.sum(weights, axis=1, keepdims=True)
            summed = jnp.dot(
                weights.astype(jnp.bfloat16), window(1, c, t), preferred_element_type=jnp.float32
            )
            o_all[c, t * rows : (t + 1) * rows, :] = (summed / total).astype(jnp.bfloat16)
            lse = jnp.where(valid, highest * scale + jnp.log(total), 0.0)
            lse_ref[c : c + 1, t * rows : (t + 1) * rows] = jnp.transpose(
                jnp.broadcast_to(lse, (rows, 128))
            )[0:1, :]

    for k in range(owners):
        place = pl.ds(pl.multiple_of(lax.rem(me + k, owners) * tok, tok), tok)
        outs[k][...] = o_all[:, place, :]


def attend(head_slot, mask, q_blocks, mid, before, after, capacity, first, tiles, tiles_all, band):
    owners = len(q_blocks)
    _, count, tok, dim = q_blocks[0].shape
    out = jax.ShapeDtypeStruct((count, tok, dim), jnp.bfloat16)
    keys = band * (tok * owners // tiles)
    pairs = count * tok * owners * keys
    return pl.pallas_call(
        functools.partial(attend_kernel, owners, capacity, first, tiles, tiles_all, band),
        out_shape=[out] * owners + [jax.ShapeDtypeStruct((count, tok * owners), jnp.float32)],
        in_specs=[SMEM, SMEM] + [VMEM] * (owners + 3),
        out_specs=[VMEM] * (owners + 1),
        scratch_shapes=[
            pltpu.VMEM((count, tok * owners, dim), jnp.bfloat16),
            pltpu.VMEM((count, tok * owners, dim), jnp.bfloat16),
            pltpu.SMEM((owners * capacity,), jnp.int32),
            pltpu.SMEM((owners * capacity,), jnp.int32),
        ],
        compiler_params=params(),
        cost_estimate=pl.CostEstimate(
            flops=4 * pairs * dim,
            bytes_accessed=4 * math.prod(mid.shape) + 4 * math.prod(before.shape),
            transcendentals=pairs,
        ),
        name="attend",
    )(head_slot, mask, *q_blocks, mid, before, after)


def unpack_kernel(owners, capacity, first, count, dim, head_slot, *refs):
    blocks = refs[:owners]
    out, head_of, used, sem = refs[-4:]
    me = lax.axis_index("head")
    for j in range(owners * capacity):
        head_of[j] = 0
        used[j] = 0
    for h in range(head_slot.shape[0]):
        head_of[head_slot[h]] = h
        used[head_slot[h]] = 1

    def each(act):
        for k in range(owners):
            owner = lax.rem(me - k + owners, owners)
            for c in range(count):
                slot = owner * capacity + first + c
                columns = pl.ds(pl.multiple_of(head_of[slot] * dim, dim), dim)
                copy = pltpu.make_async_copy(
                    blocks[k].at[c], out.at[:, columns], sem.at[k * count + c]
                )
                pl.when(used[slot] > 0)(functools.partial(act, copy))

    each(lambda copy: copy.start())
    each(lambda copy: copy.wait())


def unpack(head_slot, blocks, target, capacity, first, shape):
    owners = len(blocks)
    count, tok, dim = blocks[0].shape
    operands = list(blocks) + ([] if target is None else [target])
    return pl.pallas_call(
        functools.partial(unpack_kernel, owners, capacity, first, count, dim),
        out_shape=shape,
        in_specs=[SMEM] + [ANY] * len(operands),
        out_specs=ANY,
        input_output_aliases={} if target is None else {owners + 1: 0},
        scratch_shapes=[
            pltpu.SMEM((owners * capacity,), jnp.int32),
            pltpu.SMEM((owners * capacity,), jnp.int32),
            pltpu.SemaphoreType.DMA((owners * count,)),
        ],
        compiler_params=params(),
        cost_estimate=pl.CostEstimate(
            flops=0, bytes_accessed=4 * owners * count * tok * dim, transcendentals=0
        ),
        name="unpack",
    )(head_slot, *operands)


def exchange(blocks):
    owners = len(blocks)
    return [blocks[0]] + [
        lax.ppermute(blocks[k], "head", [(i, (i + k) % owners) for i in range(owners)])
        for k in range(1, owners)
    ]


def on_device(query_rows, key_rows, value_rows, tile_mask, head_slot):
    owners = lax.axis_size("head")
    slabs = lax.axis_size("slab")
    tok_dev = query_rows.shape[0]
    heads, tiles, band = tile_mask.shape
    capacity = (heads + owners - 1) // owners
    reach = (band - 1) // 2
    tok_slab = tok_dev * owners
    halo = reach * (tok_slab // tiles)
    mask = tile_mask.reshape(-1)
    half = (capacity + 1) // 2
    groups = [(0, half), (half, capacity - half)]
    groups = [g for g in groups if g[1]]
    up = [(i, i + 1) for i in range(slabs - 1)]
    down = [(j, i) for i, j in up]

    args = (owners, capacity)
    pairs = []
    for first, count in groups:
        packed = pack(head_slot, (key_rows, value_rows), *args, first, count, heads)
        mid = join(exchange(packed))
        last = lax.slice_in_dim(mid, tok_slab - halo, tok_slab, axis=2)
        lead = lax.slice_in_dim(mid, 0, halo, axis=2)
        before = lax.ppermute(last, "slab", up)
        after = lax.ppermute(lead, "slab", down)
        pairs.append((mid, before, after))
    queries = [
        exchange(pack(head_slot, (query_rows,), *args, first, count, heads))
        for first, count in groups
    ]
    target, lses = None, []
    for (first, count), pair, q_blocks in zip(groups, pairs, queries):
        *outs, lse = attend(
            head_slot, mask, q_blocks, *pair, capacity, first, tiles, tiles * slabs, band
        )
        lses.append(lse)
        target = unpack(
            head_slot,
            exchange(outs),
            target,
            capacity,
            first,
            jax.ShapeDtypeStruct(query_rows.shape, query_rows.dtype),
        )
    return target, jnp.concatenate(lses, axis=0)


def solution(mesh):
    rows = P(("groups", "slab", "head"), None)
    in_specs = (rows, rows, rows, P(None, ("groups", "slab"), None), P())
    out_specs = (rows, P("head", ("groups", "slab")))
    return jax.shard_map(
        on_device, mesh=mesh, in_specs=in_specs, out_specs=out_specs, check_vma=False
    )
```

time: 109 us -> 95.5 us (0.88)
  the two profiles are of different devices: /device:TPU:2 before, /device:TPU:0 now
where the time goes in v1:
time: 95.5 us; the launch traced here: 94.7 us
  starting transfers between devices  35.3 us (37%)
  waiting for transfers between devices  30.6 us (32%)
  Pallas kernels  16.8 us (18%)
  local copies, waits for them, and re-layouts  10.6 us (11%)
    ppermute x18, waiting for transfers between devices, exchange(): lax.ppermute(blocks[k], 'head', [(i, (i + k) % owners) for i in range(own...  30.6 us
    ppermute x18, starting transfers between devices, exchange(): lax.ppermute(blocks[k], 'head', [(i, (i + k) % owners) for i in range(own...  29.4 us
    unnamed x33, local copies, waits for them, and re-layouts  9.65 us
    pallas_call x2, Pallas kernels, attend(): pl.pallas_call(functools.partial(attend_kernel, owners, capacity, first,...  8.17 us
    pallas_call x4, Pallas kernels, pack(): pl.pallas_call(functools.partial(pack_kernel, owners, capacity, first, co...  5.25 us
    ppermute x2, starting transfers between devices, on_device(): before = lax.ppermute(last, 'slab', up)  3.33 us
    pallas_call x2, Pallas kernels, unpack(): pl.pallas_call(functools.partial(unpack_kernel, owners, capacity, first,...  3.07 us
    ppermute x2, starting transfers between devices, on_device(): after = lax.ppermute(lead, 'slab', down)  2.58 us
  transfers between devices with their start and end apart: 22, of which 10 were waited for; matrix products, arithmetic and copies ran while one was open for 2% of the time, Pallas kernels for 15%

profile of v1, /device:TPU:0, one launch (start us, length us, event | category | flops | bytes accessed | tf_op | source)
XLA Modules:
  0.0 94.7 jit_solution(9969732903885043879)
XLA Ops:
  0.6 1.1 %copy-done = bf16[64,5120]{1,0:T(8,128)(2,1)S(1)} copy-done((bf16[64,5120]{1,0:T(8,128)(2,1)S(1)}, bf16[64,5120]{1,0:T(8,128)(2,1)}, u32[]{:S(2)}) %copy-start) | copy-done | bytes 655384
  1.7 1.1 %copy-done.1 = bf16[64,5120]{1,0:T(8,128)(2,1)S(1)} copy-done((bf16[64,5120]{1,0:T(8,128)(2,1)S(1)}, bf16[64,5120]{1,0:T(8,128)(2,1)}, u32[]{:S(2)}) %copy-start.1) | copy-done | bytes 655384
  2.8 0.7 copy-done.13
  3.5 1.3 %pack.7 = (bf16[2,5,64,128]{3,2,1,0:T(8,128)(2,1)S(1)}, bf16[2,5,64,128]{3,2,1,0:T(8,128)(2,1)S(1)}, bf16[2,5,64,128]{3,2,1,0:T(8,128)(2,1)S(1)}, bf16[2,5,64,128]{3,2,1,0:T(8,128)(2,1)S(1)}) custom-call(s32[40]{0:T(128)S(1)} %copy-done.13, bf16[64,5120]{1,0:T(8,128)(2,1)S(1)} %copy-done, bf16[64,5120]{1,0:T(8,128)(2,1)S(1)} %copy-done.1), custom_call_target="tpu_custom_call" | custom-call | bytes 1310720 | tf_op jit(solution)/shard_map/pack/pallas_call | solution.py:56
  4.8 3.1 %collective-permute-start.14 = (bf16[2,5,64,128]{3,2,1,0:T(8,128)(2,1)S(1)}, bf16[2,5,64,128]{3,2,1,0:T(8,128)(2,1)S(1)}, u32[]{:S(2)}, u32[]{:S(2)}) collective-permute-start(bf16[2,5,64,128]{3,2,1,0:T(8,128)(2,1)S(1)} %get-tuple-element.45), channel_id=1, source_target_pairs={{0,1},{1,2},{2,3},{3,0},{4,5},{5,6},{6,7},{7,4},{8,9},{9,10},{10,1... | collective-permute-start | bytes 491528 | tf_op jit(solution)/shard_map/ppermute | solution.py:255
  7.9 2.6 %collective-permute-start.15 = (bf16[2,5,64,128]{3,2,1,0:T(8,128)(2,1)S(1)}, bf16[2,5,64,128]{3,2,1,0:T(8,128)(2,1)S(1)}, u32[]{:S(2)}, u32[]{:S(2)}) collective-permute-start(bf16[2,5,64,128]{3,2,1,0:T(8,128)(2,1)S(1)} %get-tuple-element.46), channel_id=1, source_target_pairs={{0,2},{1,3},{2,0},{3,1},{4,6},{5,7},{6,4},{7,5},{8,10},{9,11},{10,... | collective-permute-start | bytes 491528 | tf_op jit(solution)/shard_map/ppermute | solution.py:255
  10.5 1.3 %collective-permute-start.16 = (bf16[2,5,64,128]{3,2,1,0:T(8,128)(2,1)S(1)}, bf16[2,5,64,128]{3,2,1,0:T(8,128)(2,1)S(1)}, u32[]{:S(2)}, u32[]{:S(2)}) collective-permute-start(bf16[2,5,64,128]{3,2,1,0:T(8,128)(2,1)S(1)} %get-tuple-element.47), channel_id=1, source_target_pairs={{0,3},{1,0},{2,1},{3,2},{4,7},{5,4},{6,5},{7,6},{8,11},{9,8},{10,9... | collective-permute-start | bytes 491528 | tf_op jit(solution)/shard_map/ppermute | solution.py:255
  11.8 1.3 %pack.5 = (bf16[2,5,64,128]{3,2,1,0:T(8,128)(2,1)S(1)}, bf16[2,5,64,128]{3,2,1,0:T(8,128)(2,1)S(1)}, bf16[2,5,64,128]{3,2,1,0:T(8,128)(2,1)S(1)}, bf16[2,5,64,128]{3,2,1,0:T(8,128)(2,1)S(1)}) custom-call(s32[40]{0:T(128)S(1)} %copy-done.13, bf16[64,5120]{1,0:T(8,128)(2,1)S(1)} %copy-done, bf16[64,5120]{1,0:T(8,128)(2,1)S(1)} %copy-done.1), custom_call_target="tpu_custom_call" | custom-call | bytes 1310720 | tf_op jit(solution)/shard_map/pack/pallas_call | solution.py:56
  13.2 0.7 collective-permute-start.3
  13.9 0.3 collective-permute-start.4
  14.3 0.8 collective-permute-done.14.refs_1_
  15.0 2.0 %collective-permute-start.5 = (bf16[2,5,64,128]{3,2,1,0:T(8,128)(2,1)S(1)}, bf16[2,5,64,128]{3,2,1,0:T(8,128)(2,1)S(1)}, u32[]{:S(2)}, u32[]{:S(2)}) collective-permute-start(bf16[2,5,64,128]{3,2,1,0:T(8,128)(2,1)S(1)} %get-tuple-element.35), channel_id=1, source_target_pairs={{0,3},{1,0},{2,1},{3,2},{4,7},{5,4},{6,5},{7,6},{8,11},{9,8},{10,9... | collective-permute-start | bytes 491528 | tf_op jit(solution)/shard_map/ppermute | solution.py:255
  17.1 5.0 %collective-permute-done.15.refs_2_ = bf16[2,5,64,128]{3,2,1,0:T(8,128)(2,1)S(1)} collective-permute-done((bf16[2,5,64,128]{3,2,1,0:T(8,128)(2,1)S(1)}, bf16[2,5,64,128]{3,2,1,0:T(8,128)(2,1)S(1)}, u32[]{:S(2)}, u32[]{:S(2)}) %collective-permute-start.15) | collective-permute-done | bytes 163872 | tf_op jit(solution)/shard_map/ppermute | solution.py:255
  22.1 2.2 %collective-permute-done.16.refs_3_ = bf16[2,5,64,128]{3,2,1,0:T(8,128)(2,1)S(1)} collective-permute-done((bf16[2,5,64,128]{3,2,1,0:T(8,128)(2,1)S(1)}, bf16[2,5,64,128]{3,2,1,0:T(8,128)(2,1)S(1)}, u32[]{:S(2)}, u32[]{:S(2)}) %collective-permute-start.16) | collective-permute-done | bytes 163872 | tf_op jit(solution)/shard_map/ppermute | solution.py:255
  24.3 0.2 join.3.refs_4_
  24.5 1.3 %collective-permute-start.17 = (bf16[2,5,256,128]{3,2,1,0:T(8,128)(2,1)S(1)}, bf16[2,5,256,128]{3,2,1,0:T(8,128)(2,1)S(1)}, u32[]{:S(2)}, u32[]{:S(2)}) collective-permute-start(bf16[2,5,256,128]{3,2,1,0:T(8,128)(2,1)S(1)} %join.3.refs_4_), channel_id=1, source_target_pairs={{0,4},{4,8},{8,12},{1,5},{5,9},{9,13},{2,6},{6,10},{10,14},{3,7},{... | collective-permute-start | bytes 1966088 | tf_op jit(solution)/shard_map/ppermute | solution.py:283
  25.8 1.3 %collective-permute-start.18 = (bf16[2,5,256,128]{3,2,1,0:T(8,128)(2,1)S(1)}, bf16[2,5,256,128]{3,2,1,0:T(8,128)(2,1)S(1)}, u32[]{:S(2)}, u32[]{:S(2)}) collective-permute-start(bf16[2,5,256,128]{3,2,1,0:T(8,128)(2,1)S(1)} %join.3.refs_4_), channel_id=1, source_target_pairs={{4,0},{8,4},{12,8},{5,1},{9,5},{13,9},{6,2},{10,6},{14,10},{7,3},{... | collective-permute-start | bytes 1966088 | tf_op jit(solution)/shard_map/ppermute | solution.py:284
  27.1 0.0 collective-permute-done.3.refs_1_
  27.1 8.2 %collective-permute-done.4.refs_2_ = bf16[2,5,64,128]{3,2,1,0:T(8,128)(2,1)S(1)} collective-permute-done((bf16[2,5,64,128]{3,2,1,0:T(8,128)(2,1)S(1)}, bf16[2,5,64,128]{3,2,1,0:T(8,128)(2,1)S(1)}, u32[]{:S(2)}, u32[]{:S(2)}) %collective-permute-start.4) | collective-permute-done | bytes 163872 | tf_op jit(solution)/shard_map/ppermute | solution.py:255
  35.3 0.0 collective-permute-done.5.refs_3_
  35.3 0.2 join.2.refs_4_
  35.5 2.0 %collective-permute-start.6 = (bf16[2,5,256,128]{3,2,1,0:T(8,128)(2,1)S(1)}, bf16[2,5,256,128]{3,2,1,0:T(8,128)(2,1)S(1)}, u32[]{:S(2)}, u32[]{:S(2)}) collective-permute-start(bf16[2,5,256,128]{3,2,1,0:T(8,128)(2,1)S(1)} %join.2.refs_4_), channel_id=1, source_target_pairs={{0,4},{4,8},{8,12},{1,5},{5,9},{9,13},{2,6},{6,10},{10,14},{3,7},{... | collective-permute-start | bytes 1966088 | tf_op jit(solution)/shard_map/ppermute | solution.py:283
  37.5 1.3 %collective-permute-start.7 = (bf16[2,5,256,128]{3,2,1,0:T(8,128)(2,1)S(1)}, bf16[2,5,256,128]{3,2,1,0:T(8,128)(2,1)S(1)}, u32[]{:S(2)}, u32[]{:S(2)}) collective-permute-start(bf16[2,5,256,128]{3,2,1,0:T(8,128)(2,1)S(1)} %join.2.refs_4_), channel_id=1, source_target_pairs={{4,0},{8,4},{12,8},{5,1},{9,5},{13,9},{6,2},{10,6},{14,10},{7,3},{... | collective-permute-start | bytes 1966088 | tf_op jit(solution)/shard_map/ppermute | solution.py:284
  38.8 1.0 %pack.6 = (bf16[1,5,64,128]{3,2,1,0:T(8,128)(2,1)S(1)}, bf16[1,5,64,128]{3,2,1,0:T(8,128)(2,1)S(1)}, bf16[1,5,64,128]{3,2,1,0:T(8,128)(2,1)S(1)}, bf16[1,5,64,128]{3,2,1,0:T(8,128)(2,1)S(1)}) custom-call(s32[40]{0:T(128)S(1)} %copy-done.14, bf16[64,5120]{1,0:T(8,128)(2,1)S(1)} %copy-done.2), custom_call_target="tpu_custom_call" | custom-call | bytes 655360 | tf_op jit(solution)/shard_map/pack/pallas_call | solution.py:56
  39.9 4.1 %collective-permute-start.11 = (bf16[1,5,64,128]{3,2,1,0:T(8,128)(2,1)S(1)}, bf16[1,5,64,128]{3,2,1,0:T(8,128)(2,1)S(1)}, u32[]{:S(2)}, u32[]{:S(2)}) collective-permute-start(bf16[1,5,64,128]{3,2,1,0:T(8,128)(2,1)S(1)} %get-tuple-element.41), channel_id=1, source_target_pairs={{0,1},{1,2},{2,3},{3,0},{4,5},{5,6},{6,7},{7,4},{8,9},{9,10},{10,1... | collective-permute-start | bytes 245768 | tf_op jit(solution)/shard_map/ppermute | solution.py:255
  44.0 3.1 %collective-permute-done.11.refs_1_ = bf16[1,5,64,128]{3,2,1,0:T(8,128)(2,1)S(1)} collective-permute-done((bf16[1,5,64,128]{3,2,1,0:T(8,128)(2,1)S(1)}, bf16[1,5,64,128]{3,2,1,0:T(8,128)(2,1)S(1)}, u32[]{:S(2)}, u32[]{:S(2)}) %collective-permute-start.11) | collective-permute-done | bytes 81952 | tf_op jit(solution)/shard_map/ppermute | solution.py:255
  47.1 0.7 collective-permute-start.12
  47.9 6.6 %collective-permute-done.12.refs_2_ = bf16[1,5,64,128]{3,2,1,0:T(8,128)(2,1)S(1)} collective-permute-done((bf16[1,5,64,128]{3,2,1,0:T(8,128)(2,1)S(1)}, bf16[1,5,64,128]{3,2,1,0:T(8,128)(2,1)S(1)}, u32[]{:S(2)}, u32[]{:S(2)}) %collective-permute-start.12) | collective-permute-done | bytes 81952 | tf_op jit(solution)/shard_map/ppermute | solution.py:255
  54.5 2.3 %collective-permute-start.13 = (bf16[1,5,64,128]{3,2,1,0:T(8,128)(2,1)S(1)}, bf16[1,5,64,128]{3,2,1,0:T(8,128)(2,1)S(1)}, u32[]{:S(2)}, u32[]{:S(2)}) collective-permute-start(bf16[1,5,64,128]{3,2,1,0:T(8,128)(2,1)S(1)} %get-tuple-element.43), channel_id=1, source_target_pairs={{0,3},{1,0},{2,1},{3,2},{4,7},{5,4},{6,5},{7,6},{8,11},{9,8},{10,9... | collective-permute-start | bytes 245768 | tf_op jit(solution)/shard_map/ppermute | solution.py:255
  56.7 1.5 %pack.4 = (bf16[1,5,64,128]{3,2,1,0:T(8,128)(2,1)S(1)}, bf16[1,5,64,128]{3,2,1,0:T(8,128)(2,1)}, bf16[1,5,64,128]{3,2,1,0:T(8,128)(2,1)}, bf16[1,5,64,128]{3,2,1,0:T(8,128)(2,1)}) custom-call(s32[40]{0:T(128)S(1)} %copy-done.14, bf16[64,5120]{1,0:T(8,128)(2,1)S(1)} %copy-done.2), custom_call_target="tpu_custom_call" | custom-call | bytes 655360 | tf_op jit(solution)/shard_map/pack/pallas_call | solution.py:56
  58.3 0.0 copy-start.15
  58.3 1.0 %collective-permute-done.13.refs_3_ = bf16[1,5,64,128]{3,2,1,0:T(8,128)(2,1)S(1)} collective-permute-done((bf16[1,5,64,128]{3,2,1,0:T(8,128)(2,1)S(1)}, bf16[1,5,64,128]{3,2,1,0:T(8,128)(2,1)S(1)}, u32[]{:S(2)}, u32[]{:S(2)}) %collective-permute-start.13) | collective-permute-done | bytes 81952 | tf_op jit(solution)/shard_map/ppermute | solution.py:255
  59.3 0.6 copy-done.11
  59.9 0.0 collective-permute-start
  59.9 0.0 collective-permute-done.17.refs_5_
  59.9 4.3 %collective-permute-start.1 = (bf16[1,5,64,128]{3,2,1,0:T(8,128)(2,1)}, bf16[1,5,64,128]{3,2,1,0:T(8,128)(2,1)S(1)}, u32[]{:S(2)}, u32[]{:S(2)}) collective-permute-start(bf16[1,5,64,128]{3,2,1,0:T(8,128)(2,1)} %get-tuple-element.30), channel_id=1, source_target_pairs={{0,2},{1,3},{2,0},{3,1},{4,6},{5,7},{6,4},{7,5},{8,10},{9,11},{10,... | collective-permute-start | bytes 245768 | tf_op jit(solution)/shard_map/ppermute | solution.py:255
  64.2 0.0 collective-permute-done.18.refs_6_
  64.2 0.8 copy-done.3
  65.0 0.0 collective-permute-start.2
  65.0 0.7 copy.8
  65.7 0.9 reshape.7.mask
  66.7 0.0 copy-start.4
  66.7 1.1 %copy-done.4 = bf16[2,5,256,128]{3,2,1,0:T(8,128)(2,1)S(1)} copy-done((bf16[2,5,256,128]{3,2,1,0:T(8,128)(2,1)S(1)}, bf16[2,5,256,128]{3,2,1,0:T(8,128)(2,1)}, u32[]{:S(2)}) %copy-start.4) | copy-done | bytes 655384
  67.8 0.9 copy-done.6
  68.6 0.9 copy-done.8
  69.5 0.9 copy-done.10
  70.4 0.9 copy-done.12
  71.3 3.9 %attend.3 = (bf16[5,64,128]{2,1,0:T(8,128)(2,1)S(1)}, bf16[5,64,128]{2,1,0:T(8,128)(2,1)S(1)}, bf16[5,64,128]{2,1,0:T(8,128)(2,1)S(1)}, bf16[5,64,128]{2,1,0:T(8,128)(2,1)S(1)}, f32[5,256]{1,0:T(8,128)S(1)}) custom-call(s32[40]{0:T(128)S(1)} %copy-done.14, s32[400]{0:T(512)S(1)} %reshape.7.mask, bf16[1,5,64,128]{3,2,1,0:T(8,128)(2,1)S(1)} %copy-done.6, ...), custom_call_target="tpu_custom_call" | custom-call | flops 419430400 | bytes 2621440 | tf_op jit(solution)/shard_map/attend/pallas_call | solution.py:182
  75.2 0.0 collective-permute-done.refs_1_
  75.2 2.1 %collective-permute-start.19 = (bf16[5,64,128]{2,1,0:T(8,128)(2,1)S(1)}, bf16[5,64,128]{2,1,0:T(8,128)(2,1)S(1)}, u32[]{:S(2)}, u32[]{:S(2)}) collective-permute-start(bf16[5,64,128]{2,1,0:T(8,128)(2,1)S(1)} %get-tuple-element.49), channel_id=1, source_target_pairs={{0,1},{1,2},{2,3},{3,0},{4,5},{5,6},{6,7},{7,4},{8,9},{9,10},{10,1... | collective-permute-start | bytes 245768 | tf_op jit(solution)/shard_map/ppermute | solution.py:255
  77.3 0.0 collective-permute-done.1.refs_2_
  77.3 0.0 collective-permute-start.20
  77.3 2.5 %collective-permute-start.21 = (bf16[5,64,128]{2,1,0:T(8,128)(2,1)S(1)}, bf16[5,64,128]{2,1,0:T(8,128)(2,1)S(1)}, u32[]{:S(2)}, u32[]{:S(2)}) collective-permute-start(bf16[5,64,128]{2,1,0:T(8,128)(2,1)S(1)} %get-tuple-element.51), channel_id=1, source_target_pairs={{0,3},{1,0},{2,1},{3,2},{4,7},{5,4},{6,5},{7,6},{8,11},{9,8},{10,9... | collective-permute-start | bytes 245768 | tf_op jit(solution)/shard_map/ppermute | solution.py:255
  79.8 4.2 %attend.2 = (bf16[5,64,128]{2,1,0:T(8,128)(2,1)S(1)}, bf16[5,64,128]{2,1,0:T(8,128)(2,1)S(1)}, bf16[5,64,128]{2,1,0:T(8,128)(2,1)S(1)}, bf16[5,64,128]{2,1,0:T(8,128)(2,1)S(1)}, f32[5,256]{1,0:T(8,128)S(1)}) custom-call(s32[40]{0:T(128)S(1)} %copy-done.14, s32[400]{0:T(512)S(1)} %reshape.7.mask, bf16[1,5,64,128]{3,2,1,0:T(8,128)(2,1)S(1)} %get-tuple-element.28.refs_0_, ...), custom_call_target="tpu_custom_call" | custom-call | flops 419430400 | bytes 2621440 | tf_op jit(solution)/shard_map/attend/pallas_call | solution.py:182
  84.1 1.9 %collective-permute-start.10 = (bf16[5,64,128]{2,1,0:T(8,128)(2,1)S(1)}, bf16[5,64,128]{2,1,0:T(8,128)(2,1)S(1)}, u32[]{:S(2)}, u32[]{:S(2)}) collective-permute-start(bf16[5,64,128]{2,1,0:T(8,128)(2,1)S(1)} %get-tuple-element.39), channel_id=1, source_target_pairs={{0,3},{1,0},{2,1},{3,2},{4,7},{5,4},{6,5},{7,6},{8,11},{9,8},{10,9... | collective-permute-start | bytes 245768 | tf_op jit(solution)/shard_map/ppermute | solution.py:255
  86.0 0.1 collective-permute-start.8
  86.1 0.0 collective-permute-done.19.refs_1_
  86.1 1.3 %collective-permute-start.9 = (bf16[5,64,128]{2,1,0:T(8,128)(2,1)S(1)}, bf16[5,64,128]{2,1,0:T(8,128)(2,1)S(1)}, u32[]{:S(2)}, u32[]{:S(2)}) collective-permute-start(bf16[5,64,128]{2,1,0:T(8,128)(2,1)S(1)} %get-tuple-element.38), channel_id=1, source_target_pairs={{0,2},{1,3},{2,0},{3,1},{4,6},{5,7},{6,4},{7,5},{8,10},{9,11},{10,... | collective-permute-start | bytes 245768 | tf_op jit(solution)/shard_map/ppermute | solution.py:255
  87.4 0.6 pad_maximum_fusion
  88.0 1.5 %unpack.2.refs_4_ = bf16[64,5120]{1,0:T(8,128)(2,1)} custom-call(s32[40]{0:T(128)S(1)} %copy-done.14, bf16[5,64,128]{2,1,0:T(8,128)(2,1)S(1)} %get-tuple-element.48.refs_0_, bf16[5,64,128]{2,1,0:T(8,128)(2,1)S(1)} %collective-permute-done.19.refs_1_, bf16[5,64,128]{2,1,0:T(8,128)(2,1)S(1)} %collective-permute-done.20.refs_2_, ...), custom_call_target="tpu_custom_call" | custom-call | bytes 655360 | tf_op jit(solution)/shard_map/unpack/pallas_call | solution.py:233
  89.6 0.2 collective-permute-done.10.refs_3_
  89.8 2.5 %collective-permute-done.8.refs_1_ = bf16[5,64,128]{2,1,0:T(8,128)(2,1)S(1)} collective-permute-done((bf16[5,64,128]{2,1,0:T(8,128)(2,1)S(1)}, bf16[5,64,128]{2,1,0:T(8,128)(2,1)S(1)}, u32[]{:S(2)}, u32[]{:S(2)}) %collective-permute-start.8) | collective-permute-done | bytes 81952 | tf_op jit(solution)/shard_map/ppermute | solution.py:255
  92.3 0.9 collective-permute-done.9.refs_2_
  93.2 1.5 %unpack.3 = bf16[64,5120]{1,0:T(8,128)(2,1)} custom-call(s32[40]{0:T(128)S(1)} %copy-done.14, bf16[5,64,128]{2,1,0:T(8,128)(2,1)S(1)} %get-tuple-element.36.refs_0_, bf16[5,64,128]{2,1,0:T(8,128)(2,1)S(1)} %collective-permute-done.8.refs_1_, bf16[5,64,128]{2,1,0:T(8,128)(2,1)S(1)} %collective-permute-done.9.refs_2_, ...), custom_call_target="tpu_custom_call", output_to_operand_aliasing={{}: (5, {})} | custom-call | bytes 655360 | tf_op jit(solution)/shard_map/unpack/pallas_call | solution.py:233
  (25 shorter events, 0.0 us)
Async XLA Ops:
  0.6 1.1 %copy-start = (bf16[64,5120]{1,0:T(8,128)(2,1)S(1)}, bf16[64,5120]{1,0:T(8,128)(2,1)}, u32[]{:S(2)}) copy-start(bf16[64,5120]{1,0:T(8,128)(2,1)} %refs_0_.7) | copy-start | bytes 1966084
  1.7 1.1 %copy-start.1 = (bf16[64,5120]{1,0:T(8,128)(2,1)S(1)}, bf16[64,5120]{1,0:T(8,128)(2,1)}, u32[]{:S(2)}) copy-start(bf16[64,5120]{1,0:T(8,128)(2,1)} %refs_1_.3) | copy-start | bytes 1966084
  2.8 0.7 copy-start.13
  4.8 10.2 %collective-permute-start.14 = (bf16[2,5,64,128]{3,2,1,0:T(8,128)(2,1)S(1)}, bf16[2,5,64,128]{3,2,1,0:T(8,128)(2,1)S(1)}, u32[]{:S(2)}, u32[]{:S(2)}) collective-permute-start(bf16[2,5,64,128]{3,2,1,0:T(8,128)(2,1)S(1)} %get-tuple-element.45), channel_id=1, source_target_pairs={{0,1},{1,2},{2,3},{3,0},{4,5},{5,6},{6,7},{7,4},{8,9},{9,10},{10,1... | collective-permute-start | bytes 491528 | tf_op jit(solution)/shard_map/ppermute | solution.py:255
  7.9 14.2 %collective-permute-start.15 = (bf16[2,5,64,128]{3,2,1,0:T(8,128)(2,1)S(1)}, bf16[2,5,64,128]{3,2,1,0:T(8,128)(2,1)S(1)}, u32[]{:S(2)}, u32[]{:S(2)}) collective-permute-start(bf16[2,5,64,128]{3,2,1,0:T(8,128)(2,1)S(1)} %get-tuple-element.46), channel_id=1, source_target_pairs={{0,2},{1,3},{2,0},{3,1},{4,6},{5,7},{6,4},{7,5},{8,10},{9,11},{10,... | collective-permute-start | bytes 491528 | tf_op jit(solution)/shard_map/ppermute | solution.py:255
  10.5 13.8 %collective-permute-start.16 = (bf16[2,5,64,128]{3,2,1,0:T(8,128)(2,1)S(1)}, bf16[2,5,64,128]{3,2,1,0:T(8,128)(2,1)S(1)}, u32[]{:S(2)}, u32[]{:S(2)}) collective-permute-start(bf16[2,5,64,128]{3,2,1,0:T(8,128)(2,1)S(1)} %get-tuple-element.47), channel_id=1, source_target_pairs={{0,3},{1,0},{2,1},{3,2},{4,7},{5,4},{6,5},{7,6},{8,11},{9,8},{10,9... | collective-permute-start | bytes 491528 | tf_op jit(solution)/shard_map/ppermute | solution.py:255
  13.2 14.0 %collective-permute-start.3 = (bf16[2,5,64,128]{3,2,1,0:T(8,128)(2,1)S(1)}, bf16[2,5,64,128]{3,2,1,0:T(8,128)(2,1)S(1)}, u32[]{:S(2)}, u32[]{:S(2)}) collective-permute-start(bf16[2,5,64,128]{3,2,1,0:T(8,128)(2,1)S(1)} %get-tuple-element.33), channel_id=1, source_target_pairs={{0,1},{1,2},{2,3},{3,0},{4,5},{5,6},{6,7},{7,4},{8,9},{9,10},{10,1... | collective-permute-start | bytes 491528 | tf_op jit(solution)/shard_map/ppermute | solution.py:255
  13.9 21.4 %collective-permute-start.4 = (bf16[2,5,64,128]{3,2,1,0:T(8,128)(2,1)S(1)}, bf16[2,5,64,128]{3,2,1,0:T(8,128)(2,1)S(1)}, u32[]{:S(2)}, u32[]{:S(2)}) collective-permute-start(bf16[2,5,64,128]{3,2,1,0:T(8,128)(2,1)S(1)} %get-tuple-element.34), channel_id=1, source_target_pairs={{0,2},{1,3},{2,0},{3,1},{4,6},{5,7},{6,4},{7,5},{8,10},{9,11},{10,... | collective-permute-start | bytes 491528 | tf_op jit(solution)/shard_map/ppermute | solution.py:255
  15.0 20.3 %collective-permute-start.5 = (bf16[2,5,64,128]{3,2,1,0:T(8,128)(2,1)S(1)}, bf16[2,5,64,128]{3,2,1,0:T(8,128)(2,1)S(1)}, u32[]{:S(2)}, u32[]{:S(2)}) collective-permute-start(bf16[2,5,64,128]{3,2,1,0:T(8,128)(2,1)S(1)} %get-tuple-element.35), channel_id=1, source_target_pairs={{0,3},{1,0},{2,1},{3,2},{4,7},{5,4},{6,5},{7,6},{8,11},{9,8},{10,9... | collective-permute-start | bytes 491528 | tf_op jit(solution)/shard_map/ppermute | solution.py:255
  24.5 35.4 %collective-permute-start.17 = (bf16[2,5,256,128]{3,2,1,0:T(8,128)(2,1)S(1)}, bf16[2,5,256,128]{3,2,1,0:T(8,128)(2,1)S(1)}, u32[]{:S(2)}, u32[]{:S(2)}) collective-permute-start(bf16[2,5,256,128]{3,2,1,0:T(8,128)(2,1)S(1)} %join.3.refs_4_), channel_id=1, source_target_pairs={{0,4},{4,8},{8,12},{1,5},{5,9},{9,13},{2,6},{6,10},{10,14},{3,7},{... | collective-permute-start | bytes 1966088 | tf_op jit(solution)/shard_map/ppermute | solution.py:283
  25.8 38.3 %collective-permute-start.18 = (bf16[2,5,256,128]{3,2,1,0:T(8,128)(2,1)S(1)}, bf16[2,5,256,128]{3,2,1,0:T(8,128)(2,1)S(1)}, u32[]{:S(2)}, u32[]{:S(2)}) collective-permute-start(bf16[2,5,256,128]{3,2,1,0:T(8,128)(2,1)S(1)} %join.3.refs_4_), channel_id=1, source_target_pairs={{4,0},{8,4},{12,8},{5,1},{9,5},{13,9},{6,2},{10,6},{14,10},{7,3},{... | collective-permute-start | bytes 1966088 | tf_op jit(solution)/shard_map/ppermute | solution.py:284
  35.3 3.5 %copy-start.2 = (bf16[64,5120]{1,0:T(8,128)(2,1)S(1)}, bf16[64,5120]{1,0:T(8,128)(2,1)}, u32[]{:S(2)}) copy-start(bf16[64,5120]{1,0:T(8,128)(2,1)} %refs_0_.6) | copy-start | bytes 1966084
  35.3 3.5 %copy-start.14 = (s32[40]{0:T(128)S(1)}, s32[40]{0:T(128)}, u32[]{:S(2)}) copy-start(s32[40]{0:T(128)} %head_slot.15) | copy-start | bytes 484
  35.5 44.3 %collective-permute-start.6 = (bf16[2,5,256,128]{3,2,1,0:T(8,128)(2,1)S(1)}, bf16[2,5,256,128]{3,2,1,0:T(8,128)(2,1)S(1)}, u32[]{:S(2)}, u32[]{:S(2)}) collective-permute-start(bf16[2,5,256,128]{3,2,1,0:T(8,128)(2,1)S(1)} %join.2.refs_4_), channel_id=1, source_target_pairs={{0,4},{4,8},{8,12},{1,5},{5,9},{9,13},{2,6},{6,10},{10,14},{3,7},{... | collective-permute-start | bytes 1966088 | tf_op jit(solution)/shard_map/ppermute | solution.py:283
  37.5 42.3 %collective-permute-start.7 = (bf16[2,5,256,128]{3,2,1,0:T(8,128)(2,1)S(1)}, bf16[2,5,256,128]{3,2,1,0:T(8,128)(2,1)S(1)}, u32[]{:S(2)}, u32[]{:S(2)}) collective-permute-start(bf16[2,5,256,128]{3,2,1,0:T(8,128)(2,1)S(1)} %join.2.refs_4_), channel_id=1, source_target_pairs={{4,0},{8,4},{12,8},{5,1},{9,5},{13,9},{6,2},{10,6},{14,10},{7,3},{... | collective-permute-start | bytes 1966088 | tf_op jit(solution)/shard_map/ppermute | solution.py:284
  39.9 18.4 %copy-start.5 = (bf16[1,5,64,128]{3,2,1,0:T(8,128)(2,1)}, bf16[1,5,64,128]{3,2,1,0:T(8,128)(2,1)S(1)}, u32[]{:S(2)}) copy-start(bf16[1,5,64,128]{3,2,1,0:T(8,128)(2,1)S(1)} %get-tuple-element.40.refs_0_) | copy-start | bytes 245764
  39.9 7.3 %collective-permute-start.11 = (bf16[1,5,64,128]{3,2,1,0:T(8,128)(2,1)S(1)}, bf16[1,5,64,128]{3,2,1,0:T(8,128)(2,1)S(1)}, u32[]{:S(2)}, u32[]{:S(2)}) collective-permute-start(bf16[1,5,64,128]{3,2,1,0:T(8,128)(2,1)S(1)} %get-tuple-element.41), channel_id=1, source_target_pairs={{0,1},{1,2},{2,3},{3,0},{4,5},{5,6},{6,7},{7,4},{8,9},{9,10},{10,1... | collective-permute-start | bytes 245768 | tf_op jit(solution)/shard_map/ppermute | solution.py:255
  47.1 11.1 %copy-start.7 = (bf16[1,5,64,128]{3,2,1,0:T(8,128)(2,1)}, bf16[1,5,64,128]{3,2,1,0:T(8,128)(2,1)S(1)}, u32[]{:S(2)}) copy-start(bf16[1,5,64,128]{3,2,1,0:T(8,128)(2,1)S(1)} %collective-permute-done.11.refs_1_) | copy-start | bytes 245764
  47.1 7.3 %collective-permute-start.12 = (bf16[1,5,64,128]{3,2,1,0:T(8,128)(2,1)S(1)}, bf16[1,5,64,128]{3,2,1,0:T(8,128)(2,1)S(1)}, u32[]{:S(2)}, u32[]{:S(2)}) collective-permute-start(bf16[1,5,64,128]{3,2,1,0:T(8,128)(2,1)S(1)} %get-tuple-element.42), channel_id=1, source_target_pairs={{0,2},{1,3},{2,0},{3,1},{4,6},{5,7},{6,4},{7,5},{8,10},{9,11},{10,... | collective-permute-start | bytes 245768 | tf_op jit(solution)/shard_map/ppermute | solution.py:255
  54.5 3.8 %copy-start.9 = (bf16[1,5,64,128]{3,2,1,0:T(8,128)(2,1)}, bf16[1,5,64,128]{3,2,1,0:T(8,128)(2,1)S(1)}, u32[]{:S(2)}) copy-start(bf16[1,5,64,128]{3,2,1,0:T(8,128)(2,1)S(1)} %collective-permute-done.12.refs_2_) | copy-start | bytes 245764
  54.5 4.8 %collective-permute-start.13 = (bf16[1,5,64,128]{3,2,1,0:T(8,128)(2,1)S(1)}, bf16[1,5,64,128]{3,2,1,0:T(8,128)(2,1)S(1)}, u32[]{:S(2)}, u32[]{:S(2)}) collective-permute-start(bf16[1,5,64,128]{3,2,1,0:T(8,128)(2,1)S(1)} %get-tuple-element.43), channel_id=1, source_target_pairs={{0,3},{1,0},{2,1},{3,2},{4,7},{5,4},{6,5},{7,6},{8,11},{9,8},{10,9... | collective-permute-start | bytes 245768 | tf_op jit(solution)/shard_map/ppermute | solution.py:255
  58.3 6.7 %copy-start.15 = (s32[40,2,5]{0,1,2:T(2,128)S(1)}, s32[40,2,5]{0,1,2:T(2,128)}, u32[]{:S(2)}) copy-start(s32[40,2,5]{0,1,2:T(2,128)} %param.8) | copy-start | bytes 4804
  59.3 0.6 copy-start.11
  59.9 15.3 %collective-permute-start = (bf16[1,5,64,128]{3,2,1,0:T(8,128)(2,1)}, bf16[1,5,64,128]{3,2,1,0:T(8,128)(2,1)S(1)}, u32[]{:S(2)}, u32[]{:S(2)}) collective-permute-start(bf16[1,5,64,128]{3,2,1,0:T(8,128)(2,1)} %get-tuple-element.29), channel_id=1, source_target_pairs={{0,1},{1,2},{2,3},{3,0},{4,5},{5,6},{6,7},{7,4},{8,9},{9,10},{10,1... | collective-permute-start | bytes 245768 | tf_op jit(solution)/shard_map/ppermute | solution.py:255
  59.9 17.4 %collective-permute-start.1 = (bf16[1,5,64,128]{3,2,1,0:T(8,128)(2,1)}, bf16[1,5,64,128]{3,2,1,0:T(8,128)(2,1)S(1)}, u32[]{:S(2)}, u32[]{:S(2)}) collective-permute-start(bf16[1,5,64,128]{3,2,1,0:T(8,128)(2,1)} %get-tuple-element.30), channel_id=1, source_target_pairs={{0,2},{1,3},{2,0},{3,1},{4,6},{5,7},{6,4},{7,5},{8,10},{9,11},{10,... | collective-permute-start | bytes 245768 | tf_op jit(solution)/shard_map/ppermute | solution.py:255
  64.2 0.8 copy-start.3
  65.0 12.3 %collective-permute-start.2 = (bf16[1,5,64,128]{3,2,1,0:T(8,128)(2,1)}, bf16[1,5,64,128]{3,2,1,0:T(8,128)(2,1)}, u32[]{:S(2)}, u32[]{:S(2)}) collective-permute-start(bf16[1,5,64,128]{3,2,1,0:T(8,128)(2,1)} %get-tuple-element.31), channel_id=1, source_target_pairs={{0,3},{1,0},{2,1},{3,2},{4,7},{5,4},{6,5},{7,6},{8,11},{9,8},{10,9... | collective-permute-start | bytes 245768 | tf_op jit(solution)/shard_map/ppermute | solution.py:255
  66.7 1.1 %copy-start.4 = (bf16[2,5,256,128]{3,2,1,0:T(8,128)(2,1)S(1)}, bf16[2,5,256,128]{3,2,1,0:T(8,128)(2,1)}, u32[]{:S(2)}) copy-start(bf16[2,5,256,128]{3,2,1,0:T(8,128)(2,1)} %copy-done.3) | copy-start | bytes 1966084
  67.8 0.9 copy-start.6
  68.6 0.9 copy-start.8
  69.5 0.9 copy-start.10
  70.4 0.9 copy-start.12
  75.2 10.9 %collective-permute-start.19 = (bf16[5,64,128]{2,1,0:T(8,128)(2,1)S(1)}, bf16[5,64,128]{2,1,0:T(8,128)(2,1)S(1)}, u32[]{:S(2)}, u32[]{:S(2)}) collective-permute-start(bf16[5,64,128]{2,1,0:T(8,128)(2,1)S(1)} %get-tuple-element.49), channel_id=1, source_target_pairs={{0,1},{1,2},{2,3},{3,0},{4,5},{5,6},{6,7},{7,4},{8,9},{9,10},{10,1... | collective-permute-start | bytes 245768 | tf_op jit(solution)/shard_map/ppermute | solution.py:255
  77.3 10.7 %collective-permute-start.20 = (bf16[5,64,128]{2,1,0:T(8,128)(2,1)S(1)}, bf16[5,64,128]{2,1,0:T(8,128)(2,1)S(1)}, u32[]{:S(2)}, u32[]{:S(2)}) collective-permute-start(bf16[5,64,128]{2,1,0:T(8,128)(2,1)S(1)} %get-tuple-element.50), channel_id=1, source_target_pairs={{0,2},{1,3},{2,0},{3,1},{4,6},{5,7},{6,4},{7,5},{8,10},{9,11},{10,... | collective-permute-start | bytes 245768 | tf_op jit(solution)/shard_map/ppermute | solution.py:255
  77.3 10.7 %collective-permute-start.21 = (bf16[5,64,128]{2,1,0:T(8,128)(2,1)S(1)}, bf16[5,64,128]{2,1,0:T(8,128)(2,1)S(1)}, u32[]{:S(2)}, u32[]{:S(2)}) collective-permute-start(bf16[5,64,128]{2,1,0:T(8,128)(2,1)S(1)} %get-tuple-element.51), channel_id=1, source_target_pairs={{0,3},{1,0},{2,1},{3,2},{4,7},{5,4},{6,5},{7,6},{8,11},{9,8},{10,9... | collective-permute-start | bytes 245768 | tf_op jit(solution)/shard_map/ppermute | solution.py:255
  84.1 5.7 %collective-permute-start.10 = (bf16[5,64,128]{2,1,0:T(8,128)(2,1)S(1)}, bf16[5,64,128]{2,1,0:T(8,128)(2,1)S(1)}, u32[]{:S(2)}, u32[]{:S(2)}) collective-permute-start(bf16[5,64,128]{2,1,0:T(8,128)(2,1)S(1)} %get-tuple-element.39), channel_id=1, source_target_pairs={{0,3},{1,0},{2,1},{3,2},{4,7},{5,4},{6,5},{7,6},{8,11},{9,8},{10,9... | collective-permute-start | bytes 245768 | tf_op jit(solution)/shard_map/ppermute | solution.py:255
  86.0 6.3 %collective-permute-start.8 = (bf16[5,64,128]{2,1,0:T(8,128)(2,1)S(1)}, bf16[5,64,128]{2,1,0:T(8,128)(2,1)S(1)}, u32[]{:S(2)}, u32[]{:S(2)}) collective-permute-start(bf16[5,64,128]{2,1,0:T(8,128)(2,1)S(1)} %get-tuple-element.37), channel_id=1, source_target_pairs={{0,1},{1,2},{2,3},{3,0},{4,5},{5,6},{6,7},{7,4},{8,9},{9,10},{10,1... | collective-permute-start | bytes 245768 | tf_op jit(solution)/shard_map/ppermute | solution.py:255
  86.1 7.1 %collective-permute-start.9 = (bf16[5,64,128]{2,1,0:T(8,128)(2,1)S(1)}, bf16[5,64,128]{2,1,0:T(8,128)(2,1)S(1)}, u32[]{:S(2)}, u32[]{:S(2)}) collective-permute-start(bf16[5,64,128]{2,1,0:T(8,128)(2,1)S(1)} %get-tuple-element.38), channel_id=1, source_target_pairs={{0,2},{1,3},{2,0},{3,1},{4,6},{5,7},{6,4},{7,5},{8,10},{9,11},{10,... | collective-permute-start | bytes 245768 | tf_op jit(solution)/shard_map/ppermute | solution.py:255

commit v2 on v1

v2 whole, which is shorter than its diff:
```python
import functools
import math

import jax
import jax.numpy as jnp
from jax import lax
from jax.experimental import pallas as pl
from jax.experimental.pallas import tpu as pltpu
from jax.sharding import PartitionSpec as P

HBM = pl.BlockSpec(memory_space=pltpu.HBM)
ANY = pl.BlockSpec(memory_space=pl.ANY)
SMEM = pl.BlockSpec(memory_space=pltpu.SMEM)
VMEM = pl.BlockSpec(memory_space=pltpu.VMEM)
SMALL = pltpu.CompilerParams(vmem_limit_bytes=4 * 1024 * 1024)
LARGE = pltpu.CompilerParams(vmem_limit_bytes=16 * 1024 * 1024)


def in_hbm(x):
    return pltpu.with_memory_space_constraint(x, pltpu.HBM)


def cost(nbytes, flops=0, transcendentals=0):
    return pl.CostEstimate(flops=flops, bytes_accessed=nbytes, transcendentals=transcendentals)


def invert(head_slot, head_of, used=None):
    for j in range(head_of.shape[0]):
        head_of[j] = 0
        if used is not None:
            used[j] = 0
    for h in range(head_slot.shape[0]):
        head_of[head_slot[h]] = h
        if used is not None:
            used[head_slot[h]] = 1


def pack_kernel(owners, capacity, dim, parts, sources, waited, head_slot, *refs):
    rows = refs[:sources]
    outs = refs[sources + waited : sources + waited + owners]
    held = refs[sources + waited + owners : 2 * sources + waited + owners]
    slots, head_of, sem, sem_slots = refs[2 * sources + waited + owners :]
    me = lax.axis_index("head")
    slot_copy = pltpu.make_async_copy(head_slot, slots, sem_slots)
    slot_copy.start()
    chunks = sem.shape[1]
    size = rows[0].shape[0] // chunks
    copies = []
    for i in range(sources):
        for j in range(chunks):
            place = pl.ds(j * size, size)
            copies.append(
                pltpu.make_async_copy(rows[i].at[place], held[i].at[place], sem.at[i, j])
            )
            copies[-1].start()
    slot_copy.wait()
    invert(slots, head_of)
    for copy in copies:
        copy.wait()
    for k in range(owners):
        owner = lax.rem(me + k, owners)
        place = 0
        for source, first, count in parts:
            for c in range(count):
                head = head_of[owner * capacity + first + c]
                columns = pl.ds(pl.multiple_of(head * dim, dim), dim)
                outs[k][place] = held[source][:, columns]
                place += 1


def pack(head_slot, parts, owners, capacity, dim, after=()):
    rows = [row for row, _, _ in parts]
    total = sum(count for _, _, count in parts)
    tokens = rows[0].shape[0]
    shape = jax.ShapeDtypeStruct((total, tokens, dim), rows[0].dtype)
    places = tuple((i, first, count) for i, (_, first, count) in enumerate(parts))
    chunks = max(tokens // 16, 1)
    return pl.pallas_call(
        functools.partial(pack_kernel, owners, capacity, dim, places, len(rows), len(after)),
        out_shape=[shape] * owners,
        in_specs=[ANY] * (1 + len(rows) + len(after)),
        out_specs=[VMEM] * owners,
        scratch_shapes=[pltpu.VMEM(row.shape, row.dtype) for row in rows]
        + [
            pltpu.SMEM(head_slot.shape, jnp.int32),
            pltpu.SMEM((owners * capacity,), jnp.int32),
            pltpu.SemaphoreType.DMA((len(rows), chunks)),
            pltpu.SemaphoreType.DMA,
        ],
        cost_estimate=cost(4 * owners * math.prod(shape.shape)),
        compiler_params=SMALL,
        name="pack",
    )(*[in_hbm(x) for x in (head_slot, *rows)], *after)


def join_kernel(owners, count, *refs):
    blocks, out, sem = refs[:owners], refs[owners], refs[owners + 1]
    me = lax.axis_index("head")
    tokens = blocks[0].shape[1]
    copies = []
    for k in range(owners):
        start = lax.rem(me - k + owners, owners) * tokens
        place = pl.ds(pl.multiple_of(start, tokens), tokens)
        copies.append(
            pltpu.make_async_copy(blocks[k].at[pl.ds(0, count)], out.at[:, place], sem.at[k])
        )
        copies[-1].start()
    for copy in copies:
        copy.wait()


def join(blocks, count):
    owners = len(blocks)
    _, t, d = blocks[0].shape
    shape = jax.ShapeDtypeStruct((count, t * owners, d), blocks[0].dtype)
    return pl.pallas_call(
        functools.partial(join_kernel, owners, count),
        out_shape=shape,
        in_specs=[ANY] * owners,
        out_specs=ANY,
        scratch_shapes=[pltpu.SemaphoreType.DMA((owners,))],
        cost_estimate=cost(4 * math.prod(shape.shape)),
        compiler_params=SMALL,
        name="join",
    )(*blocks)


def attend_kernel(owners, capacity, first, count, skip, tiles, tiles_all, band, *refs):
    head_slot, mask, mid, before, after = refs[:5]
    q_blocks = refs[5 : 5 + owners]
    outs = refs[5 + owners : 5 + 2 * owners]
    lse_ref, q_all, kv_all, o_all, mask_all, head_of, used, sem_q, sem_kv, sem_m = refs[
        5 + 2 * owners :
    ]
    me = lax.axis_index("head")
    tile_base = lax.axis_index("slab") * tiles
    _, tok, dim = q_blocks[0].shape
    reach = (band - 1) // 2
    rows = tok * owners // tiles
    halo, own = reach * rows, tiles * rows
    scale = dim ** (-0.5)
    base2 = scale * math.log2(math.e)

    mask_copy = pltpu.make_async_copy(mask, mask_all, sem_m)
    mask_copy.start()
    copies = []
    for k in range(owners):
        start = lax.rem(me - k + owners, owners) * tok
        place = pl.ds(pl.multiple_of(start, tok), tok)
        copies.append(
            pltpu.make_async_copy(
                q_blocks[k].at[pl.ds(skip, count)], q_all.at[:, place], sem_q.at[k]
            )
        )
    for i, (source, start, size) in enumerate(
        ((before, 0, halo), (mid, halo, own), (after, halo + own, halo))
    ):
        copies.append(
            pltpu.make_async_copy(source, kv_all.at[:, pl.ds(start, size)], sem_kv.at[i])
        )
    for copy in copies:
        copy.start()

    invert(head_slot, head_of, used)
    mask_copy.wait()

    for copy in copies:
        copy.wait()
    for c in range(count):
        slot = me * capacity + first + c
        head = head_of[slot]
        valid = used[slot] > 0
        for t in range(tiles):
            queries = q_all[c, t * rows : (t + 1) * rows, :]
            keys = kv_all[c, t * rows : (t + band) * rows, :]
            values = kv_all[count + c, t * rows : (t + band) * rows, :]
            scores = lax.dot_general(
                queries, keys, (((1,), (1,)), ((), ())), preferred_element_type=jnp.float32
            )
            kept = []
            for b in range(band):
                tile = tile_base + t + b - reach
                flag = mask_all[b, t, head]
                allowed = (flag > 0) & (tile >= 0) & (tile < tiles_all)
                part = scores[:, b * rows : (b + 1) * rows]
                kept.append(jnp.where(allowed, part, -1e30))
            masked = jnp.concatenate(kept, axis=1)
            highest = jnp.max(masked, axis=1, keepdims=True)
            weights = jnp.exp2((masked - highest) * base2)
            total = jnp.sum(weights, axis=1, keepdims=True)
            summed = jnp.dot(
                weights.astype(jnp.bfloat16), values, preferred_element_type=jnp.float32
            )
            o_all[c, t * rows : (t + 1) * rows, :] = (summed / total).astype(jnp.bfloat16)
            lse = jnp.where(valid, highest * scale + jnp.log(total), 0.0)
            lse_ref[c : c + 1, t * rows : (t + 1) * rows] = jnp.transpose(
                jnp.broadcast_to(lse, (rows, 128))
            )[0:1, :]

    for k in range(owners):
        place = pl.ds(pl.multiple_of(lax.rem(me + k, owners) * tok, tok), tok)
        outs[k][...] = o_all[:, place, :]


def attend(head_slot, mask, near, q_blocks, capacity, first, count, skip, tiles, tiles_all, band):
    owners = len(q_blocks)
    _, tok, dim = q_blocks[0].shape
    rows = tok * owners // tiles
    out = jax.ShapeDtypeStruct((count, tok, dim), jnp.bfloat16)
    pairs = count * tok * owners * band * rows
    extended = tok * owners + (band - 1) * rows
    return pl.pallas_call(
        functools.partial(
            attend_kernel, owners, capacity, first, count, skip, tiles, tiles_all, band
        ),
        out_shape=[out] * owners + [jax.ShapeDtypeStruct((count, tok * owners), jnp.float32)],
        in_specs=[SMEM, HBM] + [ANY] * (owners + 3),
        out_specs=[VMEM] * (owners + 1),
        scratch_shapes=[
            pltpu.VMEM((count, tok * owners, dim), jnp.bfloat16),
            pltpu.VMEM((2 * count, extended, dim), jnp.bfloat16),
            pltpu.VMEM((count, tok * owners, dim), jnp.bfloat16),
            pltpu.SMEM(mask.shape, jnp.int32),
            pltpu.SMEM((owners * capacity,), jnp.int32),
            pltpu.SMEM((owners * capacity,), jnp.int32),
            pltpu.SemaphoreType.DMA((owners,)),
            pltpu.SemaphoreType.DMA((3,)),
            pltpu.SemaphoreType.DMA,
        ],
        cost_estimate=cost(
            4 * count * dim * (extended + tok * owners), 4 * pairs * dim, pairs
        ),
        compiler_params=LARGE,
        name="attend",
    )(head_slot, mask, *near, *q_blocks)


def unpack_kernel(owners, capacity, first, count, dim, head_slot, *refs):
    blocks = refs[:owners]
    out, head_of, used, sem = refs[-4:]
    me = lax.axis_index("head")
    invert(head_slot, head_of, used)

    def each(act):
        for k in range(owners):
            owner = lax.rem(me - k + owners, owners)
            for c in range(count):
                slot = owner * capacity + first + c
                columns = pl.ds(pl.multiple_of(head_of[slot] * dim, dim), dim)
                copy = pltpu.make_async_copy(
                    blocks[k].at[c], out.at[:, columns], sem.at[k * count + c]
                )
                pl.when(used[slot] > 0)(functools.partial(act, copy))

    each(lambda copy: copy.start())
    each(lambda copy: copy.wait())


def unpack(head_slot, blocks, target, capacity, first, shape):
    owners = len(blocks)
    count, tok, dim = blocks[0].shape
    operands = list(blocks) + ([] if target is None else [target])
    return pl.pallas_call(
        functools.partial(unpack_kernel, owners, capacity, first, count, dim),
        out_shape=shape,
        in_specs=[SMEM] + [ANY] * owners + ([] if target is None else [HBM]),
        out_specs=HBM,
        input_output_aliases={} if target is None else {owners + 1: 0},
        scratch_shapes=[
            pltpu.SMEM((owners * capacity,), jnp.int32),
            pltpu.SMEM((owners * capacity,), jnp.int32),
            pltpu.SemaphoreType.DMA((owners * count,)),
        ],
        cost_estimate=cost(4 * owners * count * tok * dim),
        compiler_params=SMALL,
        name="unpack",
    )(head_slot, *operands)


def exchange(blocks):
    owners = len(blocks)
    order = sorted(range(1, owners), key=lambda k: abs(2 * k - owners))
    moved = {
        k: lax.ppermute(blocks[k], "head", [(i, (i + k) % owners) for i in range(owners)])
        for k in order
    }
    return [blocks[0]] + [moved[k] for k in range(1, owners)]


def on_device(query_rows, key_rows, value_rows, tile_mask, head_slot):
    owners = lax.axis_size("head")
    slabs = lax.axis_size("slab")
    tok_dev, width = query_rows.shape
    heads, tiles, band = tile_mask.shape
    dim = width // heads
    capacity = (heads + owners - 1) // owners
    tok_slab = tok_dev * owners
    halo = (band - 1) // 2 * (tok_slab // tiles)
    mask = jnp.transpose(tile_mask, (2, 1, 0))
    half = (capacity + 1) // 2
    groups = [g for g in ((0, half), (half, capacity - half)) if g[1]]
    up = [(i, i + 1) for i in range(slabs - 1)]
    down = [(j, i) for i, j in up]

    stages, near, wait_for = [], [], ()
    for stage in range(len(groups) + 1):
        parts = []
        if stage < len(groups):
            parts += [(key_rows, *groups[stage]), (value_rows, *groups[stage])]
        if stage > 0:
            parts.append((query_rows, *groups[stage - 1]))
        waits = ()
        blocks = exchange(pack(head_slot, parts, owners, capacity, dim, waits))
        stages.append(blocks)
        if stage < len(groups):
            mid = join(blocks, 2 * groups[stage][1])
            last = lax.slice_in_dim(mid, tok_slab - halo, tok_slab, axis=1)
            lead = lax.slice_in_dim(mid, 0, halo, axis=1)
            before = lax.ppermute(last, "slab", up)
            after = lax.ppermute(lead, "slab", down)
            near.append((mid, before, after))

    target, lses = None, []
    for g, (first, count) in enumerate(groups):
        skip = 2 * groups[g + 1][1] if g + 1 < len(groups) else 0
        sizes = (capacity, first, count, skip, tiles, tiles * slabs, band)
        *outs, lse = attend(head_slot, mask, near[g], stages[g + 1], *sizes)
        lses.append(lse)
        shape = jax.ShapeDtypeStruct(query_rows.shape, query_rows.dtype)
        target = unpack(head_slot, exchange(outs), target, capacity, first, shape)
    return target, jnp.concatenate(lses, axis=0)


def solution(mesh):
    rows = P(("groups", "slab", "head"), None)
    in_specs = (rows, rows, rows, P(None, ("groups", "slab"), None), P())
    out_specs = (rows, P("head", ("groups", "slab")))
    return jax.shard_map(
        on_device, mesh=mesh, in_specs=in_specs, out_specs=out_specs, check_vma=False
    )
```

time: 95.5 us -> 77 us (0.81)
  local copies, waits for them, and re-layouts: 10.6 us -> 0.01 us
  waiting for transfers between devices: 30.6 us -> 21.4 us
  starting transfers between devices: 35.3 us -> 36.6 us
    unnamed x33 -> x4, local copies, waits for them, and re-layouts: 9.65 us -> 0.01 us
    ppermute x18 -> x15, waiting for transfers between devices: 30.6 us -> 21.4 us  [exchange(): lax.ppermute(blocks[k], 'head', [(i, (i + k) % owners) for i in range(own...]
    ppermute x2, starting transfers between devices: 3.33 us -> 6.14 us  [on_device(): before = lax.ppermute(last, 'slab', up)]
    ppermute x18 -> x15, starting transfers between devices: 29.4 us -> 27.9 us  [exchange(): lax.ppermute(blocks[k], 'head', [(i, (i + k) % owners) for i in range(own...]
    pallas_call x2, Pallas kernels: 8.17 us -> 9.13 us  [attend(): pl.pallas_call(functools.partial(attend_kernel, owners, capacity, first,...]
    pallas_call x6 -> x5, Pallas kernels: 5.58 us -> 5.18 us  [the longest x3 4.87 us: pack(): pl.pallas_call(functools.partial(pack_kernel, owners, capacity, dim, plac...]
  transfers between devices with their start and end apart: 22 -> 19, of which waited for: 10 -> 6; matrix products, arithmetic and copies ran while one was open for 2% -> 1% of each run, Pallas kernels for 15% -> 19%
where the time goes in v2:
time: 77 us; the launch traced here: 76.7 us
  starting transfers between devices  36.6 us (48%)
  waiting for transfers between devices  21.4 us (28%)
  Pallas kernels  17.4 us (23%)
  between operations  0.77 us (1%)
    ppermute x15, starting transfers between devices, exchange(): lax.ppermute(blocks[k], 'head', [(i, (i + k) % owners) for i in range(own...  27.9 us
    ppermute x15, waiting for transfers between devices, exchange(): lax.ppermute(blocks[k], 'head', [(i, (i + k) % owners) for i in range(own...  21.4 us
    pallas_call x2, Pallas kernels, attend(): pl.pallas_call(functools.partial(attend_kernel, owners, capacity, first,...  9.13 us
    ppermute x2, starting transfers between devices, on_device(): before = lax.ppermute(last, 'slab', up)  6.14 us
    pallas_call x3, Pallas kernels, pack(): pl.pallas_call(functools.partial(pack_kernel, owners, capacity, dim, plac...  4.87 us
    pallas_call x2, Pallas kernels, unpack(): pl.pallas_call(functools.partial(unpack_kernel, owners, capacity, first,...  3.07 us
    ppermute x2, starting transfers between devices, on_device(): after = lax.ppermute(lead, 'slab', down)  2.58 us
  transfers between devices with their start and end apart: 19, of which 6 were waited for; matrix products, arithmetic and copies ran while one was open for 1% of the time, Pallas kernels for 19%

profile of v2, /device:TPU:0, one launch (start us, length us, event | category | flops | bytes accessed | tf_op | source)
XLA Modules:
  0.0 76.7 jit_solution(9325243033415449380)
XLA Ops:
  0.6 1.6 %pack.5 = (bf16[10,64,128]{2,1,0:T(8,128)(2,1)S(1)}, bf16[10,64,128]{2,1,0:T(8,128)(2,1)S(1)}, bf16[10,64,128]{2,1,0:T(8,128)(2,1)S(1)}, bf16[10,64,128]{2,1,0:T(8,128)(2,1)S(1)}) custom-call(s32[40]{0:T(128)} %head_slot.9, bf16[64,5120]{1,0:T(8,128)(2,1)} %refs_0_.8, bf16[64,5120]{1,0:T(8,128)(2,1)} %refs_1_.3), custom_call_target="tpu_custom_call" | custom-call | bytes 1310720 | tf_op jit(solution)/shard_map/pack/pallas_call | solution.py:78
  2.3 3.1 %collective-permute-start.11 = (bf16[10,64,128]{2,1,0:T(8,128)(2,1)S(1)}, bf16[10,64,128]{2,1,0:T(8,128)(2,1)S(1)}, u32[]{:S(2)}, u32[]{:S(2)}) collective-permute-start(bf16[10,64,128]{2,1,0:T(8,128)(2,1)S(1)} %get-tuple-element.37), channel_id=1, source_target_pairs={{0,1},{1,2},{2,3},{3,0},{4,5},{5,6},{6,7},{7,4},{8,9},{9,10},{10,1... | collective-permute-start | bytes 491528 | tf_op jit(solution)/shard_map/ppermute | solution.py:284
  5.4 2.6 %collective-permute-start.12 = (bf16[10,64,128]{2,1,0:T(8,128)(2,1)S(1)}, bf16[10,64,128]{2,1,0:T(8,128)(2,1)S(1)}, u32[]{:S(2)}, u32[]{:S(2)}) collective-permute-start(bf16[10,64,128]{2,1,0:T(8,128)(2,1)S(1)} %get-tuple-element.38), channel_id=1, source_target_pairs={{0,2},{1,3},{2,0},{3,1},{4,6},{5,7},{6,4},{7,5},{8,10},{9,11},{10,... | collective-permute-start | bytes 491528 | tf_op jit(solution)/shard_map/ppermute | solution.py:284
  7.9 1.3 %collective-permute-start.13 = (bf16[10,64,128]{2,1,0:T(8,128)(2,1)S(1)}, bf16[10,64,128]{2,1,0:T(8,128)(2,1)S(1)}, u32[]{:S(2)}, u32[]{:S(2)}) collective-permute-start(bf16[10,64,128]{2,1,0:T(8,128)(2,1)S(1)} %get-tuple-element.39), channel_id=1, source_target_pairs={{0,3},{1,0},{2,1},{3,2},{4,7},{5,4},{6,5},{7,6},{8,11},{9,8},{10,9... | collective-permute-start | bytes 491528 | tf_op jit(solution)/shard_map/ppermute | solution.py:284
  9.3 1.9 %pack.3 = (bf16[15,64,128]{2,1,0:T(8,128)(2,1)S(1)}, bf16[15,64,128]{2,1,0:T(8,128)(2,1)S(1)}, bf16[15,64,128]{2,1,0:T(8,128)(2,1)S(1)}, bf16[15,64,128]{2,1,0:T(8,128)(2,1)S(1)}) custom-call(s32[40]{0:T(128)} %head_slot.9, bf16[64,5120]{1,0:T(8,128)(2,1)} %refs_0_.8, bf16[64,5120]{1,0:T(8,128)(2,1)} %refs_1_.3, bf16[64,5120]{1,0:T(8,128)(2,1)} %refs_0_.6), custom_call_target="tpu_custom_call" | custom-call | bytes 1966080 | tf_op jit(solution)/shard_map/pack/pallas_call | solution.py:78
  11.2 0.7 collective-permute-start
  12.0 0.3 collective-permute-start.1
  12.3 0.2 collective-permute-done.11.refs_1_
  12.5 2.6 %collective-permute-start.2 = (bf16[15,64,128]{2,1,0:T(8,128)(2,1)S(1)}, bf16[15,64,128]{2,1,0:T(8,128)(2,1)S(1)}, u32[]{:S(2)}, u32[]{:S(2)}) collective-permute-start(bf16[15,64,128]{2,1,0:T(8,128)(2,1)S(1)} %get-tuple-element.27), channel_id=1, source_target_pairs={{0,3},{1,0},{2,1},{3,2},{4,7},{5,4},{6,5},{7,6},{8,11},{9,8},{10,9... | collective-permute-start | bytes 737288 | tf_op jit(solution)/shard_map/ppermute | solution.py:284
  15.1 4.4 %collective-permute-done.12.refs_2_ = bf16[10,64,128]{2,1,0:T(8,128)(2,1)S(1)} collective-permute-done((bf16[10,64,128]{2,1,0:T(8,128)(2,1)S(1)}, bf16[10,64,128]{2,1,0:T(8,128)(2,1)S(1)}, u32[]{:S(2)}, u32[]{:S(2)}) %collective-permute-start.12) | collective-permute-done | bytes 163872 | tf_op jit(solution)/shard_map/ppermute | solution.py:284
  19.6 4.0 %collective-permute-done.13.refs_3_ = bf16[10,64,128]{2,1,0:T(8,128)(2,1)S(1)} collective-permute-done((bf16[10,64,128]{2,1,0:T(8,128)(2,1)S(1)}, bf16[10,64,128]{2,1,0:T(8,128)(2,1)S(1)}, u32[]{:S(2)}, u32[]{:S(2)}) %collective-permute-start.13) | collective-permute-done | bytes 163872 | tf_op jit(solution)/shard_map/ppermute | solution.py:284
  23.5 0.2 join.3.refs_2_
  23.7 1.3 %collective-permute-start.15 = (bf16[10,256,128]{2,1,0:T(8,128)(2,1)S(1)}, bf16[10,256,128]{2,1,0:T(8,128)(2,1)S(1)}, u32[]{:S(2)}, u32[]{:S(2)}) collective-permute-start(bf16[10,256,128]{2,1,0:T(8,128)(2,1)S(1)} %join.3.refs_2_), channel_id=1, source_target_pairs={{4,0},{8,4},{12,8},{5,1},{9,5},{13,9},{6,2},{10,6},{14,10},{7,3},{... | collective-permute-start | bytes 1966088 | tf_op jit(solution)/shard_map/ppermute | solution.py:320
  25.0 3.1 %collective-permute-start.14 = (bf16[10,256,128]{2,1,0:T(8,128)(2,1)S(1)}, bf16[10,256,128]{2,1,0:T(8,128)(2,1)S(1)}, u32[]{:S(2)}, u32[]{:S(2)}) collective-permute-start(bf16[10,256,128]{2,1,0:T(8,128)(2,1)S(1)} %join.3.refs_2_), channel_id=1, source_target_pairs={{0,4},{4,8},{8,12},{1,5},{5,9},{9,13},{2,6},{6,10},{10,14},{3,7},{... | collective-permute-start | bytes 1966088 | tf_op jit(solution)/shard_map/ppermute | solution.py:319
  28.1 0.0 collective-permute-done.refs_1_.refs_6_
  28.1 9.9 %collective-permute-done.1.refs_2_.refs_7_ = bf16[15,64,128]{2,1,0:T(8,128)(2,1)S(1)} collective-permute-done((bf16[15,64,128]{2,1,0:T(8,128)(2,1)S(1)}, bf16[15,64,128]{2,1,0:T(8,128)(2,1)S(1)}, u32[]{:S(2)}, u32[]{:S(2)}) %collective-permute-start.1) | collective-permute-done | bytes 245792 | tf_op jit(solution)/shard_map/ppermute | solution.py:284
  38.0 0.0 collective-permute-done.2.refs_3_.refs_8_
  38.0 0.2 join.2.refs_2_
  38.2 1.3 %collective-permute-start.4 = (bf16[10,256,128]{2,1,0:T(8,128)(2,1)S(1)}, bf16[10,256,128]{2,1,0:T(8,128)(2,1)S(1)}, u32[]{:S(2)}, u32[]{:S(2)}) collective-permute-start(bf16[10,256,128]{2,1,0:T(8,128)(2,1)S(1)} %join.2.refs_2_), channel_id=1, source_target_pairs={{4,0},{8,4},{12,8},{5,1},{9,5},{13,9},{6,2},{10,6},{14,10},{7,3},{... | collective-permute-start | bytes 1966088 | tf_op jit(solution)/shard_map/ppermute | solution.py:320
  39.5 3.1 %collective-permute-start.3 = (bf16[10,256,128]{2,1,0:T(8,128)(2,1)S(1)}, bf16[10,256,128]{2,1,0:T(8,128)(2,1)S(1)}, u32[]{:S(2)}, u32[]{:S(2)}) collective-permute-start(bf16[10,256,128]{2,1,0:T(8,128)(2,1)S(1)} %join.2.refs_2_), channel_id=1, source_target_pairs={{0,4},{4,8},{8,12},{1,5},{5,9},{9,13},{2,6},{6,10},{10,14},{3,7},{... | collective-permute-start | bytes 1966088 | tf_op jit(solution)/shard_map/ppermute | solution.py:319
  42.6 1.3 %pack.4 = (bf16[5,64,128]{2,1,0:T(8,128)(2,1)S(1)}, bf16[5,64,128]{2,1,0:T(8,128)(2,1)S(1)}, bf16[5,64,128]{2,1,0:T(8,128)(2,1)S(1)}, bf16[5,64,128]{2,1,0:T(8,128)(2,1)S(1)}) custom-call(s32[40]{0:T(128)} %head_slot.9, bf16[64,5120]{1,0:T(8,128)(2,1)} %refs_0_.6), custom_call_target="tpu_custom_call" | custom-call | bytes 655360 | tf_op jit(solution)/shard_map/pack/pallas_call | solution.py:78
  43.9 0.0 copy-start.1
  43.9 5.8 %collective-permute-start.5 = (bf16[5,64,128]{2,1,0:T(8,128)(2,1)S(1)}, bf16[5,64,128]{2,1,0:T(8,128)(2,1)S(1)}, u32[]{:S(2)}, u32[]{:S(2)}) collective-permute-start(bf16[5,64,128]{2,1,0:T(8,128)(2,1)S(1)} %get-tuple-element.29), channel_id=1, source_target_pairs={{0,1},{1,2},{2,3},{3,0},{4,5},{5,6},{6,7},{7,4},{8,9},{9,10},{10,1... | collective-permute-start | bytes 245768 | tf_op jit(solution)/shard_map/ppermute | solution.py:284
  49.7 0.0 collective-permute-done.15.refs_4_
  49.7 1.6 %collective-permute-start.6 = (bf16[5,64,128]{2,1,0:T(8,128)(2,1)S(1)}, bf16[5,64,128]{2,1,0:T(8,128)(2,1)S(1)}, u32[]{:S(2)}, u32[]{:S(2)}) collective-permute-start(bf16[5,64,128]{2,1,0:T(8,128)(2,1)S(1)} %get-tuple-element.30), channel_id=1, source_target_pairs={{0,2},{1,3},{2,0},{3,1},{4,6},{5,7},{6,4},{7,5},{8,10},{9,11},{10,... | collective-permute-start | bytes 245768 | tf_op jit(solution)/shard_map/ppermute | solution.py:284
  51.3 0.0 collective-permute-done.14.refs_3_
  51.3 0.0 copy-start
  51.3 0.8 %collective-permute-start.7 = (bf16[5,64,128]{2,1,0:T(8,128)(2,1)S(1)}, bf16[5,64,128]{2,1,0:T(8,128)(2,1)S(1)}, u32[]{:S(2)}, u32[]{:S(2)}) collective-permute-start(bf16[5,64,128]{2,1,0:T(8,128)(2,1)S(1)} %get-tuple-element.31), channel_id=1, source_target_pairs={{0,3},{1,0},{2,1},{3,2},{4,7},{5,4},{6,5},{7,6},{8,11},{9,8},{10,9... | collective-permute-start | bytes 245768 | tf_op jit(solution)/shard_map/ppermute | solution.py:284
  52.1 0.0 copy-done.1
  52.1 0.0 copy-done
  52.1 4.6 %attend.3 = (bf16[5,64,128]{2,1,0:T(8,128)(2,1)S(1)}, bf16[5,64,128]{2,1,0:T(8,128)(2,1)S(1)}, bf16[5,64,128]{2,1,0:T(8,128)(2,1)S(1)}, bf16[5,64,128]{2,1,0:T(8,128)(2,1)S(1)}, f32[5,256]{1,0:T(8,128)S(1)}) custom-call(s32[40]{0:T(128)S(1)} %copy-done, s32[5,2,40]{2,1,0:T(2,128)S(1)} %bitcast.1, bf16[10,256,128]{2,1,0:T(8,128)(2,1)S(1)} %join.3.refs_2_, ...), custom_call_target="tpu_custom_call" | custom-call | flops 419430400 | bytes 2621440 | tf_op jit(solution)/shard_map/attend/pallas_call | solution.py:212
  56.7 0.0 collective-permute-done.5.refs_6_
  56.7 1.3 %collective-permute-start.16 = (bf16[5,64,128]{2,1,0:T(8,128)(2,1)S(1)}, bf16[5,64,128]{2,1,0:T(8,128)(2,1)S(1)}, u32[]{:S(2)}, u32[]{:S(2)}) collective-permute-start(bf16[5,64,128]{2,1,0:T(8,128)(2,1)S(1)} %get-tuple-element.41), channel_id=1, source_target_pairs={{0,1},{1,2},{2,3},{3,0},{4,5},{5,6},{6,7},{7,4},{8,9},{9,10},{10,1... | collective-permute-start | bytes 245768 | tf_op jit(solution)/shard_map/ppermute | solution.py:284
  58.0 0.0 collective-permute-done.6.refs_7_
  58.0 1.3 %collective-permute-start.17 = (bf16[5,64,128]{2,1,0:T(8,128)(2,1)S(1)}, bf16[5,64,128]{2,1,0:T(8,128)(2,1)S(1)}, u32[]{:S(2)}, u32[]{:S(2)}) collective-permute-start(bf16[5,64,128]{2,1,0:T(8,128)(2,1)S(1)} %get-tuple-element.42), channel_id=1, source_target_pairs={{0,2},{1,3},{2,0},{3,1},{4,6},{5,7},{6,4},{7,5},{8,10},{9,11},{10,... | collective-permute-start | bytes 245768 | tf_op jit(solution)/shard_map/ppermute | solution.py:284
  59.3 0.0 collective-permute-done.7.refs_8_
  59.3 1.5 %collective-permute-start.18 = (bf16[5,64,128]{2,1,0:T(8,128)(2,1)S(1)}, bf16[5,64,128]{2,1,0:T(8,128)(2,1)S(1)}, u32[]{:S(2)}, u32[]{:S(2)}) collective-permute-start(bf16[5,64,128]{2,1,0:T(8,128)(2,1)S(1)} %get-tuple-element.43), channel_id=1, source_target_pairs={{0,3},{1,0},{2,1},{3,2},{4,7},{5,4},{6,5},{7,6},{8,11},{9,8},{10,9... | collective-permute-start | bytes 245768 | tf_op jit(solution)/shard_map/ppermute | solution.py:284
  60.9 0.0 collective-permute-done.4.refs_4_
  60.9 0.0 collective-permute-done.3.refs_3_
  60.9 4.6 %attend.2 = (bf16[5,64,128]{2,1,0:T(8,128)(2,1)S(1)}, bf16[5,64,128]{2,1,0:T(8,128)(2,1)S(1)}, bf16[5,64,128]{2,1,0:T(8,128)(2,1)S(1)}, bf16[5,64,128]{2,1,0:T(8,128)(2,1)S(1)}, f32[5,256]{1,0:T(8,128)S(1)}) custom-call(s32[40]{0:T(128)S(1)} %copy-done, s32[5,2,40]{2,1,0:T(2,128)S(1)} %bitcast.2, bf16[10,256,128]{2,1,0:T(8,128)(2,1)S(1)} %join.2.refs_2_, ...), custom_call_target="tpu_custom_call" | custom-call | flops 419430400 | bytes 2621440 | tf_op jit(solution)/shard_map/attend/pallas_call | solution.py:212
  65.4 0.6 collective-permute-start.8
  66.0 1.6 %collective-permute-start.9 = (bf16[5,64,128]{2,1,0:T(8,128)(2,1)S(1)}, bf16[5,64,128]{2,1,0:T(8,128)(2,1)S(1)}, u32[]{:S(2)}, u32[]{:S(2)}) collective-permute-start(bf16[5,64,128]{2,1,0:T(8,128)(2,1)S(1)} %get-tuple-element.34), channel_id=1, source_target_pairs={{0,2},{1,3},{2,0},{3,1},{4,6},{5,7},{6,4},{7,5},{8,10},{9,11},{10,... | collective-permute-start | bytes 245768 | tf_op jit(solution)/shard_map/ppermute | solution.py:284
  67.6 0.0 collective-permute-done.16.refs_1_
  67.6 2.6 %collective-permute-start.10 = (bf16[5,64,128]{2,1,0:T(8,128)(2,1)S(1)}, bf16[5,64,128]{2,1,0:T(8,128)(2,1)S(1)}, u32[]{:S(2)}, u32[]{:S(2)}) collective-permute-start(bf16[5,64,128]{2,1,0:T(8,128)(2,1)S(1)} %get-tuple-element.35), channel_id=1, source_target_pairs={{0,3},{1,0},{2,1},{3,2},{4,7},{5,4},{6,5},{7,6},{8,11},{9,8},{10,9... | collective-permute-start | bytes 245768 | tf_op jit(solution)/shard_map/ppermute | solution.py:284
  70.2 0.0 collective-permute-done.17.refs_2_
  70.2 0.0 collective-permute-done.18.refs_3_
  70.3 1.5 %unpack.2.refs_4_ = bf16[64,5120]{1,0:T(8,128)(2,1)} custom-call(s32[40]{0:T(128)S(1)} %copy-done, bf16[5,64,128]{2,1,0:T(8,128)(2,1)S(1)} %get-tuple-element.40.refs_0_, bf16[5,64,128]{2,1,0:T(8,128)(2,1)S(1)} %collective-permute-done.16.refs_1_, bf16[5,64,128]{2,1,0:T(8,128)(2,1)S(1)} %collective-permute-done.17.refs_2_, ...), custom_call_target="tpu_custom_call" | custom-call | bytes 655360 | tf_op jit(solution)/shard_map/unpack/pallas_call | solution.py:263
  71.8 0.6 pad_maximum_fusion
  72.4 0.2 collective-permute-done.8.refs_1_
  72.6 2.6 %collective-permute-done.9.refs_2_ = bf16[5,64,128]{2,1,0:T(8,128)(2,1)S(1)} collective-permute-done((bf16[5,64,128]{2,1,0:T(8,128)(2,1)S(1)}, bf16[5,64,128]{2,1,0:T(8,128)(2,1)S(1)}, u32[]{:S(2)}, u32[]{:S(2)}) %collective-permute-start.9) | collective-permute-done | bytes 81952 | tf_op jit(solution)/shard_map/ppermute | solution.py:284
  75.2 0.0 collective-permute-done.10.refs_3_
  75.2 1.5 %unpack.3 = bf16[64,5120]{1,0:T(8,128)(2,1)} custom-call(s32[40]{0:T(128)S(1)} %copy-done, bf16[5,64,128]{2,1,0:T(8,128)(2,1)S(1)} %get-tuple-element.32.refs_0_, bf16[5,64,128]{2,1,0:T(8,128)(2,1)S(1)} %collective-permute-done.8.refs_1_, bf16[5,64,128]{2,1,0:T(8,128)(2,1)S(1)} %collective-permute-done.9.refs_2_, ...), custom_call_target="tpu_custom_call", output_to_operand_aliasing={{}: (5, {})} | custom-call | bytes 655360 | tf_op jit(solution)/shard_map/unpack/pallas_call | solution.py:263
Async XLA Ops:
  2.3 10.2 %collective-permute-start.11 = (bf16[10,64,128]{2,1,0:T(8,128)(2,1)S(1)}, bf16[10,64,128]{2,1,0:T(8,128)(2,1)S(1)}, u32[]{:S(2)}, u32[]{:S(2)}) collective-permute-start(bf16[10,64,128]{2,1,0:T(8,128)(2,1)S(1)} %get-tuple-element.37), channel_id=1, source_target_pairs={{0,1},{1,2},{2,3},{3,0},{4,5},{5,6},{6,7},{7,4},{8,9},{9,10},{10,1... | collective-permute-start | bytes 491528 | tf_op jit(solution)/shard_map/ppermute | solution.py:284
  5.4 14.2 %collective-permute-start.12 = (bf16[10,64,128]{2,1,0:T(8,128)(2,1)S(1)}, bf16[10,64,128]{2,1,0:T(8,128)(2,1)S(1)}, u32[]{:S(2)}, u32[]{:S(2)}) collective-permute-start(bf16[10,64,128]{2,1,0:T(8,128)(2,1)S(1)} %get-tuple-element.38), channel_id=1, source_target_pairs={{0,2},{1,3},{2,0},{3,1},{4,6},{5,7},{6,4},{7,5},{8,10},{9,11},{10,... | collective-permute-start | bytes 491528 | tf_op jit(solution)/shard_map/ppermute | solution.py:284
  7.9 15.6 %collective-permute-start.13 = (bf16[10,64,128]{2,1,0:T(8,128)(2,1)S(1)}, bf16[10,64,128]{2,1,0:T(8,128)(2,1)S(1)}, u32[]{:S(2)}, u32[]{:S(2)}) collective-permute-start(bf16[10,64,128]{2,1,0:T(8,128)(2,1)S(1)} %get-tuple-element.39), channel_id=1, source_target_pairs={{0,3},{1,0},{2,1},{3,2},{4,7},{5,4},{6,5},{7,6},{8,11},{9,8},{10,9... | collective-permute-start | bytes 491528 | tf_op jit(solution)/shard_map/ppermute | solution.py:284
  11.2 16.8 %collective-permute-start = (bf16[15,64,128]{2,1,0:T(8,128)(2,1)S(1)}, bf16[15,64,128]{2,1,0:T(8,128)(2,1)S(1)}, u32[]{:S(2)}, u32[]{:S(2)}) collective-permute-start(bf16[15,64,128]{2,1,0:T(8,128)(2,1)S(1)} %get-tuple-element.25), channel_id=1, source_target_pairs={{0,1},{1,2},{2,3},{3,0},{4,5},{5,6},{6,7},{7,4},{8,9},{9,10},{10,1... | collective-permute-start | bytes 737288 | tf_op jit(solution)/shard_map/ppermute | solution.py:284
  12.0 26.1 %collective-permute-start.1 = (bf16[15,64,128]{2,1,0:T(8,128)(2,1)S(1)}, bf16[15,64,128]{2,1,0:T(8,128)(2,1)S(1)}, u32[]{:S(2)}, u32[]{:S(2)}) collective-permute-start(bf16[15,64,128]{2,1,0:T(8,128)(2,1)S(1)} %get-tuple-element.26), channel_id=1, source_target_pairs={{0,2},{1,3},{2,0},{3,1},{4,6},{5,7},{6,4},{7,5},{8,10},{9,11},{10,... | collective-permute-start | bytes 737288 | tf_op jit(solution)/shard_map/ppermute | solution.py:284
  12.5 25.5 %collective-permute-start.2 = (bf16[15,64,128]{2,1,0:T(8,128)(2,1)S(1)}, bf16[15,64,128]{2,1,0:T(8,128)(2,1)S(1)}, u32[]{:S(2)}, u32[]{:S(2)}) collective-permute-start(bf16[15,64,128]{2,1,0:T(8,128)(2,1)S(1)} %get-tuple-element.27), channel_id=1, source_target_pairs={{0,3},{1,0},{2,1},{3,2},{4,7},{5,4},{6,5},{7,6},{8,11},{9,8},{10,9... | collective-permute-start | bytes 737288 | tf_op jit(solution)/shard_map/ppermute | solution.py:284
  23.7 26.0 %collective-permute-start.15 = (bf16[10,256,128]{2,1,0:T(8,128)(2,1)S(1)}, bf16[10,256,128]{2,1,0:T(8,128)(2,1)S(1)}, u32[]{:S(2)}, u32[]{:S(2)}) collective-permute-start(bf16[10,256,128]{2,1,0:T(8,128)(2,1)S(1)} %join.3.refs_2_), channel_id=1, source_target_pairs={{4,0},{8,4},{12,8},{5,1},{9,5},{13,9},{6,2},{10,6},{14,10},{7,3},{... | collective-permute-start | bytes 1966088 | tf_op jit(solution)/shard_map/ppermute | solution.py:320
  25.0 26.3 %collective-permute-start.14 = (bf16[10,256,128]{2,1,0:T(8,128)(2,1)S(1)}, bf16[10,256,128]{2,1,0:T(8,128)(2,1)S(1)}, u32[]{:S(2)}, u32[]{:S(2)}) collective-permute-start(bf16[10,256,128]{2,1,0:T(8,128)(2,1)S(1)} %join.3.refs_2_), channel_id=1, source_target_pairs={{0,4},{4,8},{8,12},{1,5},{5,9},{9,13},{2,6},{6,10},{10,14},{3,7},{... | collective-permute-start | bytes 1966088 | tf_op jit(solution)/shard_map/ppermute | solution.py:319
  38.2 22.7 %collective-permute-start.4 = (bf16[10,256,128]{2,1,0:T(8,128)(2,1)S(1)}, bf16[10,256,128]{2,1,0:T(8,128)(2,1)S(1)}, u32[]{:S(2)}, u32[]{:S(2)}) collective-permute-start(bf16[10,256,128]{2,1,0:T(8,128)(2,1)S(1)} %join.2.refs_2_), channel_id=1, source_target_pairs={{4,0},{8,4},{12,8},{5,1},{9,5},{13,9},{6,2},{10,6},{14,10},{7,3},{... | collective-permute-start | bytes 1966088 | tf_op jit(solution)/shard_map/ppermute | solution.py:320
  39.5 21.4 %collective-permute-start.3 = (bf16[10,256,128]{2,1,0:T(8,128)(2,1)S(1)}, bf16[10,256,128]{2,1,0:T(8,128)(2,1)S(1)}, u32[]{:S(2)}, u32[]{:S(2)}) collective-permute-start(bf16[10,256,128]{2,1,0:T(8,128)(2,1)S(1)} %join.2.refs_2_), channel_id=1, source_target_pairs={{0,4},{4,8},{8,12},{1,5},{5,9},{9,13},{2,6},{6,10},{10,14},{3,7},{... | collective-permute-start | bytes 1966088 | tf_op jit(solution)/shard_map/ppermute | solution.py:319
  43.9 8.3 %copy-start.1 = (s32[40,2,5]{0,1,2:T(2,128)S(1)}, s32[40,2,5]{0,1,2:T(2,128)}, u32[]{:S(2)}) copy-start(s32[40,2,5]{0,1,2:T(2,128)} %param.8) | copy-start | bytes 4804
  43.9 12.8 %collective-permute-start.5 = (bf16[5,64,128]{2,1,0:T(8,128)(2,1)S(1)}, bf16[5,64,128]{2,1,0:T(8,128)(2,1)S(1)}, u32[]{:S(2)}, u32[]{:S(2)}) collective-permute-start(bf16[5,64,128]{2,1,0:T(8,128)(2,1)S(1)} %get-tuple-element.29), channel_id=1, source_target_pairs={{0,1},{1,2},{2,3},{3,0},{4,5},{5,6},{6,7},{7,4},{8,9},{9,10},{10,1... | collective-permute-start | bytes 245768 | tf_op jit(solution)/shard_map/ppermute | solution.py:284
  49.7 8.3 %collective-permute-start.6 = (bf16[5,64,128]{2,1,0:T(8,128)(2,1)S(1)}, bf16[5,64,128]{2,1,0:T(8,128)(2,1)S(1)}, u32[]{:S(2)}, u32[]{:S(2)}) collective-permute-start(bf16[5,64,128]{2,1,0:T(8,128)(2,1)S(1)} %get-tuple-element.30), channel_id=1, source_target_pairs={{0,2},{1,3},{2,0},{3,1},{4,6},{5,7},{6,4},{7,5},{8,10},{9,11},{10,... | collective-permute-start | bytes 245768 | tf_op jit(solution)/shard_map/ppermute | solution.py:284
  51.3 0.8 %copy-start = (s32[40]{0:T(128)S(1)}, s32[40]{0:T(128)}, u32[]{:S(2)}) copy-start(s32[40]{0:T(128)} %head_slot.9) | copy-start | bytes 484
  51.3 8.0 %collective-permute-start.7 = (bf16[5,64,128]{2,1,0:T(8,128)(2,1)S(1)}, bf16[5,64,128]{2,1,0:T(8,128)(2,1)S(1)}, u32[]{:S(2)}, u32[]{:S(2)}) collective-permute-start(bf16[5,64,128]{2,1,0:T(8,128)(2,1)S(1)} %get-tuple-element.31), channel_id=1, source_target_pairs={{0,3},{1,0},{2,1},{3,2},{4,7},{5,4},{6,5},{7,6},{8,11},{9,8},{10,9... | collective-permute-start | bytes 245768 | tf_op jit(solution)/shard_map/ppermute | solution.py:284
  56.7 10.9 %collective-permute-start.16 = (bf16[5,64,128]{2,1,0:T(8,128)(2,1)S(1)}, bf16[5,64,128]{2,1,0:T(8,128)(2,1)S(1)}, u32[]{:S(2)}, u32[]{:S(2)}) collective-permute-start(bf16[5,64,128]{2,1,0:T(8,128)(2,1)S(1)} %get-tuple-element.41), channel_id=1, source_target_pairs={{0,1},{1,2},{2,3},{3,0},{4,5},{5,6},{6,7},{7,4},{8,9},{9,10},{10,1... | collective-permute-start | bytes 245768 | tf_op jit(solution)/shard_map/ppermute | solution.py:284
  58.0 12.2 %collective-permute-start.17 = (bf16[5,64,128]{2,1,0:T(8,128)(2,1)S(1)}, bf16[5,64,128]{2,1,0:T(8,128)(2,1)S(1)}, u32[]{:S(2)}, u32[]{:S(2)}) collective-permute-start(bf16[5,64,128]{2,1,0:T(8,128)(2,1)S(1)} %get-tuple-element.42), channel_id=1, source_target_pairs={{0,2},{1,3},{2,0},{3,1},{4,6},{5,7},{6,4},{7,5},{8,10},{9,11},{10,... | collective-permute-start | bytes 245768 | tf_op jit(solution)/shard_map/ppermute | solution.py:284
  59.3 10.9 %collective-permute-start.18 = (bf16[5,64,128]{2,1,0:T(8,128)(2,1)S(1)}, bf16[5,64,128]{2,1,0:T(8,128)(2,1)S(1)}, u32[]{:S(2)}, u32[]{:S(2)}) collective-permute-start(bf16[5,64,128]{2,1,0:T(8,128)(2,1)S(1)} %get-tuple-element.43), channel_id=1, source_target_pairs={{0,3},{1,0},{2,1},{3,2},{4,7},{5,4},{6,5},{7,6},{8,11},{9,8},{10,9... | collective-permute-start | bytes 245768 | tf_op jit(solution)/shard_map/ppermute | solution.py:284
  65.4 7.2 %collective-permute-start.8 = (bf16[5,64,128]{2,1,0:T(8,128)(2,1)S(1)}, bf16[5,64,128]{2,1,0:T(8,128)(2,1)S(1)}, u32[]{:S(2)}, u32[]{:S(2)}) collective-permute-start(bf16[5,64,128]{2,1,0:T(8,128)(2,1)S(1)} %get-tuple-element.33), channel_id=1, source_target_pairs={{0,1},{1,2},{2,3},{3,0},{4,5},{5,6},{6,7},{7,4},{8,9},{9,10},{10,1... | collective-permute-start | bytes 245768 | tf_op jit(solution)/shard_map/ppermute | solution.py:284
  66.0 9.2 %collective-permute-start.9 = (bf16[5,64,128]{2,1,0:T(8,128)(2,1)S(1)}, bf16[5,64,128]{2,1,0:T(8,128)(2,1)S(1)}, u32[]{:S(2)}, u32[]{:S(2)}) collective-permute-start(bf16[5,64,128]{2,1,0:T(8,128)(2,1)S(1)} %get-tuple-element.34), channel_id=1, source_target_pairs={{0,2},{1,3},{2,0},{3,1},{4,6},{5,7},{6,4},{7,5},{8,10},{9,11},{10,... | collective-permute-start | bytes 245768 | tf_op jit(solution)/shard_map/ppermute | solution.py:284
  67.6 7.6 %collective-permute-start.10 = (bf16[5,64,128]{2,1,0:T(8,128)(2,1)S(1)}, bf16[5,64,128]{2,1,0:T(8,128)(2,1)S(1)}, u32[]{:S(2)}, u32[]{:S(2)}) collective-permute-start(bf16[5,64,128]{2,1,0:T(8,128)(2,1)S(1)} %get-tuple-element.35), channel_id=1, source_target_pairs={{0,3},{1,0},{2,1},{3,2},{4,7},{5,4},{6,5},{7,6},{8,11},{9,8},{10,9... | collective-permute-start | bytes 245768 | tf_op jit(solution)/shard_map/ppermute | solution.py:284

commit v3 on v2

v3 whole, which is shorter than its diff:
```python
import functools
import math

import jax
import jax.numpy as jnp
from jax import lax
from jax.experimental import pallas as pl
from jax.experimental.pallas import tpu as pltpu
from jax.sharding import PartitionSpec as P

HBM = pl.BlockSpec(memory_space=pltpu.HBM)
ANY = pl.BlockSpec(memory_space=pl.ANY)
SMEM = pl.BlockSpec(memory_space=pltpu.SMEM)
VMEM = pl.BlockSpec(memory_space=pltpu.VMEM)
SMALL = pltpu.CompilerParams(vmem_limit_bytes=4 * 1024 * 1024)
LARGE = pltpu.CompilerParams(vmem_limit_bytes=24 * 1024 * 1024)


SPLIT = 5
STAGES = ((('k', 0), ('v', 0)), (('k', 1), ('v', 1), ('q', 0)), (('q', 1),))
PACK_US = (0.0, 0.0, 0.0, 0.0)
JOIN_US = (0.0, 0.0)
QJOIN_US = (0.0, 0.0)
WAIT_LAST = False
ATTEND_US = (0.0, 0.0)
UNPACK_US = (0.0, 0.0)
CHAIN = True
HOLD = 0
ORDER = (2, 1, 3)


def hint(us):
    return pl.CostEstimate(flops=int(us * 1e9), bytes_accessed=int(us * 3e6), transcendentals=int(us * 1e6))


def in_hbm(x):
    return pltpu.with_memory_space_constraint(x, pltpu.HBM)


def invert(head_slot, head_of, used=None):
    for j in range(head_of.shape[0]):
        head_of[j] = 0
        if used is not None:
            used[j] = 0
    for h in range(head_slot.shape[0]):
        head_of[head_slot[h]] = h
        if used is not None:
            used[head_slot[h]] = 1


def pack_kernel(owners, capacity, dim, parts, sources, waited, head_slot, *refs):
    rows = refs[:sources]
    count_out = len(parts) * owners
    outs = refs[sources + waited : sources + waited + count_out]
    held = refs[sources + waited + count_out : 2 * sources + waited + count_out]
    slots, head_of, sem, sem_slots = refs[2 * sources + waited + count_out :]
    me = lax.axis_index("head")
    slot_copy = pltpu.make_async_copy(head_slot, slots, sem_slots)
    slot_copy.start()
    chunks = sem.shape[1]
    size = rows[0].shape[0] // chunks
    copies = []
    for i in range(sources):
        for j in range(chunks):
            place = pl.ds(j * size, size)
            copies.append(
                pltpu.make_async_copy(rows[i].at[place], held[i].at[place], sem.at[i, j])
            )
            copies[-1].start()
    slot_copy.wait()
    invert(slots, head_of)
    for copy in copies:
        copy.wait()
    for stage, part in enumerate(parts):
        for k in range(owners):
            owner = lax.rem(me + k, owners)
            place = 0
            for source, first, count in part:
                for c in range(count):
                    head = head_of[owner * capacity + first + c]
                    columns = pl.ds(pl.multiple_of(head * dim, dim), dim)
                    outs[stage * owners + k][place] = held[source][:, columns]
                    place += 1


def pack(head_slot, sources, stages, owners, capacity, dim, us, waits=()):
    names = sorted({name for held in stages for name, _, _ in held})
    rows = [sources[name] for name in names]
    tokens, dtype = rows[0].shape[0], rows[0].dtype
    shapes = []
    for held in stages:
        total = sum(count for _, _, count in held)
        shapes += [jax.ShapeDtypeStruct((total, tokens, dim), dtype)] * owners
    places = tuple(tuple((names.index(n), f, c) for n, f, c in held) for held in stages)
    chunks = max(tokens // 16, 1)
    packed = pl.pallas_call(
        functools.partial(pack_kernel, owners, capacity, dim, places, len(rows), len(waits)),
        out_shape=shapes,
        in_specs=[ANY] * (1 + len(rows) + len(waits)),
        out_specs=[VMEM] * len(shapes),
        scratch_shapes=[pltpu.VMEM(row.shape, row.dtype) for row in rows]
        + [
            pltpu.SMEM(head_slot.shape, jnp.int32),
            pltpu.SMEM((owners * capacity,), jnp.int32),
            pltpu.SemaphoreType.DMA((len(rows), chunks)),
            pltpu.SemaphoreType.DMA,
        ],
        cost_estimate=hint(us),
        compiler_params=SMALL,
        name="pack",
    )(*[in_hbm(x) for x in (head_slot, *rows)], *waits)
    return [packed[i * owners : (i + 1) * owners] for i in range(len(stages))]


def join_kernel(owners, skip, count, *refs):
    blocks, out, sem = refs[:owners], refs[owners], refs[owners + 1]
    me = lax.axis_index("head")
    tokens = blocks[0].shape[1]
    copies = []
    for k in range(owners):
        start = lax.rem(me - k + owners, owners) * tokens
        place = pl.ds(pl.multiple_of(start, tokens), tokens)
        copies.append(
            pltpu.make_async_copy(blocks[k].at[pl.ds(skip, count)], out.at[:, place], sem.at[k])
        )
        copies[-1].start()
    for copy in copies:
        copy.wait()


def join(blocks, skip, count, us):
    owners = len(blocks)
    _, t, d = blocks[0].shape
    shape = jax.ShapeDtypeStruct((count, t * owners, d), blocks[0].dtype)
    return pl.pallas_call(
        functools.partial(join_kernel, owners, skip, count),
        out_shape=shape,
        in_specs=[ANY] * owners,
        out_specs=ANY,
        scratch_shapes=[pltpu.SemaphoreType.DMA((owners,))],
        cost_estimate=hint(us),
        compiler_params=SMALL,
        name="join",
    )(*blocks)


def attend_kernel(owners, capacity, first, count, tiles, tiles_all, band, *refs):
    head_slot, mask, mid, even, odd, q_all = refs[:6]
    outs = refs[6 : 6 + owners]
    lse_ref, kv_all, o_all, logits, weights, totals = refs[6 + owners : 12 + owners]
    mask_all, slots, head_of, used, sem_kv, sem_m = refs[12 + owners :]
    me = lax.axis_index("head")
    tile_base = lax.axis_index("slab") * tiles
    _, tok_slab, dim = q_all.shape
    tok = tok_slab // owners
    reach = (band - 1) // 2
    rows = tok_slab // tiles
    halo, own = reach * rows, tiles * rows
    scale = dim ** (-0.5)
    base2 = scale * math.log2(math.e)
    spans = logits.shape[1]
    span = tiles // spans

    small = [
        pltpu.make_async_copy(mask, mask_all, sem_m.at[0]),
        pltpu.make_async_copy(head_slot, slots, sem_m.at[1]),
    ]
    lower = lax.rem(lax.axis_index("slab"), 2) == 0
    places = (
        (mid, halo, own),
        (even, pl.multiple_of(jnp.where(lower, halo + own, 0), rows), halo),
        (odd, pl.multiple_of(jnp.where(lower, 0, halo + own), rows), halo),
    )
    large = [
        pltpu.make_async_copy(source, kv_all.at[:, pl.ds(start, size)], sem_kv.at[i])
        for i, (source, start, size) in enumerate(places)
    ]
    for copy in large + small:
        copy.start()
    for copy in large:
        copy.wait()

    for c in range(count):
        for u in range(spans):
            low = u * span * rows
            logits[c, u] = lax.dot_general(
                kv_all[c, low : low + (span - 1 + band) * rows, :],
                q_all[c, low : low + span * rows, :],
                (((1,), (1,)), ((), ())),
                preferred_element_type=jnp.float32,
            )

    for copy in small:
        copy.wait()
    invert(slots, head_of, used)

    for c in range(count):
        slot = me * capacity + first + c
        head = head_of[slot]
        valid = used[slot] > 0
        for t in range(tiles):
            u, w = t // span, t % span
            columns = slice(w * rows, (w + 1) * rows)
            allowed, highest = [], None
            for b in range(band):
                tile = tile_base + t + b - reach
                flag = mask_all[b, t, head]
                allowed.append((flag > 0) & (tile >= 0) & (tile < tiles_all))
                part = logits[c, u, (w + b) * rows : (w + b + 1) * rows, columns]
                part = jnp.max(part.reshape(rows // 8, 8, rows), axis=0)
                part = jnp.where(allowed[b], part, -1e30)
                highest = part if highest is None else jnp.maximum(highest, part)
            highest = jnp.max(highest, axis=0, keepdims=True)
            total = None
            for b in range(band):
                shift = jnp.where(allowed[b], highest * base2, 1e30)
                part = logits[c, u, (w + b) * rows : (w + b + 1) * rows, columns]
                part = jnp.exp2(part * base2 - shift)
                weights[c * tiles + t, b * rows : (b + 1) * rows, :] = part.astype(jnp.bfloat16)
                part = jnp.sum(part.reshape(rows // 8, 8, rows), axis=0)
                total = part if total is None else total + part
            total = jnp.sum(total, axis=0, keepdims=True)
            place = slice(t * rows, (t + 1) * rows)
            totals[c : c + 1, place] = total
            lse = highest * scale + jnp.log(total)
            lse_ref[c : c + 1, place] = jnp.where(valid, lse, 0.0)

    for c in range(count):
        for t in range(tiles):
            place = slice(t * rows, (t + 1) * rows)
            summed = lax.dot_general(
                kv_all[count + c, t * rows : (t + band) * rows, :],
                weights[c * tiles + t],
                (((0,), (0,)), ((), ())),
                preferred_element_type=jnp.float32,
            )
            o_all[c, place, :] = jnp.transpose(summed / totals[c : c + 1, place]).astype(
                jnp.bfloat16
            )

    for k in range(owners):
        place = pl.ds(pl.multiple_of(lax.rem(me + k, owners) * tok, tok), tok)
        outs[k][...] = o_all[:, place, :]


def attend(head_slot, mask, near, queries, us, owners, *sizes):
    capacity, first, count, tiles, tiles_all, band = sizes
    _, tok_slab, dim = queries.shape
    rows = tok_slab // tiles
    span = 2 if tiles % 2 == 0 else 1
    out = jax.ShapeDtypeStruct((count, tok_slab // owners, dim), jnp.bfloat16)
    extended = tok_slab + (band - 1) * rows
    slots = owners * capacity
    return pl.pallas_call(
        functools.partial(attend_kernel, owners, capacity, first, count, tiles, tiles_all, band),
        out_shape=[out] * owners + [jax.ShapeDtypeStruct((count, tok_slab), jnp.float32)],
        in_specs=[ANY] * 5 + [VMEM],
        out_specs=[VMEM] * (owners + 1),
        scratch_shapes=[
            pltpu.VMEM((2 * count, extended, dim), jnp.bfloat16),
            pltpu.VMEM((count, tok_slab, dim), jnp.bfloat16),
            pltpu.VMEM((count, tiles // span, (span - 1 + band) * rows, span * rows), jnp.float32),
            pltpu.VMEM((count * tiles, band * rows, rows), jnp.bfloat16),
            pltpu.VMEM((count, tok_slab), jnp.float32),
            pltpu.SMEM(mask.shape, jnp.int32),
            pltpu.SMEM(head_slot.shape, jnp.int32),
            pltpu.SMEM((slots,), jnp.int32),
            pltpu.SMEM((slots,), jnp.int32),
            pltpu.SemaphoreType.DMA((3,)),
            pltpu.SemaphoreType.DMA((2,)),
        ],
        cost_estimate=hint(us),
        compiler_params=LARGE,
        name="attend",
    )(in_hbm(head_slot), in_hbm(mask), *near, queries)


def unpack_kernel(owners, capacity, first, count, dim, head_slot, *refs):
    blocks = refs[:owners]
    out, slots, head_of, used, sem, sem_slots = refs[-6:]
    me = lax.axis_index("head")
    slot_copy = pltpu.make_async_copy(head_slot, slots, sem_slots)
    slot_copy.start()
    slot_copy.wait()
    invert(slots, head_of, used)

    def each(act):
        for k in range(owners):
            owner = lax.rem(me - k + owners, owners)
            for c in range(count):
                slot = owner * capacity + first + c
                columns = pl.ds(pl.multiple_of(head_of[slot] * dim, dim), dim)
                copy = pltpu.make_async_copy(
                    blocks[k].at[c], out.at[:, columns], sem.at[k * count + c]
                )
                if owners * capacity == head_slot.shape[0]:
                    act(copy)
                else:
                    pl.when(used[slot] > 0)(functools.partial(act, copy))

    each(lambda copy: copy.start())
    each(lambda copy: copy.wait())


def unpack(head_slot, blocks, target, capacity, first, shape, us):
    owners = len(blocks)
    count, tok, dim = blocks[0].shape
    operands = list(blocks) + ([] if target is None else [target])
    return pl.pallas_call(
        functools.partial(unpack_kernel, owners, capacity, first, count, dim),
        out_shape=shape,
        in_specs=[ANY] * (owners + 1) + ([] if target is None else [HBM]),
        out_specs=HBM,
        input_output_aliases={} if target is None else {owners + 1: 0},
        scratch_shapes=[
            pltpu.SMEM(head_slot.shape, jnp.int32),
            pltpu.SMEM((owners * capacity,), jnp.int32),
            pltpu.SMEM((owners * capacity,), jnp.int32),
            pltpu.SemaphoreType.DMA((owners * count,)),
            pltpu.SemaphoreType.DMA,
        ],
        cost_estimate=hint(us),
        compiler_params=SMALL,
        name="unpack",
    )(in_hbm(head_slot), *operands)


def exchange(blocks):
    owners = len(blocks)
    order = ORDER if len(ORDER) == owners - 1 else range(1, owners)
    moved = {
        k: lax.ppermute(blocks[k], "head", [(i, (i + k) % owners) for i in range(owners)])
        for k in order
    }
    return [blocks[0]] + [moved[k] for k in range(1, owners)]


def swap(mid, parity, halo):
    slabs, length = lax.axis_size("slab"), mid.shape[1]
    pairs = [(i, i + 1) for i in range(parity, slabs - 1, 2)]
    if halo < length:
        lower = lax.rem(lax.axis_index("slab"), 2) == parity
        start = jnp.where(lower, length - halo, 0)
        mid = lax.dynamic_slice_in_dim(mid, start, halo, 1)
    return lax.ppermute(mid, "slab", pairs + [(j, i) for i, j in pairs])


def after(x, done):
    return pl.pallas_call(
        lambda *refs: None,
        out_shape=jax.ShapeDtypeStruct(x.shape, x.dtype),
        in_specs=[ANY, ANY],
        out_specs=ANY,
        input_output_aliases={0: 0},
        cost_estimate=hint(0.0),
        compiler_params=SMALL,
        name="after",
    )(x, done)


def on_device(query_rows, key_rows, value_rows, tile_mask, head_slot):
    owners = lax.axis_size("head")
    slabs = lax.axis_size("slab")
    tok_dev, width = query_rows.shape
    heads, tiles, band = tile_mask.shape
    dim = width // heads
    capacity = (heads + owners - 1) // owners
    tok_slab = tok_dev * owners
    halo = (band - 1) // 2 * (tok_slab // tiles)
    mask = jnp.transpose(tile_mask, (2, 1, 0))
    half = (SPLIT * capacity + 9) // 10
    groups = ((0, half), (half, capacity - half))
    source = {"q": query_rows, "k": key_rows, "v": value_rows}

    sizes = [[(name, *groups[g]) for name, g in held] for held in STAGES]
    args = (owners, capacity, dim)
    packed = pack(head_slot, source, sizes[:1], *args, PACK_US[0])
    if len(sizes) > 1:
        packed += pack(head_slot, source, sizes[1:], *args, PACK_US[1], packed[0][:1] if CHAIN else ())
    moved = [exchange(blocks) for blocks in packed]
    near, queries = {}, {}
    for blocks, held in zip(moved, STAGES):
        skip = 0
        for name, g in held:
            count = groups[g][1]
            if name == "q":
                queries[g] = join(blocks, skip, count, QJOIN_US[g])
            if name == "k":
                mid = join(blocks, skip, 2 * count, JOIN_US[g])
                if g == 1 and HOLD:
                    mid = after(mid, moved[-1][HOLD])
                even = swap(mid, 0, halo)
                mid = after(mid, even)
                near[g] = (mid, even, swap(mid, 1, halo))
            skip += count

    target, lses = None, []
    for g, (first, count) in enumerate(groups):
        sizes = (owners, capacity, first, count, tiles, tiles * slabs, band)
        *outs, lse = attend(head_slot, mask, near[g], queries[g], ATTEND_US[g], *sizes)
        lses.append(lse)
        shape = jax.ShapeDtypeStruct(query_rows.shape, query_rows.dtype)
        target = unpack(head_slot, exchange(outs), target, capacity, first, shape, UNPACK_US[g])
    return target, jnp.concatenate(lses, axis=0)


def solution(mesh):
    rows = P(("groups", "slab", "head"), None)
    in_specs = (rows, rows, rows, P(None, ("groups", "slab"), None), P())
    out_specs = (rows, P("head", ("groups", "slab")))
    return jax.shard_map(
        on_device, mesh=mesh, in_specs=in_specs, out_specs=out_specs, check_vma=False
    )
```

time: 77 us -> 72.9 us (0.947)
  the two profiles are of different devices: /device:TPU:0 before, /device:TPU:1 now
where the time goes in v3:
time: 72.9 us; the launch traced here: 72.6 us
  starting transfers between devices  38.3 us (53%)
  waiting for transfers between devices  20.6 us (28%)
  Pallas kernels  12.3 us (17%)
  between operations  0.77 us (1%)
    ppermute x15, starting transfers between devices, exchange(): lax.ppermute(blocks[k], 'head', [(i, (i + k) % owners) for i in range(own...  27.4 us
    ppermute x15, waiting for transfers between devices, exchange(): lax.ppermute(blocks[k], 'head', [(i, (i + k) % owners) for i in range(own...  20.6 us
    ppermute x4, starting transfers between devices, swap(): return lax.ppermute(mid, 'slab', pairs + [(j, i) for i, j in pairs])  10.9 us
    pallas_call x2, Pallas kernels, attend(): pl.pallas_call(functools.partial(attend_kernel, owners, capacity, first,...  4.7 us
    pallas_call x2, Pallas kernels, pack(): pl.pallas_call(functools.partial(pack_kernel, owners, capacity, dim, plac...  3.67 us
    pallas_call x2, Pallas kernels, unpack(): pl.pallas_call(functools.partial(unpack_kernel, owners, capacity, first,...  3.33 us
  transfers between devices with their start and end apart: 19, of which 5 were waited for; matrix products, arithmetic and copies ran while one was open for 1% of the time, Pallas kernels for 12%

profile of v3, /device:TPU:1, one launch (start us, length us, event | category | flops | bytes accessed | tf_op | source)
XLA Modules:
  0.0 72.6 jit_solution(17760714223815744293)
XLA Ops:
  0.6 1.6 %pack.2 = (bf16[10,64,128]{2,1,0:T(8,128)(2,1)S(1)}, bf16[10,64,128]{2,1,0:T(8,128)(2,1)S(1)}, bf16[10,64,128]{2,1,0:T(8,128)(2,1)S(1)}, bf16[10,64,128]{2,1,0:T(8,128)(2,1)S(1)}) custom-call(s32[40]{0:T(128)} %head_slot.7, bf16[64,5120]{1,0:T(8,128)(2,1)} %refs_0_.5, bf16[64,5120]{1,0:T(8,128)(2,1)} %refs_2_.1), custom_call_target="tpu_custom_call" | custom-call | tf_op jit(solution)/shard_map/pack/pallas_call | solution.py:96
  2.3 2.2 %collective-permute-start.11 = (bf16[10,64,128]{2,1,0:T(8,128)(2,1)S(1)}, bf16[10,64,128]{2,1,0:T(8,128)(2,1)S(1)}, u32[]{:S(2)}, u32[]{:S(2)}) collective-permute-start(bf16[10,64,128]{2,1,0:T(8,128)(2,1)S(1)} %get-tuple-element.37), channel_id=1, source_target_pairs={{0,1},{1,2},{2,3},{3,0},{4,5},{5,6},{6,7},{7,4},{8,9},{9,10},{10,1... | collective-permute-start | bytes 491528 | tf_op jit(solution)/shard_map/ppermute | solution.py:332
  4.5 2.3 %collective-permute-start.12 = (bf16[10,64,128]{2,1,0:T(8,128)(2,1)S(1)}, bf16[10,64,128]{2,1,0:T(8,128)(2,1)S(1)}, u32[]{:S(2)}, u32[]{:S(2)}) collective-permute-start(bf16[10,64,128]{2,1,0:T(8,128)(2,1)S(1)} %get-tuple-element.38), channel_id=1, source_target_pairs={{0,2},{1,3},{2,0},{3,1},{4,6},{5,7},{6,4},{7,5},{8,10},{9,11},{10,... | collective-permute-start | bytes 491528 | tf_op jit(solution)/shard_map/ppermute | solution.py:332
  6.8 1.1 %collective-permute-start.13 = (bf16[10,64,128]{2,1,0:T(8,128)(2,1)S(1)}, bf16[10,64,128]{2,1,0:T(8,128)(2,1)S(1)}, u32[]{:S(2)}, u32[]{:S(2)}) collective-permute-start(bf16[10,64,128]{2,1,0:T(8,128)(2,1)S(1)} %get-tuple-element.39), channel_id=1, source_target_pairs={{0,3},{1,0},{2,1},{3,2},{4,7},{5,4},{6,5},{7,6},{8,11},{9,8},{10,9... | collective-permute-start | bytes 491528 | tf_op jit(solution)/shard_map/ppermute | solution.py:332
  7.8 2.0 %pack.3 = (bf16[15,64,128]{2,1,0:T(8,128)(2,1)S(1)}, bf16[15,64,128]{2,1,0:T(8,128)(2,1)S(1)}, bf16[15,64,128]{2,1,0:T(8,128)(2,1)S(1)}, bf16[15,64,128]{2,1,0:T...) custom-call(s32[40]{0:T(128)} %head_slot.7, ...), custom_call_target="tpu_custom_call" | custom-call | tf_op jit(solution)/shard_map/pack/pallas_call | solution.py:96
  9.9 0.5 collective-permute-start
  10.3 0.1 collective-permute-start.1
  10.4 0.1 collective-permute-done.11.refs_1_
  10.4 2.7 %collective-permute-start.2 = (bf16[15,64,128]{2,1,0:T(8,128)(2,1)S(1)}, bf16[15,64,128]{2,1,0:T(8,128)(2,1)S(1)}, u32[]{:S(2)}, u32[]{:S(2)}) collective-permute-start(bf16[15,64,128]{2,1,0:T(8,128)(2,1)S(1)} %get-tuple-element.28), channel_id=1, source_target_pairs={{0,3},{1,0},{2,1},{3,2},{4,7},{5,4},{6,5},{7,6},{8,11},{9,8},{10,9... | collective-permute-start | bytes 737288 | tf_op jit(solution)/shard_map/ppermute | solution.py:332
  13.2 5.7 %collective-permute-done.12.refs_2_ = bf16[10,64,128]{2,1,0:T(8,128)(2,1)S(1)} collective-permute-done((bf16[10,64,128]{2,1,0:T(8,128)(2,1)S(1)}, bf16[10,64,128]{2,1,0:T(8,128)(2,1)S(1)}, u32[]{:S(2)}, u32[]{:S(2)}) %collective-permute-start.12) | collective-permute-done | bytes 163872 | tf_op jit(solution)/shard_map/ppermute | solution.py:332
  18.9 0.0 collective-permute-done.13.refs_3_
  18.9 0.2 join.6.refs_0_
  19.1 4.7 %collective-permute-start.14 = (bf16[10,256,128]{2,1,0:T(8,128)(2,1)S(1)}, bf16[10,256,128]{2,1,0:T(8,128)(2,1)S(1)}, u32[]{:S(2)}, u32[]{:S(2)}) collective-permute-start(bf16[10,256,128]{2,1,0:T(8,128)(2,1)S(1)} %join.6.refs_0_), channel_id=1, source_target_pairs={{0,4},{8,12},{4,0},{12,8},{1,5},{9,13},{5,1},{13,9},{2,6},{10,14},... | collective-permute-start | bytes 1966088 | tf_op jit(solution)/shard_map/ppermute | solution.py:345
  23.8 0.0 collective-permute-done.refs_1_
  23.8 13.7 %collective-permute-done.1.refs_2_ = bf16[15,64,128]{2,1,0:T(8,128)(2,1)S(1)} collective-permute-done((bf16[15,64,128]{2,1,0:T(8,128)(2,1)S(1)}, bf16[15,64,128]{2,1,0:T(8,128)(2,1)S(1)}, u32[]{:S(2)}, u32[]{:S(2)}) %collective-permute-start.1) | collective-permute-done | bytes 245792 | tf_op jit(solution)/shard_map/ppermute | solution.py:332
  37.5 0.0 collective-permute-done.2.refs_3_
  37.5 0.2 join.4.refs_0_
  37.7 0.7 collective-permute-start.3
  38.3 0.0 collective-permute-done.14.refs_1_.refs_3_
  38.3 3.0 %collective-permute-start.15 = (bf16[10,256,128]{2,1,0:T(8,128)(2,1)S(1)}, bf16[10,256,128]{2,1,0:T(8,128)(2,1)S(1)}, u32[]{:S(2)}, u32[]{:S(2)}) collective-permute-start(bf16[10,256,128]{2,1,0:T(8,128)(2,1)S(1)} %after.3.refs_2_), channel_id=1, source_target_pairs={{4,8},{8,4},{5,9},{9,5},{6,10},{10,6},{7,11},{11,7},{20,24},{24,20... | collective-permute-start | bytes 1966088 | tf_op jit(solution)/shard_map/ppermute | solution.py:345
  41.4 0.0 collective-permute-done.3.refs_1_.refs_3_
  41.4 2.5 %collective-permute-start.4 = (bf16[10,256,128]{2,1,0:T(8,128)(2,1)S(1)}, bf16[10,256,128]{2,1,0:T(8,128)(2,1)S(1)}, u32[]{:S(2)}, u32[]{:S(2)}) collective-permute-start(bf16[10,256,128]{2,1,0:T(8,128)(2,1)S(1)} %after.2.refs_2_), channel_id=1, source_target_pairs={{4,8},{8,4},{5,9},{9,5},{6,10},{10,6},{7,11},{11,7},{20,24},{24,20... | collective-permute-start | bytes 1966088 | tf_op jit(solution)/shard_map/ppermute | solution.py:345
  43.9 5.5 %collective-permute-start.5 = (bf16[5,64,128]{2,1,0:T(8,128)(2,1)S(1)}, bf16[5,64,128]{2,1,0:T(8,128)(2,1)S(1)}, u32[]{:S(2)}, u32[]{:S(2)}) collective-permute-start(bf16[5,64,128]{2,1,0:T(8,128)(2,1)S(1)} %get-tuple-element.30), channel_id=1, source_target_pairs={{0,1},{1,2},{2,3},{3,0},{4,5},{5,6},{6,7},{7,4},{8,9},{9,10},{10,1... | collective-permute-start | bytes 245768 | tf_op jit(solution)/shard_map/ppermute | solution.py:332
  49.4 1.3 %collective-permute-start.6 = (bf16[5,64,128]{2,1,0:T(8,128)(2,1)S(1)}, bf16[5,64,128]{2,1,0:T(8,128)(2,1)S(1)}, u32[]{:S(2)}, u32[]{:S(2)}) collective-permute-start(bf16[5,64,128]{2,1,0:T(8,128)(2,1)S(1)} %get-tuple-element.31), channel_id=1, source_target_pairs={{0,2},{1,3},{2,0},{3,1},{4,6},{5,7},{6,4},{7,5},{8,10},{9,11},{10,... | collective-permute-start | bytes 245768 | tf_op jit(solution)/shard_map/ppermute | solution.py:332
  50.8 0.8 %collective-permute-start.7 = (bf16[5,64,128]{2,1,0:T(8,128)(2,1)S(1)}, bf16[5,64,128]{2,1,0:T(8,128)(2,1)S(1)}, u32[]{:S(2)}, u32[]{:S(2)}) collective-permute-start(bf16[5,64,128]{2,1,0:T(8,128)(2,1)S(1)} %get-tuple-element.32), channel_id=1, source_target_pairs={{0,3},{1,0},{2,1},{3,2},{4,7},{5,4},{6,5},{7,6},{8,11},{9,8},{10,9... | collective-permute-start | bytes 245768 | tf_op jit(solution)/shard_map/ppermute | solution.py:332
  51.6 0.1 join.7.refs_5_
  51.7 0.0 collective-permute-done.15.refs_4_
  51.7 2.4 %attend.3 = (bf16[5,64,128]{2,1,0:T(8,128)(2,1)S(1)}, bf16[5,64,128]{2,1,0:T(8,128)(2,1)S(1)}, bf16[5,64,128]{2,1,0:T(8,128)(2,1)S(1)}, bf16[5,64,128]{2,1,0:T(8,128)(2,1)S(1)}, f32[5,256]{1,0:T(8,128)S(1)}) custom-call(s32[40]{0:T(128)} %head_slot.7, s32[5,2,40]{2,1,0:T(2,128)} %bitcast.1, bf16[10,256,128]{2,1,0:T(8,128)(2,1)S(1)} %after.3.refs_2_, ...), custom_call_target="tpu_custom_call" | custom-call | tf_op jit(solution)/shard_map/attend/pallas_call | solution.py:254
  54.1 4.3 %collective-permute-start.16 = (bf16[5,64,128]{2,1,0:T(8,128)(2,1)S(1)}, bf16[5,64,128]{2,1,0:T(8,128)(2,1)S(1)}, u32[]{:S(2)}, u32[]{:S(2)}) collective-permute-start(bf16[5,64,128]{2,1,0:T(8,128)(2,1)S(1)} %get-tuple-element.41), channel_id=1, source_target_pairs={{0,1},{1,2},{2,3},{3,0},{4,5},{5,6},{6,7},{7,4},{8,9},{9,10},{10,1... | collective-permute-start | bytes 245768 | tf_op jit(solution)/shard_map/ppermute | solution.py:332
  58.4 0.0 collective-permute-done.5.refs_1_
  58.4 1.4 %collective-permute-start.17 = (bf16[5,64,128]{2,1,0:T(8,128)(2,1)S(1)}, bf16[5,64,128]{2,1,0:T(8,128)(2,1)S(1)}, u32[]{:S(2)}, u32[]{:S(2)}) collective-permute-start(bf16[5,64,128]{2,1,0:T(8,128)(2,1)S(1)} %get-tuple-element.42), channel_id=1, source_target_pairs={{0,2},{1,3},{2,0},{3,1},{4,6},{5,7},{6,4},{7,5},{8,10},{9,11},{10,... | collective-permute-start | bytes 245768 | tf_op jit(solution)/shard_map/ppermute | solution.py:332
  59.8 0.0 collective-permute-done.6.refs_2_
  59.8 0.8 %collective-permute-start.18 = (bf16[5,64,128]{2,1,0:T(8,128)(2,1)S(1)}, bf16[5,64,128]{2,1,0:T(8,128)(2,1)S(1)}, u32[]{:S(2)}, u32[]{:S(2)}) collective-permute-start(bf16[5,64,128]{2,1,0:T(8,128)(2,1)S(1)} %get-tuple-element.43), channel_id=1, source_target_pairs={{0,3},{1,0},{2,1},{3,2},{4,7},{5,4},{6,5},{7,6},{8,11},{9,8},{10,9... | collective-permute-start | bytes 245768 | tf_op jit(solution)/shard_map/ppermute | solution.py:332
  60.6 0.0 collective-permute-done.7.refs_3_
  60.6 0.1 join.5.refs_5_
  60.7 0.0 collective-permute-done.4.refs_4_
  60.7 2.4 %attend.2 = (bf16[5,64,128]{2,1,0:T(8,128)(2,1)S(1)}, bf16[5,64,128]{2,1,0:T(8,128)(2,1)S(1)}, bf16[5,64,128]{2,1,0:T(8,128)(2,1)S(1)}, bf16[5,64,128]{2,1,0:T(8,128)(2,1)S(1)}, f32[5,256]{1,0:T(8,128)S(1)}) custom-call(s32[40]{0:T(128)} %head_slot.7, s32[5,2,40]{2,1,0:T(2,128)} %bitcast.2, bf16[10,256,128]{2,1,0:T(8,128)(2,1)S(1)} %after.2.refs_2_, ...), custom_call_target="tpu_custom_call" | custom-call | tf_op jit(solution)/shard_map/attend/pallas_call | solution.py:254
  63.1 2.3 %collective-permute-start.8 = (bf16[5,64,128]{2,1,0:T(8,128)(2,1)S(1)}, bf16[5,64,128]{2,1,0:T(8,128)(2,1)S(1)}, u32[]{:S(2)}, u32[]{:S(2)}) collective-permute-start(bf16[5,64,128]{2,1,0:T(8,128)(2,1)S(1)} %get-tuple-element.34), channel_id=1, source_target_pairs={{0,1},{1,2},{2,3},{3,0},{4,5},{5,6},{6,7},{7,4},{8,9},{9,10},{10,1... | collective-permute-start | bytes 245768 | tf_op jit(solution)/shard_map/ppermute | solution.py:332
  65.4 1.4 %collective-permute-start.9 = (bf16[5,64,128]{2,1,0:T(8,128)(2,1)S(1)}, bf16[5,64,128]{2,1,0:T(8,128)(2,1)S(1)}, u32[]{:S(2)}, u32[]{:S(2)}) collective-permute-start(bf16[5,64,128]{2,1,0:T(8,128)(2,1)S(1)} %get-tuple-element.35), channel_id=1, source_target_pairs={{0,2},{1,3},{2,0},{3,1},{4,6},{5,7},{6,4},{7,5},{8,10},{9,11},{10,... | collective-permute-start | bytes 245768 | tf_op jit(solution)/shard_map/ppermute | solution.py:332
  66.8 0.0 collective-permute-done.16.refs_1_
  66.8 0.8 %collective-permute-start.10 = (bf16[5,64,128]{2,1,0:T(8,128)(2,1)S(1)}, bf16[5,64,128]{2,1,0:T(8,128)(2,1)S(1)}, u32[]{:S(2)}, u32[]{:S(2)}) collective-permute-start(bf16[5,64,128]{2,1,0:T(8,128)(2,1)S(1)} %get-tuple-element.36), channel_id=1, source_target_pairs={{0,3},{1,0},{2,1},{3,2},{4,7},{5,4},{6,5},{7,6},{8,11},{9,8},{10,9... | collective-permute-start | bytes 245768 | tf_op jit(solution)/shard_map/ppermute | solution.py:332
  67.6 0.0 collective-permute-done.17.refs_2_
  67.6 0.0 collective-permute-done.18.refs_3_
  67.6 1.7 %unpack.2.refs_4_ = bf16[64,5120]{1,0:T(8,128)(2,1)} custom-call(s32[40]{0:T(128)} %head_slot.7, bf16[5,64,128]{2,1,0:T(8,128)(2,1)S(1)} %get-tuple-element.40.refs_0_, bf16[5,64,128]{2,1,0:T(8,128)(2,1)S(1)} %collective-permute-done.16.refs_1_, bf16[5,64,128]{2,1,0:T(8,128)(2,1)S(1)} %collective-permute-done.17.refs_2_, ...), custom_call_target="tpu_custom_call" | custom-call | tf_op jit(solution)/shard_map/unpack/pallas_call | solution.py:309
  69.2 0.6 pad_maximum_fusion
  69.9 0.0 collective-permute-done.8.refs_1_
  69.9 0.6 collective-permute-done.9.refs_2_
  70.4 0.5 collective-permute-done.10.refs_3_
  70.9 1.7 %unpack.3 = bf16[64,5120]{1,0:T(8,128)(2,1)} custom-call(s32[40]{0:T(128)} %head_slot.7, bf16[5,64,128]{2,1,0:T(8,128)(2,1)S(1)} %get-tuple-element.33.refs_0_, bf16[5,64,128]{2,1,0:T(8,128)(2,1)S(1)} %collective-permute-done.8.refs_1_, bf16[5,64,128]{2,1,0:T(8,128)(2,1)S(1)} %collective-permute-done.9.refs_2_, ...), custom_call_target="tpu_custom_call", output_to_operand_aliasing={{}: (5, {})} | custom-call | tf_op jit(solution)/shard_map/unpack/pallas_call | solution.py:309
  (2 shorter events, 0.0 us)
Async XLA Ops:
  2.3 8.2 %collective-permute-start.11 = (bf16[10,64,128]{2,1,0:T(8,128)(2,1)S(1)}, bf16[10,64,128]{2,1,0:T(8,128)(2,1)S(1)}, u32[]{:S(2)}, u32[]{:S(2)}) collective-permute-start(bf16[10,64,128]{2,1,0:T(8,128)(2,1)S(1)} %get-tuple-element.37), channel_id=1, source_target_pairs={{0,1},{1,2},{2,3},{3,0},{4,5},{5,6},{6,7},{7,4},{8,9},{9,10},{10,1... | collective-permute-start | bytes 491528 | tf_op jit(solution)/shard_map/ppermute | solution.py:332
  4.5 14.5 %collective-permute-start.12 = (bf16[10,64,128]{2,1,0:T(8,128)(2,1)S(1)}, bf16[10,64,128]{2,1,0:T(8,128)(2,1)S(1)}, u32[]{:S(2)}, u32[]{:S(2)}) collective-permute-start(bf16[10,64,128]{2,1,0:T(8,128)(2,1)S(1)} %get-tuple-element.38), channel_id=1, source_target_pairs={{0,2},{1,3},{2,0},{3,1},{4,6},{5,7},{6,4},{7,5},{8,10},{9,11},{10,... | collective-permute-start | bytes 491528 | tf_op jit(solution)/shard_map/ppermute | solution.py:332
  6.8 12.2 %collective-permute-start.13 = (bf16[10,64,128]{2,1,0:T(8,128)(2,1)S(1)}, bf16[10,64,128]{2,1,0:T(8,128)(2,1)S(1)}, u32[]{:S(2)}, u32[]{:S(2)}) collective-permute-start(bf16[10,64,128]{2,1,0:T(8,128)(2,1)S(1)} %get-tuple-element.39), channel_id=1, source_target_pairs={{0,3},{1,0},{2,1},{3,2},{4,7},{5,4},{6,5},{7,6},{8,11},{9,8},{10,9... | collective-permute-start | bytes 491528 | tf_op jit(solution)/shard_map/ppermute | solution.py:332
  9.9 14.0 %collective-permute-start = (bf16[15,64,128]{2,1,0:T(8,128)(2,1)S(1)}, bf16[15,64,128]{2,1,0:T(8,128)(2,1)S(1)}, u32[]{:S(2)}, u32[]{:S(2)}) collective-permute-start(bf16[15,64,128]{2,1,0:T(8,128)(2,1)S(1)} %get-tuple-element.26), channel_id=1, source_target_pairs={{0,1},{1,2},{2,3},{3,0},{4,5},{5,6},{6,7},{7,4},{8,9},{9,10},{10,1... | collective-permute-start | bytes 737288 | tf_op jit(solution)/shard_map/ppermute | solution.py:332
  10.3 27.2 %collective-permute-start.1 = (bf16[15,64,128]{2,1,0:T(8,128)(2,1)S(1)}, bf16[15,64,128]{2,1,0:T(8,128)(2,1)S(1)}, u32[]{:S(2)}, u32[]{:S(2)}) collective-permute-start(bf16[15,64,128]{2,1,0:T(8,128)(2,1)S(1)} %get-tuple-element.27), channel_id=1, source_target_pairs={{0,2},{1,3},{2,0},{3,1},{4,6},{5,7},{6,4},{7,5},{8,10},{9,11},{10,... | collective-permute-start | bytes 737288 | tf_op jit(solution)/shard_map/ppermute | solution.py:332
  10.4 27.1 %collective-permute-start.2 = (bf16[15,64,128]{2,1,0:T(8,128)(2,1)S(1)}, bf16[15,64,128]{2,1,0:T(8,128)(2,1)S(1)}, u32[]{:S(2)}, u32[]{:S(2)}) collective-permute-start(bf16[15,64,128]{2,1,0:T(8,128)(2,1)S(1)} %get-tuple-element.28), channel_id=1, source_target_pairs={{0,3},{1,0},{2,1},{3,2},{4,7},{5,4},{6,5},{7,6},{8,11},{9,8},{10,9... | collective-permute-start | bytes 737288 | tf_op jit(solution)/shard_map/ppermute | solution.py:332
  19.1 19.2 %collective-permute-start.14 = (bf16[10,256,128]{2,1,0:T(8,128)(2,1)S(1)}, bf16[10,256,128]{2,1,0:T(8,128)(2,1)S(1)}, u32[]{:S(2)}, u32[]{:S(2)}) collective-permute-start(bf16[10,256,128]{2,1,0:T(8,128)(2,1)S(1)} %join.6.refs_0_), channel_id=1, source_target_pairs={{0,4},{8,12},{4,0},{12,8},{1,5},{9,13},{5,1},{13,9},{2,6},{10,14},... | collective-permute-start | bytes 1966088 | tf_op jit(solution)/shard_map/ppermute | solution.py:345
  37.7 3.7 %collective-permute-start.3 = (bf16[10,256,128]{2,1,0:T(8,128)(2,1)S(1)}, bf16[10,256,128]{2,1,0:T(8,128)(2,1)S(1)}, u32[]{:S(2)}, u32[]{:S(2)}) collective-permute-start(bf16[10,256,128]{2,1,0:T(8,128)(2,1)S(1)} %join.4.refs_0_), channel_id=1, source_target_pairs={{0,4},{8,12},{4,0},{12,8},{1,5},{9,13},{5,1},{13,9},{2,6},{10,14},... | collective-permute-start | bytes 1966088 | tf_op jit(solution)/shard_map/ppermute | solution.py:345
  38.3 13.4 %collective-permute-start.15 = (bf16[10,256,128]{2,1,0:T(8,128)(2,1)S(1)}, bf16[10,256,128]{2,1,0:T(8,128)(2,1)S(1)}, u32[]{:S(2)}, u32[]{:S(2)}) collective-permute-start(bf16[10,256,128]{2,1,0:T(8,128)(2,1)S(1)} %after.3.refs_2_), channel_id=1, source_target_pairs={{4,8},{8,4},{5,9},{9,5},{6,10},{10,6},{7,11},{11,7},{20,24},{24,20... | collective-permute-start | bytes 1966088 | tf_op jit(solution)/shard_map/ppermute | solution.py:345
  41.4 19.3 %collective-permute-start.4 = (bf16[10,256,128]{2,1,0:T(8,128)(2,1)S(1)}, bf16[10,256,128]{2,1,0:T(8,128)(2,1)S(1)}, u32[]{:S(2)}, u32[]{:S(2)}) collective-permute-start(bf16[10,256,128]{2,1,0:T(8,128)(2,1)S(1)} %after.2.refs_2_), channel_id=1, source_target_pairs={{4,8},{8,4},{5,9},{9,5},{6,10},{10,6},{7,11},{11,7},{20,24},{24,20... | collective-permute-start | bytes 1966088 | tf_op jit(solution)/shard_map/ppermute | solution.py:345
  43.9 14.5 %collective-permute-start.5 = (bf16[5,64,128]{2,1,0:T(8,128)(2,1)S(1)}, bf16[5,64,128]{2,1,0:T(8,128)(2,1)S(1)}, u32[]{:S(2)}, u32[]{:S(2)}) collective-permute-start(bf16[5,64,128]{2,1,0:T(8,128)(2,1)S(1)} %get-tuple-element.30), channel_id=1, source_target_pairs={{0,1},{1,2},{2,3},{3,0},{4,5},{5,6},{6,7},{7,4},{8,9},{9,10},{10,1... | collective-permute-start | bytes 245768 | tf_op jit(solution)/shard_map/ppermute | solution.py:332
  49.4 10.3 %collective-permute-start.6 = (bf16[5,64,128]{2,1,0:T(8,128)(2,1)S(1)}, bf16[5,64,128]{2,1,0:T(8,128)(2,1)S(1)}, u32[]{:S(2)}, u32[]{:S(2)}) collective-permute-start(bf16[5,64,128]{2,1,0:T(8,128)(2,1)S(1)} %get-tuple-element.31), channel_id=1, source_target_pairs={{0,2},{1,3},{2,0},{3,1},{4,6},{5,7},{6,4},{7,5},{8,10},{9,11},{10,... | collective-permute-start | bytes 245768 | tf_op jit(solution)/shard_map/ppermute | solution.py:332
  50.8 9.8 %collective-permute-start.7 = (bf16[5,64,128]{2,1,0:T(8,128)(2,1)S(1)}, bf16[5,64,128]{2,1,0:T(8,128)(2,1)S(1)}, u32[]{:S(2)}, u32[]{:S(2)}) collective-permute-start(bf16[5,64,128]{2,1,0:T(8,128)(2,1)S(1)} %get-tuple-element.32), channel_id=1, source_target_pairs={{0,3},{1,0},{2,1},{3,2},{4,7},{5,4},{6,5},{7,6},{8,11},{9,8},{10,9... | collective-permute-start | bytes 245768 | tf_op jit(solution)/shard_map/ppermute | solution.py:332
  54.1 12.7 %collective-permute-start.16 = (bf16[5,64,128]{2,1,0:T(8,128)(2,1)S(1)}, bf16[5,64,128]{2,1,0:T(8,128)(2,1)S(1)}, u32[]{:S(2)}, u32[]{:S(2)}) collective-permute-start(bf16[5,64,128]{2,1,0:T(8,128)(2,1)S(1)} %get-tuple-element.41), channel_id=1, source_target_pairs={{0,1},{1,2},{2,3},{3,0},{4,5},{5,6},{6,7},{7,4},{8,9},{9,10},{10,1... | collective-permute-start | bytes 245768 | tf_op jit(solution)/shard_map/ppermute | solution.py:332
  58.4 9.2 %collective-permute-start.17 = (bf16[5,64,128]{2,1,0:T(8,128)(2,1)S(1)}, bf16[5,64,128]{2,1,0:T(8,128)(2,1)S(1)}, u32[]{:S(2)}, u32[]{:S(2)}) collective-permute-start(bf16[5,64,128]{2,1,0:T(8,128)(2,1)S(1)} %get-tuple-element.42), channel_id=1, source_target_pairs={{0,2},{1,3},{2,0},{3,1},{4,6},{5,7},{6,4},{7,5},{8,10},{9,11},{10,... | collective-permute-start | bytes 245768 | tf_op jit(solution)/shard_map/ppermute | solution.py:332
  59.8 7.8 %collective-permute-start.18 = (bf16[5,64,128]{2,1,0:T(8,128)(2,1)S(1)}, bf16[5,64,128]{2,1,0:T(8,128)(2,1)S(1)}, u32[]{:S(2)}, u32[]{:S(2)}) collective-permute-start(bf16[5,64,128]{2,1,0:T(8,128)(2,1)S(1)} %get-tuple-element.43), channel_id=1, source_target_pairs={{0,3},{1,0},{2,1},{3,2},{4,7},{5,4},{6,5},{7,6},{8,11},{9,8},{10,9... | collective-permute-start | bytes 245768 | tf_op jit(solution)/shard_map/ppermute | solution.py:332
  63.1 6.8 %collective-permute-start.8 = (bf16[5,64,128]{2,1,0:T(8,128)(2,1)S(1)}, bf16[5,64,128]{2,1,0:T(8,128)(2,1)S(1)}, u32[]{:S(2)}, u32[]{:S(2)}) collective-permute-start(bf16[5,64,128]{2,1,0:T(8,128)(2,1)S(1)} %get-tuple-element.34), channel_id=1, source_target_pairs={{0,1},{1,2},{2,3},{3,0},{4,5},{5,6},{6,7},{7,4},{8,9},{9,10},{10,1... | collective-permute-start | bytes 245768 | tf_op jit(solution)/shard_map/ppermute | solution.py:332
  65.4 5.0 %collective-permute-start.9 = (bf16[5,64,128]{2,1,0:T(8,128)(2,1)S(1)}, bf16[5,64,128]{2,1,0:T(8,128)(2,1)S(1)}, u32[]{:S(2)}, u32[]{:S(2)}) collective-permute-start(bf16[5,64,128]{2,1,0:T(8,128)(2,1)S(1)} %get-tuple-element.35), channel_id=1, source_target_pairs={{0,2},{1,3},{2,0},{3,1},{4,6},{5,7},{6,4},{7,5},{8,10},{9,11},{10,... | collective-permute-start | bytes 245768 | tf_op jit(solution)/shard_map/ppermute | solution.py:332
  66.8 4.2 %collective-permute-start.10 = (bf16[5,64,128]{2,1,0:T(8,128)(2,1)S(1)}, bf16[5,64,128]{2,1,0:T(8,128)(2,1)S(1)}, u32[]{:S(2)}, u32[]{:S(2)}) collective-permute-start(bf16[5,64,128]{2,1,0:T(8,128)(2,1)S(1)} %get-tuple-element.36), channel_id=1, source_target_pairs={{0,3},{1,0},{2,1},{3,2},{4,7},{5,4},{6,5},{7,6},{8,11},{9,8},{10,9... | collective-permute-start | bytes 245768 | tf_op jit(solution)/shard_map/ppermute | solution.py:332

commit v4 on v3

--- a/solution.py
+++ b/solution.py
@@ -21,12 +21,10 @@
 PACK_US = (0.0, 0.0, 0.0, 0.0)
 JOIN_US = (0.0, 0.0)
 QJOIN_US = (0.0, 0.0)
-WAIT_LAST = False
 ATTEND_US = (0.0, 0.0)
 UNPACK_US = (0.0, 0.0)
-CHAIN = True
-HOLD = 0
-ORDER = (2, 1, 3)
+FIRST = (1, 0)
+ORDER = (1, 3, 2)
 
 
 def hint(us):
@@ -38,10 +36,11 @@
 
 
 def invert(head_slot, head_of, used=None):
-    for j in range(head_of.shape[0]):
-        head_of[j] = 0
-        if used is not None:
-            used[j] = 0
+    if head_of.shape[0] > head_slot.shape[0] or used is not None:
+        for j in range(head_of.shape[0]):
+            head_of[j] = 0
+            if used is not None:
+                used[j] = 0
     for h in range(head_slot.shape[0]):
         head_of[head_slot[h]] = h
         if used is not None:
@@ -277,12 +276,10 @@
 
 def unpack_kernel(owners, capacity, first, count, dim, head_slot, *refs):
     blocks = refs[:owners]
-    out, slots, head_of, used, sem, sem_slots = refs[-6:]
+    out, head_of, used, sem = refs[-4:]
     me = lax.axis_index("head")
-    slot_copy = pltpu.make_async_copy(head_slot, slots, sem_slots)
-    slot_copy.start()
-    slot_copy.wait()
-    invert(slots, head_of, used)
+    whole = owners * capacity == head_slot.shape[0]
+    invert(head_slot, head_of, None if whole else used)
 
     def each(act):
         for k in range(owners):
@@ -293,7 +290,7 @@
                 copy = pltpu.make_async_copy(
                     blocks[k].at[c], out.at[:, columns], sem.at[k * count + c]
                 )
-                if owners * capacity == head_slot.shape[0]:
+                if whole:
                     act(copy)
                 else:
                     pl.when(used[slot] > 0)(functools.partial(act, copy))
@@ -309,20 +306,18 @@
     return pl.pallas_call(
         functools.partial(unpack_kernel, owners, capacity, first, count, dim),
         out_shape=shape,
-        in_specs=[ANY] * (owners + 1) + ([] if target is None else [HBM]),
+        in_specs=[SMEM] + [ANY] * owners + ([] if target is None else [HBM]),
         out_specs=HBM,
         input_output_aliases={} if target is None else {owners + 1: 0},
         scratch_shapes=[
-            pltpu.SMEM(head_slot.shape, jnp.int32),
             pltpu.SMEM((owners * capacity,), jnp.int32),
             pltpu.SMEM((owners * capacity,), jnp.int32),
             pltpu.SemaphoreType.DMA((owners * count,)),
-            pltpu.SemaphoreType.DMA,
         ],
         cost_estimate=hint(us),
         compiler_params=SMALL,
         name="unpack",
-    )(in_hbm(head_slot), *operands)
+    )(head_slot, *operands)
 
 
 def exchange(blocks):
@@ -376,7 +371,7 @@
     args = (owners, capacity, dim)
     packed = pack(head_slot, source, sizes[:1], *args, PACK_US[0])
     if len(sizes) > 1:
-        packed += pack(head_slot, source, sizes[1:], *args, PACK_US[1], packed[0][:1] if CHAIN else ())
+        packed += pack(head_slot, source, sizes[1:], *args, PACK_US[1], packed[0][:1])
     moved = [exchange(blocks) for blocks in packed]
     near, queries = {}, {}
     for blocks, held in zip(moved, STAGES):
@@ -387,11 +382,11 @@
                 queries[g] = join(blocks, skip, count, QJOIN_US[g])
             if name == "k":
                 mid = join(blocks, skip, 2 * count, JOIN_US[g])
-                if g == 1 and HOLD:
-                    mid = after(mid, moved[-1][HOLD])
-                even = swap(mid, 0, halo)
-                mid = after(mid, even)
-                near[g] = (mid, even, swap(mid, 1, halo))
+                lead = FIRST[g]
+                one = swap(mid, lead, halo)
+                mid = after(mid, one)
+                two = swap(mid, 1 - lead, halo)
+                near[g] = (mid, two, one) if lead else (mid, one, two)
             skip += count
 
     target, lses = None, []

time: 72.9 us -> 71.2 us (0.977)
  the two profiles are of different devices: /device:TPU:1 before, /device:TPU:0 now
where the time goes in v4:
time: 71.2 us; the launch traced here: 70.9 us
  starting transfers between devices  29.1 us (41%)
  waiting for transfers between devices  28.5 us (40%)
  Pallas kernels  11.9 us (17%)
  between operations  0.78 us (1%)
    ppermute x15, starting transfers between devices, exchange(): lax.ppermute(blocks[k], 'head', [(i, (i + k) % owners) for i in range(own...  27.2 us
    ppermute x15, waiting for transfers between devices, exchange(): lax.ppermute(blocks[k], 'head', [(i, (i + k) % owners) for i in range(own...  26.9 us
    pallas_call x2, Pallas kernels, attend(): pl.pallas_call(functools.partial(attend_kernel, owners, capacity, first,...  4.71 us
    pallas_call x2, Pallas kernels, pack(): pl.pallas_call(functools.partial(pack_kernel, owners, capacity, dim, plac...  3.67 us
    pallas_call x2, Pallas kernels, unpack(): pl.pallas_call(functools.partial(unpack_kernel, owners, capacity, first,...  2.95 us
    ppermute x4, starting transfers between devices, swap(): return lax.ppermute(mid, 'slab', pairs + [(j, i) for i, j in pairs])  1.95 us
    ppermute x4, waiting for transfers between devices, swap(): return lax.ppermute(mid, 'slab', pairs + [(j, i) for i, j in pairs])  1.59 us
  transfers between devices with their start and end apart: 19, of which 8 were waited for; matrix products, arithmetic and copies ran while one was open for 1% of the time, Pallas kernels for 12%

profile of v4, /device:TPU:0, one launch (start us, length us, event | category | flops | bytes accessed | tf_op | source)
XLA Modules:
  0.0 70.9 jit_solution(13538043704884908397)
XLA Ops:
  0.6 1.6 %pack.2 = (bf16[10,64,128]{2,1,0:T(8,128)(2,1)S(1)}, bf16[10,64,128]{2,1,0:T(8,128)(2,1)S(1)}, bf16[10,64,128]{2,1,0:T(8,128)(2,1)S(1)}, bf16[10,64,128]{2,1,0:T(8,128)(2,1)S(1)}) custom-call(s32[40]{0:T(128)} %head_slot.7, bf16[64,5120]{1,0:T(8,128)(2,1)} %refs_0_.5, bf16[64,5120]{1,0:T(8,128)(2,1)} %refs_2_.1), custom_call_target="tpu_custom_call" | custom-call | tf_op jit(solution)/shard_map/pack/pallas_call | solution.py:95
  2.3 3.1 %collective-permute-start.11 = (bf16[10,64,128]{2,1,0:T(8,128)(2,1)S(1)}, bf16[10,64,128]{2,1,0:T(8,128)(2,1)S(1)}, u32[]{:S(2)}, u32[]{:S(2)}) collective-permute-start(bf16[10,64,128]{2,1,0:T(8,128)(2,1)S(1)} %get-tuple-element.37), channel_id=1, source_target_pairs={{0,1},{1,2},{2,3},{3,0},{4,5},{5,6},{6,7},{7,4},{8,9},{9,10},{10,1... | collective-permute-start | bytes 491528 | tf_op jit(solution)/shard_map/ppermute | solution.py:327
  5.4 2.6 %collective-permute-start.12 = (bf16[10,64,128]{2,1,0:T(8,128)(2,1)S(1)}, bf16[10,64,128]{2,1,0:T(8,128)(2,1)S(1)}, u32[]{:S(2)}, u32[]{:S(2)}) collective-permute-start(bf16[10,64,128]{2,1,0:T(8,128)(2,1)S(1)} %get-tuple-element.38), channel_id=1, source_target_pairs={{0,2},{1,3},{2,0},{3,1},{4,6},{5,7},{6,4},{7,5},{8,10},{9,11},{10,... | collective-permute-start | bytes 491528 | tf_op jit(solution)/shard_map/ppermute | solution.py:327
  7.9 1.3 %collective-permute-start.13 = (bf16[10,64,128]{2,1,0:T(8,128)(2,1)S(1)}, bf16[10,64,128]{2,1,0:T(8,128)(2,1)S(1)}, u32[]{:S(2)}, u32[]{:S(2)}) collective-permute-start(bf16[10,64,128]{2,1,0:T(8,128)(2,1)S(1)} %get-tuple-element.39), channel_id=1, source_target_pairs={{0,3},{1,0},{2,1},{3,2},{4,7},{5,4},{6,5},{7,6},{8,11},{9,8},{10,9... | collective-permute-start | bytes 491528 | tf_op jit(solution)/shard_map/ppermute | solution.py:327
  9.3 2.0 %pack.3 = (bf16[15,64,128]{2,1,0:T(8,128)(2,1)S(1)}, bf16[15,64,128]{2,1,0:T(8,128)(2,1)S(1)}, bf16[15,64,128]{2,1,0:T(8,128)(2,1)S(1)}, bf16[15,64,128]{2,1,0:T...) custom-call(s32[40]{0:T(128)} %head_slot.7, ...), custom_call_target="tpu_custom_call" | custom-call | tf_op jit(solution)/shard_map/pack/pallas_call | solution.py:95
  11.3 0.7 %collective-permute-start = (bf16[15,64,128]{2,1,0:T(8,128)(2,1)S(1)}, bf16[15,64,128]{2,1,0:T(8,128)(2,1)S(1)}, u32[]{:S(2)}, u32[]{:S(2)}) collective-permute-start(bf16[15,64,128]{2,1,0:T(8,128)(2,1)S(1)} %get-tuple-element.26), channel_id=1, source_target_pairs={{0,1},{1,2},{2,3},{3,0},{4,5},{5,6},{6,7},{7,4},{8,9},{9,10},{10,1... | collective-permute-start | bytes 737288 | tf_op jit(solution)/shard_map/ppermute | solution.py:327
  12.1 0.3 collective-permute-start.1
  12.4 0.1 collective-permute-done.11.refs_1_
  12.5 2.7 %collective-permute-start.2 = (bf16[15,64,128]{2,1,0:T(8,128)(2,1)S(1)}, bf16[15,64,128]{2,1,0:T(8,128)(2,1)S(1)}, u32[]{:S(2)}, u32[]{:S(2)}) collective-permute-start(bf16[15,64,128]{2,1,0:T(8,128)(2,1)S(1)} %get-tuple-element.28), channel_id=1, source_target_pairs={{0,3},{1,0},{2,1},{3,2},{4,7},{5,4},{6,5},{7,6},{8,11},{9,8},{10,9... | collective-permute-start | bytes 737288 | tf_op jit(solution)/shard_map/ppermute | solution.py:327
  15.2 4.4 %collective-permute-done.12.refs_2_ = bf16[10,64,128]{2,1,0:T(8,128)(2,1)S(1)} collective-permute-done((bf16[10,64,128]{2,1,0:T(8,128)(2,1)S(1)}, bf16[10,64,128]{2,1,0:T(8,128)(2,1)S(1)}, u32[]{:S(2)}, u32[]{:S(2)}) %collective-permute-start.12) | collective-permute-done | bytes 163872 | tf_op jit(solution)/shard_map/ppermute | solution.py:327
  19.6 4.0 %collective-permute-done.13.refs_3_ = bf16[10,64,128]{2,1,0:T(8,128)(2,1)S(1)} collective-permute-done((bf16[10,64,128]{2,1,0:T(8,128)(2,1)S(1)}, bf16[10,64,128]{2,1,0:T(8,128)(2,1)S(1)}, u32[]{:S(2)}, u32[]{:S(2)}) %collective-permute-start.13) | collective-permute-done | bytes 163872 | tf_op jit(solution)/shard_map/ppermute | solution.py:327
  23.5 0.2 join.6.refs_0_
  23.7 0.7 collective-permute-start.14
  24.4 0.4 collective-permute-done.refs_1_
  24.8 13.2 %collective-permute-done.1.refs_2_ = bf16[15,64,128]{2,1,0:T(8,128)(2,1)S(1)} collective-permute-done((bf16[15,64,128]{2,1,0:T(8,128)(2,1)S(1)}, bf16[15,64,128]{2,1,0:T(8,128)(2,1)S(1)}, u32[]{:S(2)}, u32[]{:S(2)}) %collective-permute-start.1) | collective-permute-done | bytes 245792 | tf_op jit(solution)/shard_map/ppermute | solution.py:327
  38.0 0.0 collective-permute-done.2.refs_3_
  38.0 0.2 join.4.refs_0_
  38.2 0.1 collective-permute-start.3
  38.3 0.0 collective-permute-done.14.refs_1_.refs_4_
  38.3 0.5 collective-permute-start.15
  38.8 1.6 %collective-permute-done.3.refs_1_.refs_3_ = bf16[10,256,128]{2,1,0:T(8,128)(2,1)S(1)} collective-permute-done((bf16[10,256,128]{2,1,0:T(8,128)(2,1)S(1)}, bf16[10,256,128]{2,1,0:T(8,128)(2,1)S(1)}, u32[]{:S(2)}, u32[]{:S(2)}) %collective-permute-start.3) | collective-permute-done | bytes 655392 | tf_op jit(solution)/shard_map/ppermute | solution.py:340
  40.4 0.7 collective-permute-start.4
  41.1 5.8 %collective-permute-start.5 = (bf16[5,64,128]{2,1,0:T(8,128)(2,1)S(1)}, bf16[5,64,128]{2,1,0:T(8,128)(2,1)S(1)}, u32[]{:S(2)}, u32[]{:S(2)}) collective-permute-start(bf16[5,64,128]{2,1,0:T(8,128)(2,1)S(1)} %get-tuple-element.30), channel_id=1, source_target_pairs={{0,1},{1,2},{2,3},{3,0},{4,5},{5,6},{6,7},{7,4},{8,9},{9,10},{10,1... | collective-permute-start | bytes 245768 | tf_op jit(solution)/shard_map/ppermute | solution.py:327
  46.9 1.6 %collective-permute-start.6 = (bf16[5,64,128]{2,1,0:T(8,128)(2,1)S(1)}, bf16[5,64,128]{2,1,0:T(8,128)(2,1)S(1)}, u32[]{:S(2)}, u32[]{:S(2)}) collective-permute-start(bf16[5,64,128]{2,1,0:T(8,128)(2,1)S(1)} %get-tuple-element.31), channel_id=1, source_target_pairs={{0,2},{1,3},{2,0},{3,1},{4,6},{5,7},{6,4},{7,5},{8,10},{9,11},{10,... | collective-permute-start | bytes 245768 | tf_op jit(solution)/shard_map/ppermute | solution.py:327
  48.5 0.8 %collective-permute-start.7 = (bf16[5,64,128]{2,1,0:T(8,128)(2,1)S(1)}, bf16[5,64,128]{2,1,0:T(8,128)(2,1)S(1)}, u32[]{:S(2)}, u32[]{:S(2)}) collective-permute-start(bf16[5,64,128]{2,1,0:T(8,128)(2,1)S(1)} %get-tuple-element.32), channel_id=1, source_target_pairs={{0,3},{1,0},{2,1},{3,2},{4,7},{5,4},{6,5},{7,6},{8,11},{9,8},{10,9... | collective-permute-start | bytes 245768 | tf_op jit(solution)/shard_map/ppermute | solution.py:327
  49.3 0.1 join.7.refs_5_
  49.4 0.0 collective-permute-done.15.refs_3_
  49.5 2.4 %attend.3 = (bf16[5,64,128]{2,1,0:T(8,128)(2,1)S(1)}, bf16[5,64,128]{2,1,0:T(8,128)(2,1)S(1)}, bf16[5,64,128]{2,1,0:T(8,128)(2,1)S(1)}, bf16[5,64,128]{2,1,0:T(8,128)(2,1)S(1)}, f32[5,256]{1,0:T(8,128)S(1)}) custom-call(s32[40]{0:T(128)} %head_slot.7, s32[5,2,40]{2,1,0:T(2,128)} %bitcast.1, bf16[10,256,128]{2,1,0:T(8,128)(2,1)S(1)} %after.3.refs_2_, ...), custom_call_target="tpu_custom_call" | custom-call | tf_op jit(solution)/shard_map/attend/pallas_call | solution.py:253
  51.8 1.3 %collective-permute-start.16 = (bf16[5,64,128]{2,1,0:T(8,128)(2,1)S(1)}, bf16[5,64,128]{2,1,0:T(8,128)(2,1)S(1)}, u32[]{:S(2)}, u32[]{:S(2)}) collective-permute-start(bf16[5,64,128]{2,1,0:T(8,128)(2,1)S(1)} %get-tuple-element.41), channel_id=1, source_target_pairs={{0,1},{1,2},{2,3},{3,0},{4,5},{5,6},{6,7},{7,4},{8,9},{9,10},{10,1... | collective-permute-start | bytes 245768 | tf_op jit(solution)/shard_map/ppermute | solution.py:327
  53.1 0.0 collective-permute-done.5.refs_1_
  53.1 1.3 %collective-permute-start.17 = (bf16[5,64,128]{2,1,0:T(8,128)(2,1)S(1)}, bf16[5,64,128]{2,1,0:T(8,128)(2,1)S(1)}, u32[]{:S(2)}, u32[]{:S(2)}) collective-permute-start(bf16[5,64,128]{2,1,0:T(8,128)(2,1)S(1)} %get-tuple-element.42), channel_id=1, source_target_pairs={{0,2},{1,3},{2,0},{3,1},{4,6},{5,7},{6,4},{7,5},{8,10},{9,11},{10,... | collective-permute-start | bytes 245768 | tf_op jit(solution)/shard_map/ppermute | solution.py:327
  54.4 0.7 %collective-permute-done.6.refs_2_ = bf16[5,64,128]{2,1,0:T(8,128)(2,1)S(1)} collective-permute-done((bf16[5,64,128]{2,1,0:T(8,128)(2,1)S(1)}, bf16[5,64,128]{2,1,0:T(8,128)(2,1)S(1)}, u32[]{:S(2)}, u32[]{:S(2)}) %collective-permute-start.6) | collective-permute-done | bytes 81952 | tf_op jit(solution)/shard_map/ppermute | solution.py:327
  55.1 0.6 collective-permute-start.18
  55.8 0.0 collective-permute-done.7.refs_3_
  55.8 0.1 join.5.refs_5_
  55.9 0.0 collective-permute-done.4.refs_4_
  55.9 2.4 %attend.2 = (bf16[5,64,128]{2,1,0:T(8,128)(2,1)S(1)}, bf16[5,64,128]{2,1,0:T(8,128)(2,1)S(1)}, bf16[5,64,128]{2,1,0:T(8,128)(2,1)S(1)}, bf16[5,64,128]{2,1,0:T(8,128)(2,1)S(1)}, f32[5,256]{1,0:T(8,128)S(1)}) custom-call(s32[40]{0:T(128)} %head_slot.7, s32[5,2,40]{2,1,0:T(2,128)} %bitcast.2, bf16[10,256,128]{2,1,0:T(8,128)(2,1)S(1)} %after.2.refs_2_, ...), custom_call_target="tpu_custom_call" | custom-call | tf_op jit(solution)/shard_map/attend/pallas_call | solution.py:253
  58.3 1.7 %collective-permute-start.8 = (bf16[5,64,128]{2,1,0:T(8,128)(2,1)S(1)}, bf16[5,64,128]{2,1,0:T(8,128)(2,1)S(1)}, u32[]{:S(2)}, u32[]{:S(2)}) collective-permute-start(bf16[5,64,128]{2,1,0:T(8,128)(2,1)S(1)} %get-tuple-element.34), channel_id=1, source_target_pairs={{0,1},{1,2},{2,3},{3,0},{4,5},{5,6},{6,7},{7,4},{8,9},{9,10},{10,1... | collective-permute-start | bytes 245768 | tf_op jit(solution)/shard_map/ppermute | solution.py:327
  60.0 0.7 collective-permute-start.9
  60.6 0.0 collective-permute-done.16.refs_1_
  60.6 0.0 copy-start
  60.6 2.6 %collective-permute-start.10 = (bf16[5,64,128]{2,1,0:T(8,128)(2,1)S(1)}, bf16[5,64,128]{2,1,0:T(8,128)(2,1)S(1)}, u32[]{:S(2)}, u32[]{:S(2)}) collective-permute-start(bf16[5,64,128]{2,1,0:T(8,128)(2,1)S(1)} %get-tuple-element.36), channel_id=1, source_target_pairs={{0,3},{1,0},{2,1},{3,2},{4,7},{5,4},{6,5},{7,6},{8,11},{9,8},{10,9... | collective-permute-start | bytes 245768 | tf_op jit(solution)/shard_map/ppermute | solution.py:327
  63.2 0.0 collective-permute-done.17.refs_2_
  63.2 0.0 collective-permute-done.18.refs_3_
  63.2 0.0 copy-done
  63.2 1.5 %unpack.2.refs_4_ = bf16[64,5120]{1,0:T(8,128)(2,1)} custom-call(s32[40]{0:T(128)S(1)} %copy-done, bf16[5,64,128]{2,1,0:T(8,128)(2,1)S(1)} %get-tuple-element.40.refs_0_, bf16[5,64,128]{2,1,0:T(8,128)(2,1)S(1)} %collective-permute-done.16.refs_1_, bf16[5,64,128]{2,1,0:T(8,128)(2,1)S(1)} %collective-permute-done.17.refs_2_, ...), custom_call_target="tpu_custom_call" | custom-call | tf_op jit(solution)/shard_map/unpack/pallas_call | solution.py:306
  64.7 0.6 pad_maximum_fusion
  65.3 0.0 collective-permute-done.8.refs_1_
  65.3 4.1 %collective-permute-done.9.refs_2_ = bf16[5,64,128]{2,1,0:T(8,128)(2,1)S(1)} collective-permute-done((bf16[5,64,128]{2,1,0:T(8,128)(2,1)S(1)}, bf16[5,64,128]{2,1,0:T(8,128)(2,1)S(1)}, u32[]{:S(2)}, u32[]{:S(2)}) %collective-permute-start.9) | collective-permute-done | bytes 81952 | tf_op jit(solution)/shard_map/ppermute | solution.py:327
  69.4 0.0 collective-permute-done.10.refs_3_
  69.5 1.5 %unpack.3 = bf16[64,5120]{1,0:T(8,128)(2,1)} custom-call(s32[40]{0:T(128)S(1)} %copy-done, bf16[5,64,128]{2,1,0:T(8,128)(2,1)S(1)} %get-tuple-element.33.refs_0_, bf16[5,64,128]{2,1,0:T(8,128)(2,1)S(1)} %collective-permute-done.8.refs_1_, bf16[5,64,128]{2,1,0:T(8,128)(2,1)S(1)} %collective-permute-done.9.refs_2_, ...), custom_call_target="tpu_custom_call", output_to_operand_aliasing={{}: (5, {})} | custom-call | tf_op jit(solution)/shard_map/unpack/pallas_call | solution.py:306
  (2 shorter events, 0.0 us)
Async XLA Ops:
  2.3 10.2 %collective-permute-start.11 = (bf16[10,64,128]{2,1,0:T(8,128)(2,1)S(1)}, bf16[10,64,128]{2,1,0:T(8,128)(2,1)S(1)}, u32[]{:S(2)}, u32[]{:S(2)}) collective-permute-start(bf16[10,64,128]{2,1,0:T(8,128)(2,1)S(1)} %get-tuple-element.37), channel_id=1, source_target_pairs={{0,1},{1,2},{2,3},{3,0},{4,5},{5,6},{6,7},{7,4},{8,9},{9,10},{10,1... | collective-permute-start | bytes 491528 | tf_op jit(solution)/shard_map/ppermute | solution.py:327
  5.4 14.2 %collective-permute-start.12 = (bf16[10,64,128]{2,1,0:T(8,128)(2,1)S(1)}, bf16[10,64,128]{2,1,0:T(8,128)(2,1)S(1)}, u32[]{:S(2)}, u32[]{:S(2)}) collective-permute-start(bf16[10,64,128]{2,1,0:T(8,128)(2,1)S(1)} %get-tuple-element.38), channel_id=1, source_target_pairs={{0,2},{1,3},{2,0},{3,1},{4,6},{5,7},{6,4},{7,5},{8,10},{9,11},{10,... | collective-permute-start | bytes 491528 | tf_op jit(solution)/shard_map/ppermute | solution.py:327
  7.9 15.6 %collective-permute-start.13 = (bf16[10,64,128]{2,1,0:T(8,128)(2,1)S(1)}, bf16[10,64,128]{2,1,0:T(8,128)(2,1)S(1)}, u32[]{:S(2)}, u32[]{:S(2)}) collective-permute-start(bf16[10,64,128]{2,1,0:T(8,128)(2,1)S(1)} %get-tuple-element.39), channel_id=1, source_target_pairs={{0,3},{1,0},{2,1},{3,2},{4,7},{5,4},{6,5},{7,6},{8,11},{9,8},{10,9... | collective-permute-start | bytes 491528 | tf_op jit(solution)/shard_map/ppermute | solution.py:327
  11.3 13.5 %collective-permute-start = (bf16[15,64,128]{2,1,0:T(8,128)(2,1)S(1)}, bf16[15,64,128]{2,1,0:T(8,128)(2,1)S(1)}, u32[]{:S(2)}, u32[]{:S(2)}) collective-permute-start(bf16[15,64,128]{2,1,0:T(8,128)(2,1)S(1)} %get-tuple-element.26), channel_id=1, source_target_pairs={{0,1},{1,2},{2,3},{3,0},{4,5},{5,6},{6,7},{7,4},{8,9},{9,10},{10,1... | collective-permute-start | bytes 737288 | tf_op jit(solution)/shard_map/ppermute | solution.py:327
  12.1 26.0 %collective-permute-start.1 = (bf16[15,64,128]{2,1,0:T(8,128)(2,1)S(1)}, bf16[15,64,128]{2,1,0:T(8,128)(2,1)S(1)}, u32[]{:S(2)}, u32[]{:S(2)}) collective-permute-start(bf16[15,64,128]{2,1,0:T(8,128)(2,1)S(1)} %get-tuple-element.27), channel_id=1, source_target_pairs={{0,2},{1,3},{2,0},{3,1},{4,6},{5,7},{6,4},{7,5},{8,10},{9,11},{10,... | collective-permute-start | bytes 737288 | tf_op jit(solution)/shard_map/ppermute | solution.py:327
  12.5 25.5 %collective-permute-start.2 = (bf16[15,64,128]{2,1,0:T(8,128)(2,1)S(1)}, bf16[15,64,128]{2,1,0:T(8,128)(2,1)S(1)}, u32[]{:S(2)}, u32[]{:S(2)}) collective-permute-start(bf16[15,64,128]{2,1,0:T(8,128)(2,1)S(1)} %get-tuple-element.28), channel_id=1, source_target_pairs={{0,3},{1,0},{2,1},{3,2},{4,7},{5,4},{6,5},{7,6},{8,11},{9,8},{10,9... | collective-permute-start | bytes 737288 | tf_op jit(solution)/shard_map/ppermute | solution.py:327
  23.7 14.6 %collective-permute-start.14 = (bf16[10,256,128]{2,1,0:T(8,128)(2,1)S(1)}, bf16[10,256,128]{2,1,0:T(8,128)(2,1)S(1)}, u32[]{:S(2)}, u32[]{:S(2)}) collective-permute-start(bf16[10,256,128]{2,1,0:T(8,128)(2,1)S(1)} %join.6.refs_0_), channel_id=1, source_target_pairs={{4,8},{8,4},{5,9},{9,5},{6,10},{10,6},{7,11},{11,7},{20,24},{24,20... | collective-permute-start | bytes 1966088 | tf_op jit(solution)/shard_map/ppermute | solution.py:340
  38.2 2.2 %collective-permute-start.3 = (bf16[10,256,128]{2,1,0:T(8,128)(2,1)S(1)}, bf16[10,256,128]{2,1,0:T(8,128)(2,1)S(1)}, u32[]{:S(2)}, u32[]{:S(2)}) collective-permute-start(bf16[10,256,128]{2,1,0:T(8,128)(2,1)S(1)} %join.4.refs_0_), channel_id=1, source_target_pairs={{0,4},{8,12},{4,0},{12,8},{1,5},{9,13},{5,1},{13,9},{2,6},{10,14},... | collective-permute-start | bytes 1966088 | tf_op jit(solution)/shard_map/ppermute | solution.py:340
  38.3 11.1 %collective-permute-start.15 = (bf16[10,256,128]{2,1,0:T(8,128)(2,1)S(1)}, bf16[10,256,128]{2,1,0:T(8,128)(2,1)S(1)}, u32[]{:S(2)}, u32[]{:S(2)}) collective-permute-start(bf16[10,256,128]{2,1,0:T(8,128)(2,1)S(1)} %after.3.refs_2_), channel_id=1, source_target_pairs={{0,4},{8,12},{4,0},{12,8},{1,5},{9,13},{5,1},{13,9},{2,6},{10,14},... | collective-permute-start | bytes 1966088 | tf_op jit(solution)/shard_map/ppermute | solution.py:340
  40.4 15.5 %collective-permute-start.4 = (bf16[10,256,128]{2,1,0:T(8,128)(2,1)S(1)}, bf16[10,256,128]{2,1,0:T(8,128)(2,1)S(1)}, u32[]{:S(2)}, u32[]{:S(2)}) collective-permute-start(bf16[10,256,128]{2,1,0:T(8,128)(2,1)S(1)} %after.2.refs_2_), channel_id=1, source_target_pairs={{4,8},{8,4},{5,9},{9,5},{6,10},{10,6},{7,11},{11,7},{20,24},{24,20... | collective-permute-start | bytes 1966088 | tf_op jit(solution)/shard_map/ppermute | solution.py:340
  41.1 12.0 %collective-permute-start.5 = (bf16[5,64,128]{2,1,0:T(8,128)(2,1)S(1)}, bf16[5,64,128]{2,1,0:T(8,128)(2,1)S(1)}, u32[]{:S(2)}, u32[]{:S(2)}) collective-permute-start(bf16[5,64,128]{2,1,0:T(8,128)(2,1)S(1)} %get-tuple-element.30), channel_id=1, source_target_pairs={{0,1},{1,2},{2,3},{3,0},{4,5},{5,6},{6,7},{7,4},{8,9},{9,10},{10,1... | collective-permute-start | bytes 245768 | tf_op jit(solution)/shard_map/ppermute | solution.py:327
  46.9 8.3 %collective-permute-start.6 = (bf16[5,64,128]{2,1,0:T(8,128)(2,1)S(1)}, bf16[5,64,128]{2,1,0:T(8,128)(2,1)S(1)}, u32[]{:S(2)}, u32[]{:S(2)}) collective-permute-start(bf16[5,64,128]{2,1,0:T(8,128)(2,1)S(1)} %get-tuple-element.31), channel_id=1, source_target_pairs={{0,2},{1,3},{2,0},{3,1},{4,6},{5,7},{6,4},{7,5},{8,10},{9,11},{10,... | collective-permute-start | bytes 245768 | tf_op jit(solution)/shard_map/ppermute | solution.py:327
  48.5 7.3 %collective-permute-start.7 = (bf16[5,64,128]{2,1,0:T(8,128)(2,1)S(1)}, bf16[5,64,128]{2,1,0:T(8,128)(2,1)S(1)}, u32[]{:S(2)}, u32[]{:S(2)}) collective-permute-start(bf16[5,64,128]{2,1,0:T(8,128)(2,1)S(1)} %get-tuple-element.32), channel_id=1, source_target_pairs={{0,3},{1,0},{2,1},{3,2},{4,7},{5,4},{6,5},{7,6},{8,11},{9,8},{10,9... | collective-permute-start | bytes 245768 | tf_op jit(solution)/shard_map/ppermute | solution.py:327
  51.8 8.8 %collective-permute-start.16 = (bf16[5,64,128]{2,1,0:T(8,128)(2,1)S(1)}, bf16[5,64,128]{2,1,0:T(8,128)(2,1)S(1)}, u32[]{:S(2)}, u32[]{:S(2)}) collective-permute-start(bf16[5,64,128]{2,1,0:T(8,128)(2,1)S(1)} %get-tuple-element.41), channel_id=1, source_target_pairs={{0,1},{1,2},{2,3},{3,0},{4,5},{5,6},{6,7},{7,4},{8,9},{9,10},{10,1... | collective-permute-start | bytes 245768 | tf_op jit(solution)/shard_map/ppermute | solution.py:327
  53.1 10.1 %collective-permute-start.17 = (bf16[5,64,128]{2,1,0:T(8,128)(2,1)S(1)}, bf16[5,64,128]{2,1,0:T(8,128)(2,1)S(1)}, u32[]{:S(2)}, u32[]{:S(2)}) collective-permute-start(bf16[5,64,128]{2,1,0:T(8,128)(2,1)S(1)} %get-tuple-element.42), channel_id=1, source_target_pairs={{0,2},{1,3},{2,0},{3,1},{4,6},{5,7},{6,4},{7,5},{8,10},{9,11},{10,... | collective-permute-start | bytes 245768 | tf_op jit(solution)/shard_map/ppermute | solution.py:327
  55.1 8.1 %collective-permute-start.18 = (bf16[5,64,128]{2,1,0:T(8,128)(2,1)S(1)}, bf16[5,64,128]{2,1,0:T(8,128)(2,1)S(1)}, u32[]{:S(2)}, u32[]{:S(2)}) collective-permute-start(bf16[5,64,128]{2,1,0:T(8,128)(2,1)S(1)} %get-tuple-element.43), channel_id=1, source_target_pairs={{0,3},{1,0},{2,1},{3,2},{4,7},{5,4},{6,5},{7,6},{8,11},{9,8},{10,9... | collective-permute-start | bytes 245768 | tf_op jit(solution)/shard_map/ppermute | solution.py:327
  58.3 7.1 %collective-permute-start.8 = (bf16[5,64,128]{2,1,0:T(8,128)(2,1)S(1)}, bf16[5,64,128]{2,1,0:T(8,128)(2,1)S(1)}, u32[]{:S(2)}, u32[]{:S(2)}) collective-permute-start(bf16[5,64,128]{2,1,0:T(8,128)(2,1)S(1)} %get-tuple-element.34), channel_id=1, source_target_pairs={{0,1},{1,2},{2,3},{3,0},{4,5},{5,6},{6,7},{7,4},{8,9},{9,10},{10,1... | collective-permute-start | bytes 245768 | tf_op jit(solution)/shard_map/ppermute | solution.py:327
  60.0 9.5 %collective-permute-start.9 = (bf16[5,64,128]{2,1,0:T(8,128)(2,1)S(1)}, bf16[5,64,128]{2,1,0:T(8,128)(2,1)S(1)}, u32[]{:S(2)}, u32[]{:S(2)}) collective-permute-start(bf16[5,64,128]{2,1,0:T(8,128)(2,1)S(1)} %get-tuple-element.35), channel_id=1, source_target_pairs={{0,2},{1,3},{2,0},{3,1},{4,6},{5,7},{6,4},{7,5},{8,10},{9,11},{10,... | collective-permute-start | bytes 245768 | tf_op jit(solution)/shard_map/ppermute | solution.py:327
  60.6 2.6 %copy-start = (s32[40]{0:T(128)S(1)}, s32[40]{0:T(128)}, u32[]{:S(2)}) copy-start(s32[40]{0:T(128)} %head_slot.7) | copy-start | bytes 484
  60.6 8.8 %collective-permute-start.10 = (bf16[5,64,128]{2,1,0:T(8,128)(2,1)S(1)}, bf16[5,64,128]{2,1,0:T(8,128)(2,1)S(1)}, u32[]{:S(2)}, u32[]{:S(2)}) collective-permute-start(bf16[5,64,128]{2,1,0:T(8,128)(2,1)S(1)} %get-tuple-element.36), channel_id=1, source_target_pairs={{0,3},{1,0},{2,1},{3,2},{4,7},{5,4},{6,5},{7,6},{8,11},{9,8},{10,9... | collective-permute-start | bytes 245768 | tf_op jit(solution)/shard_map/ppermute | solution.py:327

commit v5 on v4

--- a/solution.py
+++ b/solution.py
@@ -59,8 +59,8 @@
     chunks = sem.shape[1]
     size = rows[0].shape[0] // chunks
     copies = []
-    for i in range(sources):
-        for j in range(chunks):
+    for j in range(chunks):
+        for i in range(sources):
             place = pl.ds(j * size, size)
             copies.append(
                 pltpu.make_async_copy(rows[i].at[place], held[i].at[place], sem.at[i, j])
@@ -68,18 +68,20 @@
             copies[-1].start()
     slot_copy.wait()
     invert(slots, head_of)
-    for copy in copies:
-        copy.wait()
-    for stage, part in enumerate(parts):
-        for k in range(owners):
-            owner = lax.rem(me + k, owners)
-            place = 0
-            for source, first, count in part:
-                for c in range(count):
-                    head = head_of[owner * capacity + first + c]
-                    columns = pl.ds(pl.multiple_of(head * dim, dim), dim)
-                    outs[stage * owners + k][place] = held[source][:, columns]
-                    place += 1
+    for j in range(chunks):
+        for i in range(sources):
+            copies[j * sources + i].wait()
+        place = slice(j * size, (j + 1) * size)
+        for stage, part in enumerate(parts):
+            for k in range(owners):
+                owner = lax.rem(me + k, owners)
+                at = 0
+                for source, first, count in part:
+                    for c in range(count):
+                        head = head_of[owner * capacity + first + c]
+                        columns = pl.ds(pl.multiple_of(head * dim, dim), dim)
+                        outs[stage * owners + k][at, place, :] = held[source][place, columns]
+                        at += 1
 
 
 def pack(head_slot, sources, stages, owners, capacity, dim, us, waits=()):

time: 71.2 us -> 71.1 us (level)
  no operation moved by 1% of the time
where the time goes in v5:
time: 71.1 us; the launch traced here: 70.8 us
  starting transfers between devices  28.9 us (41%)
  waiting for transfers between devices  28.9 us (41%)
  Pallas kernels  11.6 us (16%)
  between operations  0.78 us (1%)
    ppermute x15, waiting for transfers between devices, exchange(): lax.ppermute(blocks[k], 'head', [(i, (i + k) % owners) for i in range(own...  27.3 us
    ppermute x15, starting transfers between devices, exchange(): lax.ppermute(blocks[k], 'head', [(i, (i + k) % owners) for i in range(own...  27 us
    pallas_call x2, Pallas kernels, attend(): pl.pallas_call(functools.partial(attend_kernel, owners, capacity, first,...  4.7 us
    pallas_call x2, Pallas kernels, pack(): pl.pallas_call(functools.partial(pack_kernel, owners, capacity, dim, plac...  3.35 us
    pallas_call x2, Pallas kernels, unpack(): pl.pallas_call(functools.partial(unpack_kernel, owners, capacity, first,...  2.95 us
    ppermute x4, starting transfers between devices, swap(): return lax.ppermute(mid, 'slab', pairs + [(j, i) for i, j in pairs])  1.95 us
    ppermute x4, waiting for transfers between devices, swap(): return lax.ppermute(mid, 'slab', pairs + [(j, i) for i, j in pairs])  1.59 us
  transfers between devices with their start and end apart: 19, of which 8 were waited for; matrix products, arithmetic and copies ran while one was open for 1% of the time, Pallas kernels for 12%

profile of v5, /device:TPU:0, one launch (start us, length us, event | category | flops | bytes accessed | tf_op | source)
XLA Modules:
  0.0 70.8 jit_solution(6931033351767199755)
XLA Ops:
  0.6 1.5 %pack.2 = (bf16[10,64,128]{2,1,0:T(8,128)(2,1)S(1)}, bf16[10,64,128]{2,1,0:T(8,128)(2,1)S(1)}, bf16[10,64,128]{2,1,0:T(8,128)(2,1)S(1)}, bf16[10,64,128]{2,1,0:T(8,128)(2,1)S(1)}) custom-call(s32[40]{0:T(128)} %head_slot.7, bf16[64,5120]{1,0:T(8,128)(2,1)} %refs_0_.5, bf16[64,5120]{1,0:T(8,128)(2,1)} %refs_2_.1), custom_call_target="tpu_custom_call" | custom-call | tf_op jit(solution)/shard_map/pack/pallas_call | solution.py:97
  2.2 3.1 %collective-permute-start.11 = (bf16[10,64,128]{2,1,0:T(8,128)(2,1)S(1)}, bf16[10,64,128]{2,1,0:T(8,128)(2,1)S(1)}, u32[]{:S(2)}, u32[]{:S(2)}) collective-permute-start(bf16[10,64,128]{2,1,0:T(8,128)(2,1)S(1)} %get-tuple-element.37), channel_id=1, source_target_pairs={{0,1},{1,2},{2,3},{3,0},{4,5},{5,6},{6,7},{7,4},{8,9},{9,10},{10,1... | collective-permute-start | bytes 491528 | tf_op jit(solution)/shard_map/ppermute | solution.py:329
  5.2 2.6 %collective-permute-start.12 = (bf16[10,64,128]{2,1,0:T(8,128)(2,1)S(1)}, bf16[10,64,128]{2,1,0:T(8,128)(2,1)S(1)}, u32[]{:S(2)}, u32[]{:S(2)}) collective-permute-start(bf16[10,64,128]{2,1,0:T(8,128)(2,1)S(1)} %get-tuple-element.38), channel_id=1, source_target_pairs={{0,2},{1,3},{2,0},{3,1},{4,6},{5,7},{6,4},{7,5},{8,10},{9,11},{10,... | collective-permute-start | bytes 491528 | tf_op jit(solution)/shard_map/ppermute | solution.py:329
  7.8 1.3 %collective-permute-start.13 = (bf16[10,64,128]{2,1,0:T(8,128)(2,1)S(1)}, bf16[10,64,128]{2,1,0:T(8,128)(2,1)S(1)}, u32[]{:S(2)}, u32[]{:S(2)}) collective-permute-start(bf16[10,64,128]{2,1,0:T(8,128)(2,1)S(1)} %get-tuple-element.39), channel_id=1, source_target_pairs={{0,3},{1,0},{2,1},{3,2},{4,7},{5,4},{6,5},{7,6},{8,11},{9,8},{10,9... | collective-permute-start | bytes 491528 | tf_op jit(solution)/shard_map/ppermute | solution.py:329
  9.2 1.8 %pack.3 = (bf16[15,64,128]{2,1,0:T(8,128)(2,1)S(1)}, bf16[15,64,128]{2,1,0:T(8,128)(2,1)S(1)}, bf16[15,64,128]{2,1,0:T(8,128)(2,1)S(1)}, bf16[15,64,128]{2,1,0:T...) custom-call(s32[40]{0:T(128)} %head_slot.7, ...), custom_call_target="tpu_custom_call" | custom-call | tf_op jit(solution)/shard_map/pack/pallas_call | solution.py:97
  11.0 0.7 %collective-permute-start = (bf16[15,64,128]{2,1,0:T(8,128)(2,1)S(1)}, bf16[15,64,128]{2,1,0:T(8,128)(2,1)S(1)}, u32[]{:S(2)}, u32[]{:S(2)}) collective-permute-start(bf16[15,64,128]{2,1,0:T(8,128)(2,1)S(1)} %get-tuple-element.26), channel_id=1, source_target_pairs={{0,1},{1,2},{2,3},{3,0},{4,5},{5,6},{6,7},{7,4},{8,9},{9,10},{10,1... | collective-permute-start | bytes 737288 | tf_op jit(solution)/shard_map/ppermute | solution.py:329
  11.7 0.3 collective-permute-start.1
  12.1 0.3 collective-permute-done.11.refs_1_
  12.4 2.5 %collective-permute-start.2 = (bf16[15,64,128]{2,1,0:T(8,128)(2,1)S(1)}, bf16[15,64,128]{2,1,0:T(8,128)(2,1)S(1)}, u32[]{:S(2)}, u32[]{:S(2)}) collective-permute-start(bf16[15,64,128]{2,1,0:T(8,128)(2,1)S(1)} %get-tuple-element.28), channel_id=1, source_target_pairs={{0,3},{1,0},{2,1},{3,2},{4,7},{5,4},{6,5},{7,6},{8,11},{9,8},{10,9... | collective-permute-start | bytes 737288 | tf_op jit(solution)/shard_map/ppermute | solution.py:329
  14.9 4.6 %collective-permute-done.12.refs_2_ = bf16[10,64,128]{2,1,0:T(8,128)(2,1)S(1)} collective-permute-done((bf16[10,64,128]{2,1,0:T(8,128)(2,1)S(1)}, bf16[10,64,128]{2,1,0:T(8,128)(2,1)S(1)}, u32[]{:S(2)}, u32[]{:S(2)}) %collective-permute-start.12) | collective-permute-done | bytes 163872 | tf_op jit(solution)/shard_map/ppermute | solution.py:329
  19.5 4.0 %collective-permute-done.13.refs_3_ = bf16[10,64,128]{2,1,0:T(8,128)(2,1)S(1)} collective-permute-done((bf16[10,64,128]{2,1,0:T(8,128)(2,1)S(1)}, bf16[10,64,128]{2,1,0:T(8,128)(2,1)S(1)}, u32[]{:S(2)}, u32[]{:S(2)}) %collective-permute-start.13) | collective-permute-done | bytes 163872 | tf_op jit(solution)/shard_map/ppermute | solution.py:329
  23.4 0.2 join.6.refs_0_
  23.6 0.7 collective-permute-start.14
  24.3 0.4 collective-permute-done.refs_1_
  24.7 13.2 %collective-permute-done.1.refs_2_ = bf16[15,64,128]{2,1,0:T(8,128)(2,1)S(1)} collective-permute-done((bf16[15,64,128]{2,1,0:T(8,128)(2,1)S(1)}, bf16[15,64,128]{2,1,0:T(8,128)(2,1)S(1)}, u32[]{:S(2)}, u32[]{:S(2)}) %collective-permute-start.1) | collective-permute-done | bytes 245792 | tf_op jit(solution)/shard_map/ppermute | solution.py:329
  37.9 0.0 collective-permute-done.2.refs_3_
  37.9 0.2 join.4.refs_0_
  38.1 0.1 collective-permute-start.3
  38.2 0.0 collective-permute-done.14.refs_1_.refs_4_
  38.2 0.5 collective-permute-start.15
  38.7 1.6 %collective-permute-done.3.refs_1_.refs_3_ = bf16[10,256,128]{2,1,0:T(8,128)(2,1)S(1)} collective-permute-done((bf16[10,256,128]{2,1,0:T(8,128)(2,1)S(1)}, bf16[10,256,128]{2,1,0:T(8,128)(2,1)S(1)}, u32[]{:S(2)}, u32[]{:S(2)}) %collective-permute-start.3) | collective-permute-done | bytes 655392 | tf_op jit(solution)/shard_map/ppermute | solution.py:342
  40.3 0.7 collective-permute-start.4
  41.0 5.8 %collective-permute-start.5 = (bf16[5,64,128]{2,1,0:T(8,128)(2,1)S(1)}, bf16[5,64,128]{2,1,0:T(8,128)(2,1)S(1)}, u32[]{:S(2)}, u32[]{:S(2)}) collective-permute-start(bf16[5,64,128]{2,1,0:T(8,128)(2,1)S(1)} %get-tuple-element.30), channel_id=1, source_target_pairs={{0,1},{1,2},{2,3},{3,0},{4,5},{5,6},{6,7},{7,4},{8,9},{9,10},{10,1... | collective-permute-start | bytes 245768 | tf_op jit(solution)/shard_map/ppermute | solution.py:329
  46.7 1.6 %collective-permute-start.6 = (bf16[5,64,128]{2,1,0:T(8,128)(2,1)S(1)}, bf16[5,64,128]{2,1,0:T(8,128)(2,1)S(1)}, u32[]{:S(2)}, u32[]{:S(2)}) collective-permute-start(bf16[5,64,128]{2,1,0:T(8,128)(2,1)S(1)} %get-tuple-element.31), channel_id=1, source_target_pairs={{0,2},{1,3},{2,0},{3,1},{4,6},{5,7},{6,4},{7,5},{8,10},{9,11},{10,... | collective-permute-start | bytes 245768 | tf_op jit(solution)/shard_map/ppermute | solution.py:329
  48.4 0.8 %collective-permute-start.7 = (bf16[5,64,128]{2,1,0:T(8,128)(2,1)S(1)}, bf16[5,64,128]{2,1,0:T(8,128)(2,1)S(1)}, u32[]{:S(2)}, u32[]{:S(2)}) collective-permute-start(bf16[5,64,128]{2,1,0:T(8,128)(2,1)S(1)} %get-tuple-element.32), channel_id=1, source_target_pairs={{0,3},{1,0},{2,1},{3,2},{4,7},{5,4},{6,5},{7,6},{8,11},{9,8},{10,9... | collective-permute-start | bytes 245768 | tf_op jit(solution)/shard_map/ppermute | solution.py:329
  49.2 0.1 join.7.refs_5_
  49.3 0.0 collective-permute-done.15.refs_3_
  49.3 2.4 %attend.3 = (bf16[5,64,128]{2,1,0:T(8,128)(2,1)S(1)}, bf16[5,64,128]{2,1,0:T(8,128)(2,1)S(1)}, bf16[5,64,128]{2,1,0:T(8,128)(2,1)S(1)}, bf16[5,64,128]{2,1,0:T(8,128)(2,1)S(1)}, f32[5,256]{1,0:T(8,128)S(1)}) custom-call(s32[40]{0:T(128)} %head_slot.7, s32[5,2,40]{2,1,0:T(2,128)} %bitcast.1, bf16[10,256,128]{2,1,0:T(8,128)(2,1)S(1)} %after.3.refs_2_, ...), custom_call_target="tpu_custom_call" | custom-call | tf_op jit(solution)/shard_map/attend/pallas_call | solution.py:255
  51.7 1.3 %collective-permute-start.16 = (bf16[5,64,128]{2,1,0:T(8,128)(2,1)S(1)}, bf16[5,64,128]{2,1,0:T(8,128)(2,1)S(1)}, u32[]{:S(2)}, u32[]{:S(2)}) collective-permute-start(bf16[5,64,128]{2,1,0:T(8,128)(2,1)S(1)} %get-tuple-element.41), channel_id=1, source_target_pairs={{0,1},{1,2},{2,3},{3,0},{4,5},{5,6},{6,7},{7,4},{8,9},{9,10},{10,1... | collective-permute-start | bytes 245768 | tf_op jit(solution)/shard_map/ppermute | solution.py:329
  53.0 0.0 collective-permute-done.5.refs_1_
  53.0 1.3 %collective-permute-start.17 = (bf16[5,64,128]{2,1,0:T(8,128)(2,1)S(1)}, bf16[5,64,128]{2,1,0:T(8,128)(2,1)S(1)}, u32[]{:S(2)}, u32[]{:S(2)}) collective-permute-start(bf16[5,64,128]{2,1,0:T(8,128)(2,1)S(1)} %get-tuple-element.42), channel_id=1, source_target_pairs={{0,2},{1,3},{2,0},{3,1},{4,6},{5,7},{6,4},{7,5},{8,10},{9,11},{10,... | collective-permute-start | bytes 245768 | tf_op jit(solution)/shard_map/ppermute | solution.py:329
  54.3 0.7 %collective-permute-done.6.refs_2_ = bf16[5,64,128]{2,1,0:T(8,128)(2,1)S(1)} collective-permute-done((bf16[5,64,128]{2,1,0:T(8,128)(2,1)S(1)}, bf16[5,64,128]{2,1,0:T(8,128)(2,1)S(1)}, u32[]{:S(2)}, u32[]{:S(2)}) %collective-permute-start.6) | collective-permute-done | bytes 81952 | tf_op jit(solution)/shard_map/ppermute | solution.py:329
  55.0 0.6 collective-permute-start.18
  55.6 0.0 collective-permute-done.7.refs_3_
  55.6 0.1 join.5.refs_5_
  55.8 0.0 collective-permute-done.4.refs_4_
  55.8 2.4 %attend.2 = (bf16[5,64,128]{2,1,0:T(8,128)(2,1)S(1)}, bf16[5,64,128]{2,1,0:T(8,128)(2,1)S(1)}, bf16[5,64,128]{2,1,0:T(8,128)(2,1)S(1)}, bf16[5,64,128]{2,1,0:T(8,128)(2,1)S(1)}, f32[5,256]{1,0:T(8,128)S(1)}) custom-call(s32[40]{0:T(128)} %head_slot.7, s32[5,2,40]{2,1,0:T(2,128)} %bitcast.2, bf16[10,256,128]{2,1,0:T(8,128)(2,1)S(1)} %after.2.refs_2_, ...), custom_call_target="tpu_custom_call" | custom-call | tf_op jit(solution)/shard_map/attend/pallas_call | solution.py:255
  58.2 1.7 %collective-permute-start.8 = (bf16[5,64,128]{2,1,0:T(8,128)(2,1)S(1)}, bf16[5,64,128]{2,1,0:T(8,128)(2,1)S(1)}, u32[]{:S(2)}, u32[]{:S(2)}) collective-permute-start(bf16[5,64,128]{2,1,0:T(8,128)(2,1)S(1)} %get-tuple-element.34), channel_id=1, source_target_pairs={{0,1},{1,2},{2,3},{3,0},{4,5},{5,6},{6,7},{7,4},{8,9},{9,10},{10,1... | collective-permute-start | bytes 245768 | tf_op jit(solution)/shard_map/ppermute | solution.py:329
  59.9 0.7 collective-permute-start.9
  60.5 0.0 collective-permute-done.16.refs_1_
  60.5 0.0 copy-start
  60.5 2.6 %collective-permute-start.10 = (bf16[5,64,128]{2,1,0:T(8,128)(2,1)S(1)}, bf16[5,64,128]{2,1,0:T(8,128)(2,1)S(1)}, u32[]{:S(2)}, u32[]{:S(2)}) collective-permute-start(bf16[5,64,128]{2,1,0:T(8,128)(2,1)S(1)} %get-tuple-element.36), channel_id=1, source_target_pairs={{0,3},{1,0},{2,1},{3,2},{4,7},{5,4},{6,5},{7,6},{8,11},{9,8},{10,9... | collective-permute-start | bytes 245768 | tf_op jit(solution)/shard_map/ppermute | solution.py:329
  63.1 0.0 collective-permute-done.17.refs_2_
  63.1 0.0 collective-permute-done.18.refs_3_
  63.1 0.0 copy-done
  63.1 1.5 %unpack.2.refs_4_ = bf16[64,5120]{1,0:T(8,128)(2,1)} custom-call(s32[40]{0:T(128)S(1)} %copy-done, bf16[5,64,128]{2,1,0:T(8,128)(2,1)S(1)} %get-tuple-element.40.refs_0_, bf16[5,64,128]{2,1,0:T(8,128)(2,1)S(1)} %collective-permute-done.16.refs_1_, bf16[5,64,128]{2,1,0:T(8,128)(2,1)S(1)} %collective-permute-done.17.refs_2_, ...), custom_call_target="tpu_custom_call" | custom-call | tf_op jit(solution)/shard_map/unpack/pallas_call | solution.py:308
  64.6 0.6 pad_maximum_fusion
  65.2 0.0 collective-permute-done.8.refs_1_
  65.2 4.1 %collective-permute-done.9.refs_2_ = bf16[5,64,128]{2,1,0:T(8,128)(2,1)S(1)} collective-permute-done((bf16[5,64,128]{2,1,0:T(8,128)(2,1)S(1)}, bf16[5,64,128]{2,1,0:T(8,128)(2,1)S(1)}, u32[]{:S(2)}, u32[]{:S(2)}) %collective-permute-start.9) | collective-permute-done | bytes 81952 | tf_op jit(solution)/shard_map/ppermute | solution.py:329
  69.3 0.0 collective-permute-done.10.refs_3_
  69.3 1.5 %unpack.3 = bf16[64,5120]{1,0:T(8,128)(2,1)} custom-call(s32[40]{0:T(128)S(1)} %copy-done, bf16[5,64,128]{2,1,0:T(8,128)(2,1)S(1)} %get-tuple-element.33.refs_0_, bf16[5,64,128]{2,1,0:T(8,128)(2,1)S(1)} %collective-permute-done.8.refs_1_, bf16[5,64,128]{2,1,0:T(8,128)(2,1)S(1)} %collective-permute-done.9.refs_2_, ...), custom_call_target="tpu_custom_call", output_to_operand_aliasing={{}: (5, {})} | custom-call | tf_op jit(solution)/shard_map/unpack/pallas_call | solution.py:308
  (2 shorter events, 0.0 us)
Async XLA Ops:
  2.2 10.2 %collective-permute-start.11 = (bf16[10,64,128]{2,1,0:T(8,128)(2,1)S(1)}, bf16[10,64,128]{2,1,0:T(8,128)(2,1)S(1)}, u32[]{:S(2)}, u32[]{:S(2)}) collective-permute-start(bf16[10,64,128]{2,1,0:T(8,128)(2,1)S(1)} %get-tuple-element.37), channel_id=1, source_target_pairs={{0,1},{1,2},{2,3},{3,0},{4,5},{5,6},{6,7},{7,4},{8,9},{9,10},{10,1... | collective-permute-start | bytes 491528 | tf_op jit(solution)/shard_map/ppermute | solution.py:329
  5.2 14.2 %collective-permute-start.12 = (bf16[10,64,128]{2,1,0:T(8,128)(2,1)S(1)}, bf16[10,64,128]{2,1,0:T(8,128)(2,1)S(1)}, u32[]{:S(2)}, u32[]{:S(2)}) collective-permute-start(bf16[10,64,128]{2,1,0:T(8,128)(2,1)S(1)} %get-tuple-element.38), channel_id=1, source_target_pairs={{0,2},{1,3},{2,0},{3,1},{4,6},{5,7},{6,4},{7,5},{8,10},{9,11},{10,... | collective-permute-start | bytes 491528 | tf_op jit(solution)/shard_map/ppermute | solution.py:329
  7.8 15.6 %collective-permute-start.13 = (bf16[10,64,128]{2,1,0:T(8,128)(2,1)S(1)}, bf16[10,64,128]{2,1,0:T(8,128)(2,1)S(1)}, u32[]{:S(2)}, u32[]{:S(2)}) collective-permute-start(bf16[10,64,128]{2,1,0:T(8,128)(2,1)S(1)} %get-tuple-element.39), channel_id=1, source_target_pairs={{0,3},{1,0},{2,1},{3,2},{4,7},{5,4},{6,5},{7,6},{8,11},{9,8},{10,9... | collective-permute-start | bytes 491528 | tf_op jit(solution)/shard_map/ppermute | solution.py:329
  11.0 13.7 %collective-permute-start = (bf16[15,64,128]{2,1,0:T(8,128)(2,1)S(1)}, bf16[15,64,128]{2,1,0:T(8,128)(2,1)S(1)}, u32[]{:S(2)}, u32[]{:S(2)}) collective-permute-start(bf16[15,64,128]{2,1,0:T(8,128)(2,1)S(1)} %get-tuple-element.26), channel_id=1, source_target_pairs={{0,1},{1,2},{2,3},{3,0},{4,5},{5,6},{6,7},{7,4},{8,9},{9,10},{10,1... | collective-permute-start | bytes 737288 | tf_op jit(solution)/shard_map/ppermute | solution.py:329
  11.7 26.2 %collective-permute-start.1 = (bf16[15,64,128]{2,1,0:T(8,128)(2,1)S(1)}, bf16[15,64,128]{2,1,0:T(8,128)(2,1)S(1)}, u32[]{:S(2)}, u32[]{:S(2)}) collective-permute-start(bf16[15,64,128]{2,1,0:T(8,128)(2,1)S(1)} %get-tuple-element.27), channel_id=1, source_target_pairs={{0,2},{1,3},{2,0},{3,1},{4,6},{5,7},{6,4},{7,5},{8,10},{9,11},{10,... | collective-permute-start | bytes 737288 | tf_op jit(solution)/shard_map/ppermute | solution.py:329
  12.4 25.5 %collective-permute-start.2 = (bf16[15,64,128]{2,1,0:T(8,128)(2,1)S(1)}, bf16[15,64,128]{2,1,0:T(8,128)(2,1)S(1)}, u32[]{:S(2)}, u32[]{:S(2)}) collective-permute-start(bf16[15,64,128]{2,1,0:T(8,128)(2,1)S(1)} %get-tuple-element.28), channel_id=1, source_target_pairs={{0,3},{1,0},{2,1},{3,2},{4,7},{5,4},{6,5},{7,6},{8,11},{9,8},{10,9... | collective-permute-start | bytes 737288 | tf_op jit(solution)/shard_map/ppermute | solution.py:329
  23.6 14.6 %collective-permute-start.14 = (bf16[10,256,128]{2,1,0:T(8,128)(2,1)S(1)}, bf16[10,256,128]{2,1,0:T(8,128)(2,1)S(1)}, u32[]{:S(2)}, u32[]{:S(2)}) collective-permute-start(bf16[10,256,128]{2,1,0:T(8,128)(2,1)S(1)} %join.6.refs_0_), channel_id=1, source_target_pairs={{4,8},{8,4},{5,9},{9,5},{6,10},{10,6},{7,11},{11,7},{20,24},{24,20... | collective-permute-start | bytes 1966088 | tf_op jit(solution)/shard_map/ppermute | solution.py:342
  38.1 2.2 %collective-permute-start.3 = (bf16[10,256,128]{2,1,0:T(8,128)(2,1)S(1)}, bf16[10,256,128]{2,1,0:T(8,128)(2,1)S(1)}, u32[]{:S(2)}, u32[]{:S(2)}) collective-permute-start(bf16[10,256,128]{2,1,0:T(8,128)(2,1)S(1)} %join.4.refs_0_), channel_id=1, source_target_pairs={{0,4},{8,12},{4,0},{12,8},{1,5},{9,13},{5,1},{13,9},{2,6},{10,14},... | collective-permute-start | bytes 1966088 | tf_op jit(solution)/shard_map/ppermute | solution.py:342
  38.2 11.1 %collective-permute-start.15 = (bf16[10,256,128]{2,1,0:T(8,128)(2,1)S(1)}, bf16[10,256,128]{2,1,0:T(8,128)(2,1)S(1)}, u32[]{:S(2)}, u32[]{:S(2)}) collective-permute-start(bf16[10,256,128]{2,1,0:T(8,128)(2,1)S(1)} %after.3.refs_2_), channel_id=1, source_target_pairs={{0,4},{8,12},{4,0},{12,8},{1,5},{9,13},{5,1},{13,9},{2,6},{10,14},... | collective-permute-start | bytes 1966088 | tf_op jit(solution)/shard_map/ppermute | solution.py:342
  40.3 15.5 %collective-permute-start.4 = (bf16[10,256,128]{2,1,0:T(8,128)(2,1)S(1)}, bf16[10,256,128]{2,1,0:T(8,128)(2,1)S(1)}, u32[]{:S(2)}, u32[]{:S(2)}) collective-permute-start(bf16[10,256,128]{2,1,0:T(8,128)(2,1)S(1)} %after.2.refs_2_), channel_id=1, source_target_pairs={{4,8},{8,4},{5,9},{9,5},{6,10},{10,6},{7,11},{11,7},{20,24},{24,20... | collective-permute-start | bytes 1966088 | tf_op jit(solution)/shard_map/ppermute | solution.py:342
  41.0 12.0 %collective-permute-start.5 = (bf16[5,64,128]{2,1,0:T(8,128)(2,1)S(1)}, bf16[5,64,128]{2,1,0:T(8,128)(2,1)S(1)}, u32[]{:S(2)}, u32[]{:S(2)}) collective-permute-start(bf16[5,64,128]{2,1,0:T(8,128)(2,1)S(1)} %get-tuple-element.30), channel_id=1, source_target_pairs={{0,1},{1,2},{2,3},{3,0},{4,5},{5,6},{6,7},{7,4},{8,9},{9,10},{10,1... | collective-permute-start | bytes 245768 | tf_op jit(solution)/shard_map/ppermute | solution.py:329
  46.7 8.3 %collective-permute-start.6 = (bf16[5,64,128]{2,1,0:T(8,128)(2,1)S(1)}, bf16[5,64,128]{2,1,0:T(8,128)(2,1)S(1)}, u32[]{:S(2)}, u32[]{:S(2)}) collective-permute-start(bf16[5,64,128]{2,1,0:T(8,128)(2,1)S(1)} %get-tuple-element.31), channel_id=1, source_target_pairs={{0,2},{1,3},{2,0},{3,1},{4,6},{5,7},{6,4},{7,5},{8,10},{9,11},{10,... | collective-permute-start | bytes 245768 | tf_op jit(solution)/shard_map/ppermute | solution.py:329
  48.4 7.3 %collective-permute-start.7 = (bf16[5,64,128]{2,1,0:T(8,128)(2,1)S(1)}, bf16[5,64,128]{2,1,0:T(8,128)(2,1)S(1)}, u32[]{:S(2)}, u32[]{:S(2)}) collective-permute-start(bf16[5,64,128]{2,1,0:T(8,128)(2,1)S(1)} %get-tuple-element.32), channel_id=1, source_target_pairs={{0,3},{1,0},{2,1},{3,2},{4,7},{5,4},{6,5},{7,6},{8,11},{9,8},{10,9... | collective-permute-start | bytes 245768 | tf_op jit(solution)/shard_map/ppermute | solution.py:329
  51.7 8.8 %collective-permute-start.16 = (bf16[5,64,128]{2,1,0:T(8,128)(2,1)S(1)}, bf16[5,64,128]{2,1,0:T(8,128)(2,1)S(1)}, u32[]{:S(2)}, u32[]{:S(2)}) collective-permute-start(bf16[5,64,128]{2,1,0:T(8,128)(2,1)S(1)} %get-tuple-element.41), channel_id=1, source_target_pairs={{0,1},{1,2},{2,3},{3,0},{4,5},{5,6},{6,7},{7,4},{8,9},{9,10},{10,1... | collective-permute-start | bytes 245768 | tf_op jit(solution)/shard_map/ppermute | solution.py:329
  53.0 10.1 %collective-permute-start.17 = (bf16[5,64,128]{2,1,0:T(8,128)(2,1)S(1)}, bf16[5,64,128]{2,1,0:T(8,128)(2,1)S(1)}, u32[]{:S(2)}, u32[]{:S(2)}) collective-permute-start(bf16[5,64,128]{2,1,0:T(8,128)(2,1)S(1)} %get-tuple-element.42), channel_id=1, source_target_pairs={{0,2},{1,3},{2,0},{3,1},{4,6},{5,7},{6,4},{7,5},{8,10},{9,11},{10,... | collective-permute-start | bytes 245768 | tf_op jit(solution)/shard_map/ppermute | solution.py:329
  55.0 8.1 %collective-permute-start.18 = (bf16[5,64,128]{2,1,0:T(8,128)(2,1)S(1)}, bf16[5,64,128]{2,1,0:T(8,128)(2,1)S(1)}, u32[]{:S(2)}, u32[]{:S(2)}) collective-permute-start(bf16[5,64,128]{2,1,0:T(8,128)(2,1)S(1)} %get-tuple-element.43), channel_id=1, source_target_pairs={{0,3},{1,0},{2,1},{3,2},{4,7},{5,4},{6,5},{7,6},{8,11},{9,8},{10,9... | collective-permute-start | bytes 245768 | tf_op jit(solution)/shard_map/ppermute | solution.py:329
  58.2 7.1 %collective-permute-start.8 = (bf16[5,64,128]{2,1,0:T(8,128)(2,1)S(1)}, bf16[5,64,128]{2,1,0:T(8,128)(2,1)S(1)}, u32[]{:S(2)}, u32[]{:S(2)}) collective-permute-start(bf16[5,64,128]{2,1,0:T(8,128)(2,1)S(1)} %get-tuple-element.34), channel_id=1, source_target_pairs={{0,1},{1,2},{2,3},{3,0},{4,5},{5,6},{6,7},{7,4},{8,9},{9,10},{10,1... | collective-permute-start | bytes 245768 | tf_op jit(solution)/shard_map/ppermute | solution.py:329
  59.9 9.5 %collective-permute-start.9 = (bf16[5,64,128]{2,1,0:T(8,128)(2,1)S(1)}, bf16[5,64,128]{2,1,0:T(8,128)(2,1)S(1)}, u32[]{:S(2)}, u32[]{:S(2)}) collective-permute-start(bf16[5,64,128]{2,1,0:T(8,128)(2,1)S(1)} %get-tuple-element.35), channel_id=1, source_target_pairs={{0,2},{1,3},{2,0},{3,1},{4,6},{5,7},{6,4},{7,5},{8,10},{9,11},{10,... | collective-permute-start | bytes 245768 | tf_op jit(solution)/shard_map/ppermute | solution.py:329
  60.5 2.6 %copy-start = (s32[40]{0:T(128)S(1)}, s32[40]{0:T(128)}, u32[]{:S(2)}) copy-start(s32[40]{0:T(128)} %head_slot.7) | copy-start | bytes 484
  60.5 8.8 %collective-permute-start.10 = (bf16[5,64,128]{2,1,0:T(8,128)(2,1)S(1)}, bf16[5,64,128]{2,1,0:T(8,128)(2,1)S(1)}, u32[]{:S(2)}, u32[]{:S(2)}) collective-permute-start(bf16[5,64,128]{2,1,0:T(8,128)(2,1)S(1)} %get-tuple-element.36), channel_id=1, source_target_pairs={{0,3},{1,0},{2,1},{3,2},{4,7},{5,4},{6,5},{7,6},{8,11},{9,8},{10,9... | collective-permute-start | bytes 245768 | tf_op jit(solution)/shard_map/ppermute | solution.py:329
